TPU v7x, 32 devices: a whole 2x2x4 slice. The times are simulated.
32 devices in a mesh: wide: 4 (over x, core), narrow: 8 (over z, y).
Axes of the slice: x: 2, y: 2, z: 4, core: 2. Of those that a mesh axis runs over, the one named last changes fastest.
Arguments:
- block_input: bfloat16 [8, 1024, 1024], P('wide'), may hold values from -6 to 6
- output_cotangent: bfloat16 [8, 1024, 1024], P('wide'), may hold values from -8 to 8
- loss_weight: float32 [8, 1024], P('wide'), may hold values from 0.25 to 5.25, as said below
- segments: int32 [8, 1024], P('wide'), may hold values from 0 to 5, never falling along the last dimension, each value on 1 to 512 neighbouring positions
- nbr_keys: bfloat16 [8, 1024, 1024, 128], P('wide', None, 'narrow'), may hold values from -0.375 to 0.375
- nbr_count: int32 [8, 1024], P('wide'), may hold values from 1 to 128, as said below
- nbr_ids: int32 [8, 1024, 128], P('wide'), may hold values from 0 to 249999
- targets: int32 [8, 1024], P('wide'), may hold values from 0 to 249999
- base_prob: float32 [8, 1024], P('wide'), may hold values from 0.001 to 0.05
- w_query: bfloat16 [1024, 1024], P('narrow'), may hold values from -0.1875 to 0.1875
- w_key: bfloat16 [1024, 1024], P('narrow'), may hold values from -0.1875 to 0.1875
- w_value: bfloat16 [1024, 1024], P('narrow'), may hold values from -0.1875 to 0.1875
- w_proj: bfloat16 [1024, 1024], P('narrow'), may hold values from -0.75 to 0.75
- w_in: bfloat16 [1024, 4096], P(None, 'narrow'), may hold values from -0.1875 to 0.1875
- w_out: bfloat16 [4096, 1024], P('narrow'), may hold values from -0.125 to 0.125
- gain_attn: float32 [1024], replicated, may hold values from 0.5 to 1.5
- gain_ffn: float32 [1024], replicated, may hold values from 0.5 to 1.5
- gain_key: float32 [1024], replicated, may hold values from 0.5 to 1.5
- temper: float32 [1], replicated, may hold values from 1 to 4
- mix_weight: float32 [1], replicated, may hold values from 0.2 to 0.8
Outputs:
- block_output: bfloat16 [8, 1024, 1024], P('wide')
- token_loss: float32 [8, 1024], P('wide')
- grad_input: float32 [8, 1024, 1024], P('wide')
- grad_w_query: float32 [1024, 1024], P('narrow', 'wide')
- grad_w_key: float32 [1024, 1024], P('narrow', 'wide')
- grad_w_value: float32 [1024, 1024], P('narrow', 'wide')
- grad_w_proj: float32 [1024, 1024], P('narrow', 'wide')
- grad_w_in: float32 [1024, 4096], P('wide', 'narrow')
- grad_w_out: float32 [4096, 1024], P('narrow', 'wide')
- grad_gain_attn: float32 [1024], P('wide')
- grad_gain_ffn: float32 [1024], P('wide')
- grad_gain_key: float32 [1024], P('wide')
- grad_temper: float32 [1], replicated
- grad_mix_weight: float32 [1], replicated
Inputs may be any that keep to these rules, and one draw needn't show every extreme that they name: `nbr_count`: every token has 1 to 128 valid neighbours; some token has 128, some 1. `loss_weight`: Positive.
All inputs are finite; a program needn't handle non-finite values.
Results may differ from a plain program's by a relative error of at most 0.013.
Values may be sent and summed in bfloat16 or wider, within the bound.
A program may use at most 256 MiB of HBM per device.

v0:
```python
import jax
import jax.numpy as jnp
from jax import lax
from jax.sharding import PartitionSpec as P

HD = 64


EPSILON = 1e-05


def product(left, right):
    return jnp.dot(left, right, preferred_element_type=jnp.float32)


def through_t(grads, weight):
    return lax.dot_general(
        grads, weight, (((1,), (1,)), ((), ())), preferred_element_type=jnp.float32
    )


def outer_sum(left, right):
    return jnp.einsum("ta,tb->ab", left, right, preferred_element_type=jnp.float32)


def norm_parts(values):
    centred = values - jnp.mean(values, axis=-1, keepdims=True)
    inverse = lax.rsqrt(jnp.mean(centred * centred, axis=-1, keepdims=True) + EPSILON)
    return (centred * inverse, inverse)


def norm_back(grad_out, normed, inverse, gain):
    scaled = grad_out * gain
    grad_in = inverse * (
        scaled
        - jnp.mean(scaled, axis=-1, keepdims=True)
        - normed * jnp.mean(scaled * normed, axis=-1, keepdims=True)
    )
    return (grad_in, jnp.sum(grad_out * normed, axis=0))


def gelu_tanh(values):
    return jax.nn.gelu(values, approximate=True)


def on_device(
    block_input,
    output_cotangent,
    loss_weight,
    segments,
    nbr_keys,
    nbr_count,
    nbr_ids,
    targets,
    base_prob,
    w_query,
    w_key,
    w_value,
    w_proj,
    w_in,
    w_out,
    gain_attn,
    gain_ffn,
    gain_key,
    temper,
    mix_weight,
):
    seqs_here, length, width = block_input.shape
    rows = seqs_here * length
    local_width = w_query.shape[0]
    heads_here = local_width // HD
    scale = HD ** (-0.5)
    inputs = block_input.reshape(rows, width).astype(jnp.float32)
    normed_in, inverse_in = norm_parts(inputs)
    normed_one = (normed_in * gain_attn).astype(jnp.bfloat16)
    queries = (
        (through_t(normed_one, w_query) * scale)
        .astype(jnp.bfloat16)
        .reshape(seqs_here, length, heads_here, HD)
    )
    keys_attn = (
        through_t(normed_one, w_key).astype(jnp.bfloat16).reshape(seqs_here, length, heads_here, HD)
    )
    values_attn = (
        through_t(normed_one, w_value)
        .astype(jnp.bfloat16)
        .reshape(seqs_here, length, heads_here, HD)
    )
    q_rows = min(512, length)
    key_pos = jnp.arange(length, dtype=jnp.int32)

    def masked_scores(row_start):
        query_block = queries[:, row_start : row_start + q_rows]
        raw_scores = jnp.einsum(
            "sqhd,skhd->shqk", query_block, keys_attn, preferred_element_type=jnp.float32
        )
        query_pos = row_start + jnp.arange(q_rows, dtype=jnp.int32)
        allowed = (key_pos[None, None, :] <= query_pos[None, :, None]) & (
            segments[:, None, :] == segments[:, row_start : row_start + q_rows, None]
        )
        return (jnp.where(allowed[:, None], raw_scores, -1e30), allowed, query_block)

    block_outputs = []
    block_lse = []
    for row_start in range(0, length, q_rows):
        scores, allowed, query_block = masked_scores(row_start)
        peak = jnp.max(scores, axis=-1, keepdims=True)
        expo = jnp.exp(scores - peak)
        totals = jnp.sum(expo, axis=-1, keepdims=True)
        probs = (expo / totals).astype(jnp.bfloat16)
        block_lse.append(peak + jnp.log(totals))
        block_outputs.append(
            jnp.einsum("shqk,skhd->sqhd", probs, values_attn, preferred_element_type=jnp.float32)
        )
    attended = (
        jnp.concatenate(block_outputs, axis=1).astype(jnp.bfloat16).reshape(rows, local_width)
    )
    hidden_one = inputs + lax.psum(product(attended, w_proj), "narrow")
    normed_h, inverse_h = norm_parts(hidden_one)
    normed_two = (normed_h * gain_ffn).astype(jnp.bfloat16)
    pre_act = product(normed_two, w_in)
    activated = gelu_tanh(pre_act).astype(jnp.bfloat16)
    hidden_two = hidden_one + lax.psum(product(activated, w_out), "narrow")
    block_output = hidden_two.astype(jnp.bfloat16).reshape(seqs_here, length, width)
    normed_f, inverse_f = norm_parts(hidden_two)
    query_key = (normed_f * gain_key).astype(jnp.bfloat16)
    key_slices = nbr_keys.reshape(rows, nbr_keys.shape[2], nbr_keys.shape[3])
    slice_width = key_slices.shape[1]
    query_slice = lax.dynamic_slice_in_dim(
        query_key, lax.axis_index("narrow") * slice_width, slice_width, 1
    )
    part_products = jnp.einsum(
        "td,tdj->tj", query_slice, key_slices, preferred_element_type=jnp.float32
    )
    part_norms = jnp.einsum(
        "tdj,tdj->tj", key_slices, key_slices, preferred_element_type=jnp.float32
    )
    distance = lax.psum(2.0 * part_products - part_norms, "narrow")
    temper_value = temper[0]
    mix_value = mix_weight[0]
    logits = distance / temper_value
    live = (
        jnp.arange(key_slices.shape[2], dtype=jnp.int32)[None, :] < nbr_count.reshape(rows)[:, None]
    )
    masked_logits = jnp.where(live, logits, -1e30)
    peak_knn = jnp.max(masked_logits, axis=-1, keepdims=True)
    expo_knn = jnp.exp(masked_logits - peak_knn)
    weights = expo_knn / jnp.sum(expo_knn, axis=-1, keepdims=True)
    matches = (nbr_ids.reshape(rows, -1) == targets.reshape(rows)[:, None]).astype(jnp.float32)
    knn_prob = jnp.sum(weights * matches, axis=-1)
    base_values = base_prob.reshape(rows)
    mixture = mix_value * knn_prob + (1.0 - mix_value) * base_values
    token_loss = (-jnp.log(mixture)).reshape(seqs_here, length)
    grad_mixture = -loss_weight.reshape(rows) / mixture
    term_mix = (knn_prob - base_values) * grad_mixture
    grad_logits = weights * (mix_value * grad_mixture)[:, None] * (matches - knn_prob[:, None])
    term_temper = -jnp.sum(grad_logits * logits, axis=-1) / temper_value
    grad_products = (2.0 * grad_logits / temper_value).astype(jnp.bfloat16)
    grad_slice = jnp.einsum(
        "tj,tdj->td", grad_products, key_slices, preferred_element_type=jnp.float32
    )
    grad_query_key = lax.all_gather(grad_slice, "narrow", axis=1, tiled=True)
    grad_hidden_f, grad_gain_key = norm_back(grad_query_key, normed_f, inverse_f, gain_key)
    grad_hidden_two = output_cotangent.reshape(rows, width).astype(jnp.float32) + grad_hidden_f
    grad_ffn = grad_hidden_two.astype(jnp.bfloat16)
    grad_w_out = outer_sum(activated, grad_ffn)
    grad_activated = through_t(grad_ffn, w_out)
    gelu_pull = jax.vjp(gelu_tanh, pre_act)[1]
    grad_pre = gelu_pull(grad_activated)[0].astype(jnp.bfloat16)
    grad_w_in = outer_sum(normed_two, grad_pre)
    grad_normed_two = lax.psum(through_t(grad_pre, w_in), "narrow")
    grad_hidden_n, grad_gain_ffn = norm_back(grad_normed_two, normed_h, inverse_h, gain_ffn)
    grad_hidden_one = grad_hidden_two + grad_hidden_n
    grad_branch = grad_hidden_one.astype(jnp.bfloat16)
    grad_w_proj = outer_sum(attended, grad_branch)
    grad_attended = (
        through_t(grad_branch, w_proj)
        .astype(jnp.bfloat16)
        .reshape(seqs_here, length, heads_here, HD)
    )
    grad_query_blocks = []
    grad_keys_acc = jnp.zeros((seqs_here, length, heads_here, HD), jnp.float32)
    grad_values_acc = jnp.zeros((seqs_here, length, heads_here, HD), jnp.float32)
    for block_index, row_start in enumerate(range(0, length, q_rows)):
        scores, allowed, query_block = masked_scores(row_start)
        probs_full = jnp.where(allowed[:, None], jnp.exp(scores - block_lse[block_index]), 0.0)
        grad_block = grad_attended[:, row_start : row_start + q_rows]
        grad_probs = jnp.einsum(
            "sqhd,skhd->shqk", grad_block, values_attn, preferred_element_type=jnp.float32
        )
        delta = jnp.sum(probs_full * grad_probs, axis=-1, keepdims=True)
        grad_scores = (probs_full * (grad_probs - delta)).astype(jnp.bfloat16)
        grad_query_blocks.append(
            jnp.einsum(
                "shqk,skhd->sqhd", grad_scores, keys_attn, preferred_element_type=jnp.float32
            )
        )
        grad_keys_acc = grad_keys_acc + jnp.einsum(
            "shqk,sqhd->skhd", grad_scores, query_block, preferred_element_type=jnp.float32
        )
        grad_values_acc = grad_values_acc + jnp.einsum(
            "shqk,sqhd->skhd",
            probs_full.astype(jnp.bfloat16),
            grad_block,
            preferred_element_type=jnp.float32,
        )
    grad_queries = (
        jnp.concatenate(grad_query_blocks, axis=1).astype(jnp.bfloat16).reshape(rows, local_width)
    )
    grad_keys = grad_keys_acc.astype(jnp.bfloat16).reshape(rows, local_width)
    grad_values = grad_values_acc.astype(jnp.bfloat16).reshape(rows, local_width)
    grad_w_query = scale * outer_sum(grad_queries, normed_one)
    grad_w_key = outer_sum(grad_keys, normed_one)
    grad_w_value = outer_sum(grad_values, normed_one)
    grad_normed_part = (
        scale * product(grad_queries, w_query)
        + product(grad_keys, w_key)
        + product(grad_values, w_value)
    )
    grad_normed_one = lax.psum(grad_normed_part, "narrow")
    grad_input_n, grad_gain_attn = norm_back(grad_normed_one, normed_in, inverse_in, gain_attn)
    grad_input_rows = grad_hidden_one + grad_input_n
    grad_input = grad_input_rows.reshape(seqs_here, length, width)
    summed = (
        lax.psum_scatter(grad_w_query, "wide", scatter_dimension=1, tiled=True),
        lax.psum_scatter(grad_w_key, "wide", scatter_dimension=1, tiled=True),
        lax.psum_scatter(grad_w_value, "wide", scatter_dimension=1, tiled=True),
        lax.psum_scatter(grad_w_proj, "wide", scatter_dimension=1, tiled=True),
        lax.psum_scatter(grad_w_in, "wide", scatter_dimension=0, tiled=True),
        lax.psum_scatter(grad_w_out, "wide", scatter_dimension=1, tiled=True),
    )
    own_temper = jnp.sum(term_temper)
    own_mix = jnp.sum(term_mix)
    total_attn, total_ffn, total_key, sum_temper, sum_mix = lax.psum(
        (grad_gain_attn, grad_gain_ffn, grad_gain_key, own_temper, own_mix), "wide"
    )
    gain_piece = width // lax.axis_size("wide")
    gain_start = lax.axis_index("wide") * gain_piece
    piece_attn = lax.dynamic_slice_in_dim(total_attn, gain_start, gain_piece, 0)
    piece_ffn = lax.dynamic_slice_in_dim(total_ffn, gain_start, gain_piece, 0)
    piece_key = lax.dynamic_slice_in_dim(total_key, gain_start, gain_piece, 0)
    grad_temper = jnp.reshape(sum_temper, (1,))
    grad_mix_weight = jnp.reshape(sum_mix, (1,))
    return (
        block_output,
        token_loss,
        grad_input,
        summed[0],
        summed[1],
        summed[2],
        summed[3],
        summed[4],
        summed[5],
        piece_attn,
        piece_ffn,
        piece_key,
        grad_temper,
        grad_mix_weight,
    )


def solution(mesh):
    return jax.shard_map(
        on_device,
        mesh=mesh,
        in_specs=(
            P("wide", None, None),
            P("wide", None, None),
            P("wide", None),
            P("wide", None),
            P("wide", None, "narrow", None),
            P("wide", None),
            P("wide", None, None),
            P("wide", None),
            P("wide", None),
            P("narrow", None),
            P("narrow", None),
            P("narrow", None),
            P("narrow", None),
            P(None, "narrow"),
            P("narrow", None),
            P(),
            P(),
            P(),
            P(),
            P(),
        ),
        out_specs=(
            P("wide", None, None),
            P("wide", None),
            P("wide", None, None),
            P("narrow", "wide"),
            P("narrow", "wide"),
            P("narrow", "wide"),
            P("narrow", "wide"),
            P("wide", "narrow"),
            P("narrow", "wide"),
            P("wide"),
            P("wide"),
            P("wide"),
            P(),
            P(),
        ),
        check_vma=False,
    )
```

profile of v0, /device:TPU:0, one launch (start us, length us, event | category | flops | bytes accessed | tf_op | source)
XLA Modules:
  0.0 1738.1 jit_solution(16336933078594423159)
XLA Ops:
  56.2 273.2 %all-reduce.7.cloned.1.call-done = f32[2048,1024]{1,0:T(8,128)} async-done(((f32[2048,1024]{1,0:T(8,128)}), f32[2048,1024]{1,0:T(8,128)}) %all-reduce.7.cloned.1.call-update) | async-done | bytes 8388624 | tf_op jit(solution)/shard_map/psum | solution.py:118
  349.3 22.4 %fusion = f32[2048,128]{1,0:T(8,128)S(1)} fusion(bf16[2,1024,128,128]{3,2,1,0:T(8,128)(2,1)} %param.24), kind=kLoop, calls=%fused_computation.1 | loop fusion | flops 100401152 | bytes 68157440 | tf_op jit(solution)/shard_map/tdj,tdj->tj/dot_general | solution.py:135
  371.7 246.4 %all-reduce.9.cloned.1.call-done = f32[2048,1024]{1,0:T(8,128)} async-done(((f32[2048,1024]{1,0:T(8,128)}), f32[2048,1024]{1,0:T(8,128)}) %all-reduce.9.cloned.1.call-update) | async-done | bytes 8388624 | tf_op jit(solution)/shard_map/psum | solution.py:123
  618.1 9.8 fusion.85
  640.0 25.2 %fusion.64 = f32[2048,1,128]{2,1,0:T(1,128)S(1)} fusion(bf16[2048,128,128]{2,1,0:T(8,128)(2,1)} %bitcast.9, bf16[2048,128,1]{1,0,2:T(8,128)(2,1)S(1)} %fusion.70), kind=kOutput, calls=%fused_computation.104 | convolution fusion | flops 67108864 | bytes 68681728 | tf_op jit(solution)/shard_map/td,tdj->tj/dot_general | solution.py:132
  667.8 75.8 %all-reduce.11.cloned.1.call-done = f32[2048,128]{1,0:T(8,128)} async-done(((f32[2048,128]{1,0:T(8,128)}), f32[2048,128]{1,0:T(8,128)}) %all-reduce.11.cloned.1.call-update) | async-done | bytes 1048592 | tf_op jit(solution)/shard_map/psum | solution.py:138
  754.4 40.1 %fusion.62 = f32[2048,1,128]{2,1,0:T(1,128)} fusion(bf16[2048,128,128]{2,1,0:T(8,128)(2,1)} %bitcast.9, bf16[2048,128,1]{1,0,2:T(8,128)(2,1)S(1)} %get-tuple-element.38), kind=kOutput, calls=%fused_computation.102 | convolution fusion | flops 67108864 | bytes 68681728 | tf_op jit(solution)/shard_map/tj,tdj->td/dot_general | solution.py:159
  794.6 125.1 %all-gather.2.cloned.1.call-done = f32[2048,1024]{1,0:T(8,128)} async-done(((f32[2048,128]{1,0:T(8,128)}), f32[2048,1024]{1,0:T(8,128)}) %all-gather.2.cloned.1.call-update) | async-done | bytes 8388624 | tf_op jit(solution)/shard_map/all_gather | solution.py:162
  919.7 7.6 multiply_reduce_fusion
  934.4 8.0 fusion.27
  949.6 268.6 %all-reduce.13.cloned.1.call-done = f32[2048,1024]{1,0:T(8,128)} async-done(((f32[2048,1024]{1,0:T(8,128)}), f32[2048,1024]{1,0:T(8,128)}) %all-reduce.13.cloned.1.call-update) | async-done | bytes 8388624 | tf_op jit(solution)/shard_map/psum | solution.py:171
  1218.3 7.7 multiply_reduce_fusion.1
  1226.5 7.4 multiply_add_fusion
  1250.8 7.5 multiply_reduce_fusion.2
  1259.5 7.1 multiply_reduce_fusion.3
  1294.2 8.6 fusion.40
  1329.7 234.0 %all-reduce.15.cloned.1.call-done = f32[2048,1024]{1,0:T(8,128)} async-done(((f32[2048,1024]{1,0:T(8,128)}), f32[2048,1024]{1,0:T(8,128)}) %all-reduce.15.cloned.1.call-update) | async-done | bytes 8388624 | tf_op jit(solution)/shard_map/psum | solution.py:220
  1570.0 12.0 all-reduce
  1583.9 11.9 fusion.15
  1597.4 34.6 %reduce-scatter.15.cloned.1.call-done = f32[256,512]{1,0:T(8,128)} async-done(((f32[1024,512]{1,0:T(8,128)}), f32[256,512]{1,0:T(8,128)}) %reduce-scatter.15.cloned.1.call-update) | async-done | bytes 524304 | tf_op jit(solution)/shard_map/reduce_scatter | solution.py:229
  1632.0 24.9 %reduce-scatter.11.cloned.1.call-done = f32[128,256]{1,0:T(8,128)} async-done(((f32[128,1024]{1,0:T(8,128)}), f32[128,256]{1,0:T(8,128)}) %reduce-scatter.11.cloned.1.call-update) | async-done | bytes 131088 | tf_op jit(solution)/shard_map/reduce_scatter | solution.py:227
  1656.9 24.6 %reduce-scatter.7.cloned.1.call-done = f32[128,256]{1,0:T(8,128)} async-done(((f32[128,1024]{1,0:T(8,128)}), f32[128,256]{1,0:T(8,128)}) %reduce-scatter.7.cloned.1.call-update) | async-done | bytes 131088 | tf_op jit(solution)/shard_map/reduce_scatter | solution.py:225
  1681.5 24.9 %reduce-scatter.9.cloned.1.call-done = f32[128,256]{1,0:T(8,128)} async-done(((f32[128,1024]{1,0:T(8,128)}), f32[128,256]{1,0:T(8,128)}) %reduce-scatter.9.cloned.1.call-update) | async-done | bytes 131088 | tf_op jit(solution)/shard_map/reduce_scatter | solution.py:226
  1706.5 24.6 %reduce-scatter.13.cloned.1.call-done = f32[128,256]{1,0:T(8,128)} async-done(((f32[128,1024]{1,0:T(8,128)}), f32[128,256]{1,0:T(8,128)}) %reduce-scatter.13.cloned.1.call-update) | async-done | bytes 131088 | tf_op jit(solution)/shard_map/reduce_scatter | solution.py:228
  (273 shorter events, 188.8 us)
Async XLA Ops:
  7.2 335.4 %copy-start = (bf16[512,1024]{1,0:T(8,128)(2,1)S(1)}, bf16[512,1024]{1,0:T(8,128)(2,1)}, u32[]{:S(2)}) copy-start(bf16[512,1024]{1,0:T(8,128)(2,1)} %param.34) | copy-start | bytes 3145732
  7.2 322.2 %all-reduce.7.cloned.1.call-start = ((), (), s32[]{:S(2)}) async-start(), calls=%async_computation.6 | async-start | bytes 16777216 | tf_op jit(solution)/shard_map/psum | solution.py:118
  19.9 23.3 %copy-start.18 = (bf16[2,1024,2,64]{1,3,2,0:T(8,128)(2,1)}, bf16[2,1024,2,64]{1,3,2,0:T(8,128)(2,1)S(1)}, u32[]{:S(2)}) copy-start(bf16[2,1024,2,64]{1,3,2,0:T(8,128)(2,1)S(1)} %copy.50) | copy-start | bytes 1572868
  25.8 12.1 copy-start.32
  31.9 15.1 copy-start.25
  56.2 562.0 %all-reduce.9.cloned.1.call-start = ((), (), s32[]{:S(2)}) async-start(), calls=%async_computation.7 | async-start | bytes 16777216 | tf_op jit(solution)/shard_map/psum | solution.py:123
  348.5 395.0 %all-reduce.11.cloned.1.call-start = ((), (), s32[]{:S(2)}) async-start(), calls=%async_computation.8 | async-start | bytes 2097152 | tf_op jit(solution)/shard_map/psum | solution.py:138
  640.0 27.7 %copy-start.62 = (s32[2,1024]{1,0:T(2,128)S(1)}, s32[2,1024]{1,0:T(2,128)}, u32[]{:S(2)}) copy-start(s32[2,1024]{1,0:T(2,128)} %param.25) | copy-start | bytes 24580
  640.0 27.7 %copy-start.63 = (s32[2,1024]{1,0:T(2,128)S(1)}, s32[2,1024]{1,0:T(2,128)}, u32[]{:S(2)}) copy-start(s32[2,1024]{1,0:T(2,128)} %param.27) | copy-start | bytes 24580
  665.3 85.9 %copy-start.60 = (f32[2,1024]{1,0:T(2,128)S(1)}, f32[2,1024]{1,0:T(2,128)}, u32[]{:S(2)}) copy-start(f32[2,1024]{1,0:T(2,128)} %param.28) | copy-start | bytes 24580
  665.3 85.9 %copy-start.61 = (f32[2,1024]{1,0:T(2,128)S(1)}, f32[2,1024]{1,0:T(2,128)}, u32[]{:S(2)}) copy-start(f32[2,1024]{1,0:T(2,128)} %param.22) | copy-start | bytes 24580
  666.4 253.3 %all-gather.2.cloned.1.call-start = ((), (), s32[]{:S(2)}) async-start(), calls=%async_computation.9 | async-start | bytes 9437184 | tf_op jit(solution)/shard_map/all_gather | solution.py:162
  794.6 423.7 %all-reduce.13.cloned.1.call-start = ((), (), s32[]{:S(2)}) async-start(), calls=%async_computation.10 | async-start | bytes 16777216 | tf_op jit(solution)/shard_map/psum | solution.py:171
  949.5 614.1 %all-reduce.15.cloned.1.call-start = ((), (), s32[]{:S(2)}) async-start(), calls=%async_computation.11 | async-start | bytes 16777216 | tf_op jit(solution)/shard_map/psum | solution.py:220
  1259.5 17.2 slice-start.2
  1294.1 303.3 %reduce-scatter.17.cloned.1.call-start = ((), (), s32[]{:S(2)}) async-start(), calls=%async_computation.17 | async-start | bytes 2621440 | tf_op jit(solution)/shard_map/reduce_scatter | solution.py:230
  1302.8 11.9 copy-start.24
  1302.9 329.2 %reduce-scatter.15.cloned.1.call-start = ((), (), s32[]{:S(2)}) async-start(), calls=%async_computation.16 | async-start | bytes 2621440 | tf_op jit(solution)/shard_map/reduce_scatter | solution.py:229
  1309.6 347.4 %reduce-scatter.11.cloned.1.call-start = ((), (), s32[]{:S(2)}) async-start(), calls=%async_computation.14 | async-start | bytes 655360 | tf_op jit(solution)/shard_map/reduce_scatter | solution.py:227
  1316.3 365.2 %reduce-scatter.7.cloned.1.call-start = ((), (), s32[]{:S(2)}) async-start(), calls=%async_computation.12 | async-start | bytes 655360 | tf_op jit(solution)/shard_map/reduce_scatter | solution.py:225
  1320.1 243.6 %copy-start.45 = (f32[2048]{0:T(1024)S(1)}, f32[2048]{0:T(1024)}, u32[]{:S(2)}) copy-start(f32[2048]{0:T(1024)} %copy-done.44) | copy-start | bytes 24580
  1320.1 243.6 %copy-start.47 = (f32[2048]{0:T(1024)S(1)}, f32[2048]{0:T(1024)}, u32[]{:S(2)}) copy-start(f32[2048]{0:T(1024)} %copy-done.46) | copy-start | bytes 24580
  1320.1 386.3 %reduce-scatter.9.cloned.1.call-start = ((), (), s32[]{:S(2)}) async-start(), calls=%async_computation.13 | async-start | bytes 655360 | tf_op jit(solution)/shard_map/reduce_scatter | solution.py:226
  1323.9 407.2 %reduce-scatter.13.cloned.1.call-start = ((), (), s32[]{:S(2)}) async-start(), calls=%async_computation.15 | async-start | bytes 655360 | tf_op jit(solution)/shard_map/reduce_scatter | solution.py:228
  (62 other events, 330.8 us)
Sparse Core Ops, SparseCore 0:
  56.3 273.0 all-reduce.6
  348.7 269.4 all-reduce.8
  666.5 77.0 all-reduce.10
  794.7 124.9 all-gather.1
  949.7 268.5 all-reduce.12
  1294.3 269.3 all-reduce.14
  1566.9 30.4 reduce-scatter.16
  1600.5 31.4 reduce-scatter.14
  1635.3 21.6 reduce-scatter.10
  1659.9 21.6 reduce-scatter.6
  1684.8 21.6 reduce-scatter.8
  1709.4 21.6 reduce-scatter.12
where the time goes:
time: 1750 us; the launch traced here: 1740 us
  waiting for transfers between devices  1360 us (78%)
  matrix products  179 us (10%)
  other arithmetic  134 us (8%)
  local copies, waits for them, and re-layouts  37.8 us (2%)
    psum x1, waiting for transfers between devices, on_device(): hidden_one = inputs + lax.psum(product(attended, w_proj), 'narrow')  273 us
    psum x1, waiting for transfers between devices, on_device(): grad_normed_two = lax.psum(through_t(grad_pre, w_in), 'narrow')  269 us
    psum x1, waiting for transfers between devices, on_device(): hidden_two = hidden_one + lax.psum(product(activated, w_out), 'narrow')  246 us
    psum x1, waiting for transfers between devices, on_device(): grad_normed_one = lax.psum(grad_normed_part, 'narrow')  234 us
    all_gather x1, waiting for transfers between devices, on_device(): grad_query_key = lax.all_gather(grad_slice, 'narrow', axis=1, tiled=True)  125 us
    psum x1, waiting for transfers between devices, on_device(): distance = lax.psum(2.0 * part_products - part_norms, 'narrow')  75.8 us
    dot_general x1, matrix products, on_device(): jnp.einsum('tj,tdj->td', grad_products, key_slices, preferred_element_typ...  40.1 us
  transfers between devices with their start and end apart: 12, of which 12 were waited for; matrix products, arithmetic and copies ran while one was open for 4% of the time, Pallas kernels for 0%

commit v1 on v0

v1 whole, which is shorter than its diff:
```python
import functools

import jax
import jax.numpy as jnp
from jax import lax
from jax.experimental import pallas as pl
from jax.experimental.pallas import tpu as pltpu
from jax.sharding import PartitionSpec as P

HD = 64
EPSILON = 1e-05
F32 = jnp.float32
BF16 = jnp.bfloat16
MESH = pl.DeviceIdType.MESH
J = 128
KEPT_BYTES = 44 * 2**20


def product(left, right):
    return jnp.dot(left, right, preferred_element_type=F32)


def through_t(grads, weight):
    return lax.dot_general(grads, weight, (((1,), (1,)), ((), ())), preferred_element_type=F32)


def outer_sum(left, right):
    return jnp.einsum("ta,tb->ab", left, right, preferred_element_type=F32)


def norm_parts(values):
    centred = values - jnp.mean(values, axis=-1, keepdims=True)
    inverse = lax.rsqrt(jnp.mean(centred * centred, axis=-1, keepdims=True) + EPSILON)
    return (centred * inverse, inverse)


def norm_back(grad_out, normed, inverse, gain):
    scaled = grad_out * gain
    grad_in = inverse * (
        scaled
        - jnp.mean(scaled, axis=-1, keepdims=True)
        - normed * jnp.mean(scaled * normed, axis=-1, keepdims=True)
    )
    return (grad_in, jnp.sum(grad_out * normed, axis=0))


def gelu_tanh(values):
    return jax.nn.gelu(values, approximate=True)


def gather_weight(shard):
    wide, nar = lax.axis_size("wide"), lax.axis_size("narrow")
    rows = shard.shape[0] // wide
    own = lax.dynamic_slice_in_dim(shard, lax.axis_index("wide") * rows, rows, 0)
    full = lax.all_gather(own, ("narrow", "wide"), axis=0, tiled=True)
    return full.reshape(nar, shard.shape[0], shard.shape[1])


def normalise(values):
    centred = values - jnp.mean(values, axis=-1, keepdims=True)
    inverse = lax.rsqrt(jnp.mean(centred * centred, axis=-1, keepdims=True) + EPSILON)
    return centred * inverse, inverse


def normalise_back(grad_out, normed, inverse, gain):
    scaled = grad_out * gain
    return inverse * (
        scaled
        - jnp.mean(scaled, axis=-1, keepdims=True)
        - normed * jnp.mean(scaled * normed, axis=-1, keepdims=True)
    )


def head_lanes(values, head):
    lanes = lax.broadcasted_iota(jnp.int32, values.shape, 1)
    return jnp.where(lanes // HD == head, values, jnp.zeros_like(values))


def allowed_keys(col_ref, row_ref, start, count, keys):
    query_segment = col_ref[pl.ds(start, count), 0:1]
    key_segment = row_ref[0, 0:1, 0:keys]
    spot = lax.broadcasted_iota(jnp.int32, (count, keys), 1)
    own = lax.broadcasted_iota(jnp.int32, (count, keys), 0) + start
    return (spot <= own) & (query_segment == key_segment)


def attend_kernel(heads, block, qkv_ref, col_ref, row_ref, out_ref, lse_ref):
    length = qkv_ref.shape[0]
    width = heads * HD
    for start in range(0, length, block):
        keys = start + block
        allowed = allowed_keys(col_ref, row_ref, start, block, keys)
        query = qkv_ref[start : start + block, 0:width]
        key = qkv_ref[0:keys, width : 2 * width]
        value = qkv_ref[0:keys, 2 * width : 3 * width]
        total = jnp.zeros((block, width), F32)
        for head in range(heads):
            scores = lax.dot_general(
                head_lanes(query, head), key, (((1,), (1,)), ((), ())), preferred_element_type=F32
            )
            scores = jnp.where(allowed, scores, -1e30)
            peak = jnp.max(scores, axis=-1, keepdims=True)
            expo = jnp.exp(scores - peak)
            sums = jnp.sum(expo, axis=-1, keepdims=True)
            out = jnp.dot(expo.astype(BF16), value, preferred_element_type=F32) / sums
            total = total + head_lanes(out, head)
            lse_ref[start : start + block, head : head + 1] = peak + jnp.log(sums)
        out_ref[start : start + block, :] = total.astype(BF16)


def attend(qkv, columns, row_form, seqs, heads):
    rows, wide = qkv.shape
    length = rows // seqs
    width = wide // 3
    return pl.pallas_call(
        functools.partial(attend_kernel, heads, min(256, length)),
        grid=(seqs,),
        out_shape=(
            jax.ShapeDtypeStruct((rows, width), BF16),
            jax.ShapeDtypeStruct((rows, heads), F32),
        ),
        in_specs=[
            pl.BlockSpec((length, wide), lambda s: (s, 0)),
            pl.BlockSpec((length, 1), lambda s: (s, 0)),
            pl.BlockSpec((1, 1, length), lambda s: (s, 0, 0)),
        ],
        out_specs=(
            pl.BlockSpec((length, width), lambda s: (s, 0)),
            pl.BlockSpec((length, heads), lambda s: (s, 0)),
        ),
        compiler_params=pltpu.CompilerParams(vmem_limit_bytes=40 * 2**20),
    )(qkv, columns, row_form)


def attend_back_kernel(
    heads, block, qkv_ref, grad_ref, lse_ref, col_ref, row_ref, out_ref, grad_key, grad_value
):
    length = qkv_ref.shape[0]
    width = heads * HD
    grad_key[...] = jnp.zeros_like(grad_key)
    grad_value[...] = jnp.zeros_like(grad_value)
    across = (((0,), (0,)), ((), ()))
    last = (((1,), (1,)), ((), ()))
    for start in range(0, length, block):
        keys = start + block
        allowed = allowed_keys(col_ref, row_ref, start, block, keys)
        query = qkv_ref[start : start + block, 0:width]
        key = qkv_ref[0:keys, width : 2 * width]
        value = qkv_ref[0:keys, 2 * width : 3 * width]
        grad = grad_ref[start : start + block, :]
        total = jnp.zeros((block, width), F32)
        for head in range(heads):
            own_query = head_lanes(query, head)
            own_grad = head_lanes(grad, head)
            scores = lax.dot_general(own_query, key, last, preferred_element_type=F32)
            probs = jnp.where(
                allowed, jnp.exp(scores - lse_ref[start : start + block, head : head + 1]), 0.0
            )
            grad_probs = lax.dot_general(own_grad, value, last, preferred_element_type=F32)
            delta = jnp.sum(probs * grad_probs, axis=-1, keepdims=True)
            grad_scores = (probs * (grad_probs - delta)).astype(BF16)
            total = total + head_lanes(
                jnp.dot(grad_scores, key, preferred_element_type=F32), head
            )
            grad_key[0:keys, :] += lax.dot_general(
                grad_scores, own_query, across, preferred_element_type=F32
            )
            grad_value[0:keys, :] += lax.dot_general(
                probs.astype(BF16), own_grad, across, preferred_element_type=F32
            )
        out_ref[start : start + block, 0:width] = (total * HD ** (-0.5)).astype(BF16)
    out_ref[:, width : 2 * width] = grad_key[...].astype(BF16)
    out_ref[:, 2 * width : 3 * width] = grad_value[...].astype(BF16)


def attend_back(qkv, grad, lse, columns, row_form, seqs, heads):
    rows, wide = qkv.shape
    length = rows // seqs
    width = wide // 3
    return pl.pallas_call(
        functools.partial(attend_back_kernel, heads, min(256, length)),
        grid=(seqs,),
        out_shape=jax.ShapeDtypeStruct((rows, wide), BF16),
        in_specs=[
            pl.BlockSpec((length, wide), lambda s: (s, 0)),
            pl.BlockSpec((length, width), lambda s: (s, 0)),
            pl.BlockSpec((length, heads), lambda s: (s, 0)),
            pl.BlockSpec((length, 1), lambda s: (s, 0)),
            pl.BlockSpec((1, 1, length), lambda s: (s, 0, 0)),
        ],
        out_specs=pl.BlockSpec((length, wide), lambda s: (s, 0)),
        scratch_shapes=[pltpu.VMEM((length, width), F32)] * 2,
        compiler_params=pltpu.CompilerParams(vmem_limit_bytes=48 * 2**20),
    )(qkv, grad, lse, columns, row_form)


INNER = 0.7978845608028654
CUBIC = 0.044715


def gelu_parts(values):
    tanh = jnp.tanh(INNER * (values + CUBIC * values * values * values))
    return 0.5 * values * (1.0 + tanh), tanh


def ffn_kernel(
    parts,
    att_ref,
    input_ref,
    gains_ref,
    proj_ref,
    bundle_ref,
    one_ref,
    two_ref,
    normed_ref,
    output_ref,
    key_ref,
    pre_ref,
    total,
):
    step = pl.program_id(0)
    nar, tok, local = att_ref.shape
    width = input_ref.shape[1]
    hidden = pre_ref.shape[2]
    piece = width // parts

    @pl.when(step == 0)
    def _():
        branch = input_ref[...].astype(F32)
        for n in range(nar):
            branch = branch + jnp.dot(att_ref[n], proj_ref[n], preferred_element_type=F32)
        one_ref[...] = branch
        total[...] = branch
        normed, _ = normalise(branch)
        normed_ref[...] = (normed * gains_ref[1:2, :]).astype(BF16)

    pre = jnp.zeros((tok, hidden), F32)
    for i in range(parts):
        pre = pre + jnp.dot(
            normed_ref[:, i * piece : (i + 1) * piece],
            bundle_ref[0, 0:piece, i * hidden : (i + 1) * hidden],
            preferred_element_type=F32,
        )
    pre_ref[0] = pre
    activated = gelu_parts(pre)[0].astype(BF16)
    total[...] += jnp.dot(activated, bundle_ref[0, piece:, :], preferred_element_type=F32)

    @pl.when(step == nar - 1)
    def _():
        hidden_two = total[...]
        two_ref[...] = hidden_two
        output_ref[...] = hidden_two.astype(BF16)
        normed, _ = normalise(hidden_two)
        query_key = (normed * gains_ref[2:3, :]).astype(BF16)
        for n in range(nar):
            key_ref[n] = query_key[:, n * (width // nar) : (n + 1) * (width // nar)]


def ffn(att, inputs, gains, bundle, hidden):
    nar, tok, local = att.shape
    width = inputs.shape[1]
    rows = 2 * hidden
    whole = pl.BlockSpec((tok, width), lambda s: (0, 0))
    return pl.pallas_call(
        functools.partial(ffn_kernel, width // hidden),
        grid=(nar,),
        out_shape=(
            jax.ShapeDtypeStruct((tok, width), F32),
            jax.ShapeDtypeStruct((tok, width), F32),
            jax.ShapeDtypeStruct((tok, width), BF16),
            jax.ShapeDtypeStruct((tok, width), BF16),
            jax.ShapeDtypeStruct((nar, tok, width // nar), BF16),
            jax.ShapeDtypeStruct((nar, tok, hidden), F32),
        ),
        in_specs=[
            pl.BlockSpec((nar, tok, local), lambda s: (0, 0, 0)),
            whole,
            pl.BlockSpec((3, width), lambda s: (0, 0)),
            pl.BlockSpec((nar, local, width), lambda s: (0, rows // local, 0)),
            pl.BlockSpec((1, rows, width), lambda s: (s, 0, 0)),
        ],
        out_specs=(
            whole,
            whole,
            whole,
            whole,
            pl.BlockSpec((nar, tok, width // nar), lambda s: (0, 0, 0)),
            pl.BlockSpec((1, tok, hidden), lambda s: (s, 0, 0)),
        ),
        scratch_shapes=[pltpu.VMEM((tok, width), F32)],
        compiler_params=pltpu.CompilerParams(vmem_limit_bytes=48 * 2**20),
    )(att, inputs, gains, bundle, bundle)


def ffn_back_kernel(
    parts,
    slices_ref,
    att_ref,
    cot_ref,
    one_ref,
    two_ref,
    gains_ref,
    pre_ref,
    proj_ref,
    bundle_ref,
    ffn_ref,
    grad_one_ref,
    grad_att_ref,
    proj_part_ref,
    gain_ref,
    grad_two,
    total,
):
    step = pl.program_id(0)
    nar, tok, local = att_ref.shape
    width = cot_ref.shape[1]
    hidden = pre_ref.shape[2]
    piece = width // parts
    last = (((1,), (1,)), ((), ()))

    @pl.when(step == 0)
    def _():
        grad_key = jnp.concatenate([slices_ref[n] for n in range(nar)], axis=1).astype(F32)
        normed, inverse = normalise(two_ref[...])
        gain_ref[1:2, :] = jnp.sum(grad_key * normed, axis=0, keepdims=True)
        grad = cot_ref[...].astype(F32) + normalise_back(
            grad_key, normed, inverse, gains_ref[2:3, :]
        )
        grad_two[...] = grad
        ffn_ref[...] = grad.astype(BF16)
        total[...] = jnp.zeros_like(total)

    pre = pre_ref[0]
    tanh = gelu_parts(pre)[1]
    slope = 0.5 * (1.0 + tanh) + 0.5 * pre * (1.0 - tanh * tanh) * INNER * (
        1.0 + 3.0 * CUBIC * pre * pre
    )
    grad_act = lax.dot_general(
        ffn_ref[...], bundle_ref[0, piece:, :], last, preferred_element_type=F32
    )
    grad_pre = (slope * grad_act).astype(BF16)
    for i in range(parts):
        total[:, i * piece : (i + 1) * piece] += lax.dot_general(
            grad_pre,
            bundle_ref[0, 0:piece, i * hidden : (i + 1) * hidden],
            last,
            preferred_element_type=F32,
        )

    @pl.when(step == nar - 1)
    def _():
        normed, inverse = normalise(one_ref[...])
        gain_ref[0:1, :] = jnp.sum(total[...] * normed, axis=0, keepdims=True)
        grad = grad_two[...] + normalise_back(total[...], normed, inverse, gains_ref[1:2, :])
        grad_one_ref[...] = grad
        branch = grad.astype(BF16)
        for n in range(nar):
            grad_att_ref[n] = lax.dot_general(
                branch, proj_ref[n], last, preferred_element_type=F32
            ).astype(BF16)
            proj_part_ref[n] = lax.dot_general(
                att_ref[n], branch, (((0,), (0,)), ((), ())), preferred_element_type=F32
            ).astype(BF16)


def ffn_back(slices, att, cot, one, two, gains, pre, bundle):
    nar, tok, local = att.shape
    width = cot.shape[1]
    hidden = pre.shape[2]
    rows = 2 * hidden
    whole = pl.BlockSpec((tok, width), lambda s: (0, 0))
    stack = pl.BlockSpec((nar, tok, local), lambda s: (0, 0, 0))
    return pl.pallas_call(
        functools.partial(ffn_back_kernel, width // hidden),
        grid=(nar,),
        out_shape=(
            jax.ShapeDtypeStruct((tok, width), BF16),
            jax.ShapeDtypeStruct((tok, width), F32),
            jax.ShapeDtypeStruct((nar, tok, local), BF16),
            jax.ShapeDtypeStruct((nar, local, width), BF16),
            jax.ShapeDtypeStruct((2, width), F32),
        ),
        in_specs=[
            pl.BlockSpec(slices.shape, lambda s: (0, 0, 0)),
            stack,
            whole,
            whole,
            whole,
            pl.BlockSpec((3, width), lambda s: (0, 0)),
            pl.BlockSpec((1, tok, hidden), lambda s: (s, 0, 0)),
            pl.BlockSpec((nar, local, width), lambda s: (0, rows // local, 0)),
            pl.BlockSpec((1, rows, width), lambda s: (s, 0, 0)),
        ],
        out_specs=(
            whole,
            whole,
            stack,
            pl.BlockSpec((nar, local, width), lambda s: (0, 0, 0)),
            pl.BlockSpec((2, width), lambda s: (0, 0)),
        ),
        scratch_shapes=[pltpu.VMEM((tok, width), F32)] * 2,
        compiler_params=pltpu.CompilerParams(vmem_limit_bytes=48 * 2**20),
    )(slices, att, cot, one, two, gains, pre, bundle, bundle)


def exchange_kernel(nar, in_ref, out_ref, send, recv):
    me = lax.axis_index("narrow")
    greet([{"narrow": lax.rem(me + k, nar)} for k in range(1, nar)])

    def copy(k):
        target = lax.rem(me + k, nar)
        return pltpu.make_async_remote_copy(
            src_ref=in_ref.at[target],
            dst_ref=out_ref.at[me],
            send_sem=send.at[k],
            recv_sem=recv.at[k],
            device_id={"narrow": target},
            device_id_type=MESH,
        )

    for k in range(1, nar):
        copy(k).start()
    out_ref[me] = in_ref[me]
    for k in range(1, nar):
        copy(k).wait()


def exchange(values, name):
    nar = values.shape[0]
    vmem = pl.BlockSpec(memory_space=pltpu.VMEM)
    return pl.pallas_call(
        functools.partial(exchange_kernel, nar),
        out_shape=jax.ShapeDtypeStruct(values.shape, values.dtype),
        in_specs=[vmem],
        out_specs=vmem,
        scratch_shapes=[pltpu.SemaphoreType.DMA((nar,))] * 2,
        compiler_params=pltpu.CompilerParams(collective_id=name, has_side_effects=True),
    )(values)


def greet(peers):
    barrier = pltpu.get_barrier_semaphore()
    for peer in peers:
        pl.semaphore_signal(barrier, inc=1, device_id=peer, device_id_type=MESH)
    pl.semaphore_wait(barrier, len(peers))


def tail_kernel(
    nar,
    wid,
    first,
    chunks,
    grad_ref,
    weight_ref,
    input_ref,
    above_ref,
    gain_ref,
    sums_ref,
    out_ref,
    total_ref,
    got,
    own_sums,
    all_sums,
    pieces_out,
    pieces_in,
    a_send,
    a_recv,
    z_send,
    z_recv,
    y_send,
    y_recv,
    s_send,
    s_recv,
    p_send,
    p_recv,
):
    me = lax.axis_index("narrow")
    mine = lax.axis_index("wide")
    second = nar // first
    za, yb = me // second, lax.rem(me, second)
    tok = input_ref.shape[0]
    piece = total_ref.shape[1]
    part = tok // chunks

    def peer(k):
        return lax.rem(me + k, nar)

    greet(
        [{"narrow": peer(k)} for k in range(1, nar)]
        + [{"wide": lax.rem(mine + w, wid)} for w in range(1, wid)]
    )

    def remote(src, dst, send, recv, target):
        return pltpu.make_async_remote_copy(
            src_ref=src,
            dst_ref=dst,
            send_sem=send,
            recv_sem=recv,
            device_id=target,
            device_id_type=MESH,
        )

    def a_copy(k):
        return remote(
            grad_ref.at[peer(k)], got.at[k], a_send.at[k], a_recv.at[k], {"narrow": peer(k)}
        )

    def z_copy(i, c):
        rows = out_ref.at[me, pl.ds(c * part, part)]
        target = lax.rem(za + i, first) * second + yb
        return remote(rows, rows, z_send.at[i, c], z_recv.at[i, c], {"narrow": target})

    def y_copy(i, j, c):
        source = lax.rem(za + first - i, first) * second + yb
        rows = out_ref.at[source, pl.ds(c * part, part)]
        target = za * second + lax.rem(yb + j, second)
        return remote(rows, rows, y_send.at[i, j, c], y_recv.at[i, j, c], {"narrow": target})

    def s_copy(k):
        return remote(own_sums, all_sums.at[k], s_send.at[k], s_recv.at[k], {"narrow": peer(k)})

    def p_copy(w):
        target = lax.rem(mine + w, wid)
        return remote(
            pieces_out.at[target], pieces_in.at[w], p_send.at[w], p_recv.at[w], {"wide": target}
        )

    for k in range(1, nar):
        a_copy(k).start()
    normed, inverse = normalise(input_ref[...].astype(F32))
    total = jnp.dot(grad_ref[me], weight_ref[me], preferred_element_type=F32)
    for k in range(1, nar):
        a_copy(k).wait_recv()
        total = total + jnp.dot(
            got[k], weight_ref[lax.rem(me + nar - k, nar)], preferred_element_type=F32
        )
    grad = above_ref[...] + normalise_back(total, normed, inverse, gain_ref[0:1, :])
    out_ref[me] = grad.astype(BF16)
    own_sums[...] = sums_ref[...]
    own_sums[0:1, :] = jnp.sum(total * normed, axis=0, keepdims=True)
    for k in range(1, nar):
        s_copy(k).start()
    for c in range(chunks):
        for i in range(1, first):
            z_copy(i, c).start()
        for j in range(1, second):
            y_copy(0, j, c).start()
    sums = own_sums[...]
    for k in range(1, nar):
        s_copy(k).wait_recv()
        sums = sums + all_sums[k]
    for w in range(wid):
        pieces_out[w] = sums[:, w * piece : (w + 1) * piece]
    for w in range(1, wid):
        p_copy(w).start()
    for c in range(chunks):
        for i in range(1, first):
            z_copy(i, c).wait_recv()
            for j in range(1, second):
                y_copy(i, j, c).start()
    answer = pieces_out[mine]
    for w in range(1, wid):
        p_copy(w).wait()
        answer = answer + pieces_in[w]
    total_ref[...] = answer
    for k in range(1, nar):
        a_copy(k).wait_send()
        s_copy(k).wait_send()
    for c in range(chunks):
        for i in range(1, first):
            z_copy(i, c).wait_send()
        for i in range(first):
            for j in range(1, second):
                y_copy(i, j, c).wait()


def tail(grads, weights, inputs, above, gain, sums, wid, name):
    nar, tok, columns = grads.shape
    width = inputs.shape[1]
    first = 4 if nar % 4 == 0 else nar
    second = nar // first
    chunks = 4
    vmem = pl.BlockSpec(memory_space=pltpu.VMEM)
    dma = pltpu.SemaphoreType.DMA
    return pl.pallas_call(
        functools.partial(tail_kernel, nar, wid, first, chunks),
        out_shape=(
            jax.ShapeDtypeStruct((nar, tok, width), BF16),
            jax.ShapeDtypeStruct((8, width // wid), F32),
        ),
        in_specs=[vmem] * 6,
        out_specs=(vmem, vmem),
        scratch_shapes=[
            pltpu.VMEM((nar, tok, columns), BF16),
            pltpu.VMEM((8, width), F32),
            pltpu.VMEM((nar, 8, width), F32),
            pltpu.VMEM((wid, 8, width // wid), F32),
            pltpu.VMEM((wid, 8, width // wid), F32),
            dma((nar,)),
            dma((nar,)),
            dma((first, chunks)),
            dma((first, chunks)),
            dma((first, second, chunks)),
            dma((first, second, chunks)),
            dma((nar,)),
            dma((nar,)),
            dma((wid,)),
            dma((wid,)),
        ],
        compiler_params=pltpu.CompilerParams(
            collective_id=name, has_side_effects=True, vmem_limit_bytes=48 * 2**20
        ),
    )(grads, weights, inputs, above, gain, sums)


def neighbour_kernel(
    nar,
    tiles,
    tile,
    kept,
    ring,
    query_ref,
    keys_ref,
    norms_ref,
    ids_ref,
    cols_ref,
    scal_ref,
    grad_ref,
    loss_ref,
    stat_ref,
    queries,
    partial,
    dist,
    grads,
    sends,
    slots,
    loss_own,
    slot_sem,
    q_send,
    q_recv,
    d_send,
    d_recv,
    g_send,
    g_recv,
    l_send,
    l_recv,
    o_send,
    o_recv,
):
    me = lax.axis_index("narrow")
    tok = query_ref.shape[1]
    depth = query_ref.shape[2]
    group = 16
    per_block = tok // tile
    late = tiles - kept

    def peer(k):
        return lax.rem(me + k, nar)

    def origin(k):
        return lax.rem(me + nar - k, nar)

    def remote(src, dst, send, recv, target):
        return pltpu.make_async_remote_copy(
            src_ref=src,
            dst_ref=dst,
            send_sem=send,
            recv_sem=recv,
            device_id={"narrow": target},
            device_id_type=MESH,
        )

    def load(index, slot):
        block, sub = index // per_block, lax.rem(index, per_block)
        row = origin(block) * tok + sub * tile
        return pltpu.make_async_copy(
            keys_ref.at[pl.ds(row, tile)], slots.at[slot], slot_sem.at[slot]
        )

    for i in range(kept + ring):
        load(i, i).start()

    barrier = pltpu.get_barrier_semaphore()
    for k in range(1, nar):
        pl.semaphore_signal(
            barrier, inc=1, device_id={"narrow": peer(k)}, device_id_type=MESH
        )
    pl.semaphore_wait(barrier, nar - 1)

    def q_copy(k):
        return remote(
            query_ref.at[peer(k)], queries.at[k], q_send.at[k], q_recv.at[k], peer(k)
        )

    def d_copy(k):
        return remote(partial.at[k], dist.at[k], d_send.at[k], d_recv.at[k], origin(k))

    def g_copy(k):
        return remote(grads.at[0], grads.at[k], g_send.at[k], g_recv.at[k], peer(k))

    def l_copy(k):
        return remote(loss_own, loss_ref.at[me], l_send.at[k], l_recv.at[k], peer(k))

    def o_copy(k):
        return remote(sends.at[k], grad_ref.at[me], o_send.at[k], o_recv.at[k], origin(k))

    for k in range(1, nar):
        q_copy(k).start()
    queries[0] = query_ref[me]

    row_of = lax.broadcasted_iota(jnp.int32, (group, J), 0)

    def slot_of(index):
        return jnp.where(index < kept, index, kept + lax.rem(index - kept, ring))

    def slot_late(n):
        return kept + lax.rem(n, ring)

    def forward_tile(k, sub, slot):
        def one(g, carry):
            at = pl.multiple_of(sub * tile + g * group, group)
            own = queries[k, pl.ds(at, group), :].astype(F32)
            keys = slots[slot, pl.ds(g * group, group), :, :].reshape(group * depth, J)
            wide = jnp.concatenate(
                [jnp.where(row_of[:, :depth] == t, own, 0.0) for t in range(group)], axis=1
            ).astype(BF16)
            out = jnp.dot(wide, keys, preferred_element_type=F32)
            row = pl.multiple_of(origin(k) * tok + at, group)
            partial[k, pl.ds(at, group), :] = 2.0 * out - norms_ref[pl.ds(row, group), :]
            return carry

        lax.fori_loop(0, tile // group, one, 0, unroll=True)

    def forward_block(k):
        def body(sub, carry):
            index = k * per_block + sub
            slot = slot_of(index)
            load(index, slot).wait()
            forward_tile(k, sub, slot)

            @pl.when(index >= kept)
            def _():
                nxt = index - kept + ring

                @pl.when(nxt < 2 * late)
                def _():
                    load(kept + lax.rem(nxt, late), slot).start()

            return carry

        lax.fori_loop(0, per_block, body, 0)

    forward_block(0)

    def forward_rest(k, carry):
        q_copy(k).wait_recv()
        forward_block(k)
        d_copy(k).start()
        return carry

    lax.fori_loop(1, nar, forward_rest, 0)

    def collect(k, total):
        d_copy(k).wait_recv()
        return total + dist[k]

    distance = lax.fori_loop(1, nar, collect, partial[0])
    temper_value = scal_ref[0]
    mix_value = scal_ref[1]
    count = cols_ref[:, 0:1]
    target = cols_ref[:, 1:2]
    base = cols_ref[:, 2:3]
    loss_weight = cols_ref[:, 3:4]
    logits = distance / temper_value
    spot = lax.broadcasted_iota(jnp.int32, (tok, J), 1).astype(F32)
    masked = jnp.where(spot < count, logits, -1e30)
    peak = jnp.max(masked, axis=-1, keepdims=True)
    expo = jnp.exp(masked - peak)
    weights = expo / jnp.sum(expo, axis=-1, keepdims=True)
    matches = jnp.where(ids_ref[...].astype(F32) == target, 1.0, 0.0)
    knn_prob = jnp.sum(weights * matches, axis=-1, keepdims=True)
    mixture = mix_value * knn_prob + (1.0 - mix_value) * base
    grad_mixture = -loss_weight / mixture
    grad_logits = weights * (mix_value * grad_mixture) * (matches - knn_prob)
    grads[0] = (2.0 * grad_logits / temper_value).astype(BF16)
    for k in range(1, nar):
        g_copy(k).start()
    loss = jnp.transpose(jnp.broadcast_to(-jnp.log(mixture), (tok, J)))[0:8, :]
    loss_own[...] = loss
    for k in range(1, nar):
        l_copy(k).start()
    loss_ref[me] = loss
    term_temper = -jnp.sum(grad_logits * logits, axis=0, keepdims=True) / temper_value
    term_mix = jnp.sum((knn_prob - base) * grad_mixture, axis=0, keepdims=True)
    stat_ref[0:1, :] = term_temper
    stat_ref[1:2, :] = jnp.broadcast_to(term_mix, (1, J))

    def backward_tile(k, sub, slot):
        def one(g, carry):
            at = pl.multiple_of(sub * tile + g * group, group)
            own = grads[k, pl.ds(at, group), :]
            keys = slots[slot, pl.ds(g * group, group), :, :].reshape(group * depth, J)
            out = lax.dot_general(
                own, keys, (((1,), (1,)), ((), ())), preferred_element_type=F32
            )
            total = jnp.zeros((group, depth), F32)
            for t in range(group):
                total = jnp.where(
                    row_of[:, :depth] == t, out[:, t * depth : (t + 1) * depth], total
                )
            sends[k, pl.ds(at, group), :] = total.astype(BF16)
            return carry

        lax.fori_loop(0, tile // group, one, 0, unroll=True)

    def backward_block(k):
        def body(sub, carry):
            index = k * per_block + sub

            @pl.when(index < kept)
            def _():
                backward_tile(k, sub, index)

            @pl.when(index >= kept)
            def _():
                n = index - kept + late
                slot = slot_late(n)
                load(index, slot).wait()
                backward_tile(k, sub, slot)

                @pl.when(n + ring < 2 * late)
                def _():
                    load(kept + lax.rem(n + ring, late), slot).start()

            return carry

        lax.fori_loop(0, per_block, body, 0)

    backward_block(0)
    grad_ref[me] = sends[0]

    def backward_rest(k, carry):
        g_copy(k).wait_recv()
        backward_block(k)
        o_copy(k).start()
        return carry

    lax.fori_loop(1, nar, backward_rest, 0)

    for k in range(1, nar):
        q_copy(k).wait_send()
        d_copy(k).wait_send()
        g_copy(k).wait_send()
        l_copy(k).wait()
        o_copy(k).wait()


def neighbours(nar, query, keys, norms, ids, cols, scal):
    tok, depth = query.shape[1:]
    rows = keys.shape[0]
    tile = 32
    tiles = rows // tile
    bytes_tile = tile * depth * J * 2
    ring = 4
    kept = min(tiles - 2 * ring, (KEPT_BYTES // bytes_tile))
    late = tiles - kept
    vmem = pl.BlockSpec(memory_space=pltpu.VMEM)
    dma = pltpu.SemaphoreType.DMA((nar,))
    return pl.pallas_call(
        functools.partial(neighbour_kernel, nar, tiles, tile, kept, ring),
        out_shape=(
            jax.ShapeDtypeStruct((nar, tok, depth), BF16),
            jax.ShapeDtypeStruct((nar, 8, tok), F32),
            jax.ShapeDtypeStruct((2, J), F32),
        ),
        in_specs=[
            vmem,
            pl.BlockSpec(memory_space=pl.ANY),
            vmem,
            vmem,
            vmem,
            pl.BlockSpec(memory_space=pltpu.SMEM),
        ],
        out_specs=(vmem, vmem, vmem),
        scratch_shapes=[
            pltpu.VMEM((nar, tok, depth), BF16),
            pltpu.VMEM((nar, tok, J), F32),
            pltpu.VMEM((nar, tok, J), F32),
            pltpu.VMEM((nar, tok, J), BF16),
            pltpu.VMEM((nar, tok, depth), BF16),
            pltpu.VMEM((kept + ring, tile, depth, J), BF16),
            pltpu.VMEM((8, tok), F32),
            pltpu.SemaphoreType.DMA((kept + ring,)),
        ]
        + [dma] * 10,
        compiler_params=pltpu.CompilerParams(
            collective_id=1, has_side_effects=True, vmem_limit_bytes=60 * 2**20
        ),
    )(query, keys, norms, ids, cols, scal)


def on_device(
    block_input,
    output_cotangent,
    loss_weight,
    segments,
    nbr_keys,
    nbr_count,
    nbr_ids,
    targets,
    base_prob,
    w_query,
    w_key,
    w_value,
    w_proj,
    w_in,
    w_out,
    gain_attn,
    gain_ffn,
    gain_key,
    temper,
    mix_weight,
):
    seqs_here, length, width = block_input.shape
    rows = seqs_here * length
    nar = lax.axis_size("narrow")
    own = lax.axis_index("narrow")
    tok = rows // nar
    local_width = w_query.shape[0]
    heads_here = local_width // HD
    scale = HD ** (-0.5)

    def mine(values):
        flat = values.reshape((rows,) + values.shape[2:])
        return lax.dynamic_slice_in_dim(flat, own * tok, tok, 0)

    wid = lax.axis_size("wide")
    hidden = w_in.shape[1]
    parts = width // hidden
    packed = w_in.reshape(parts, width // parts, hidden).transpose(1, 0, 2)
    bundle = gather_weight(
        jnp.concatenate([packed.reshape(width // parts, width), w_out, w_proj], axis=0)
    )

    inputs = block_input.reshape(rows, width).astype(F32)
    normed_in, _ = norm_parts(inputs)
    normed_one = (normed_in * gain_attn).astype(BF16)
    w_qkv = jnp.concatenate([w_query, w_key, w_value], axis=0)
    column_scale = jnp.where(jnp.arange(3 * local_width) < local_width, scale, 1.0)
    qkv = (through_t(normed_one, w_qkv) * column_scale[None, :]).astype(BF16)
    seg_column = segments.reshape(rows, 1)
    seg_row = segments.reshape(seqs_here, 1, length)
    attended, lse = attend(qkv, seg_column, seg_row, seqs_here, heads_here)

    key_slices = nbr_keys.reshape(rows, nbr_keys.shape[2], nbr_keys.shape[3])
    part_norms = jnp.einsum("tdj,tdj->tj", key_slices, key_slices, preferred_element_type=F32)

    attended_own = exchange(attended.reshape(nar, tok, local_width), 2)
    inputs_own = mine(block_input)
    gains = jnp.stack([gain_attn, gain_ffn, gain_key])
    hidden_one, hidden_two, normed_two, output_own, query_key, pre_act = ffn(
        attended_own, inputs_own, gains, bundle, hidden
    )
    normed_two_all = lax.all_gather(normed_two, "narrow", axis=0, tiled=True)
    block_output = lax.all_gather(output_own, "narrow", axis=0, tiled=True)
    cols = jnp.stack(
        [
            mine(nbr_count).astype(F32),
            mine(targets).astype(F32),
            mine(base_prob),
            mine(loss_weight),
        ],
        axis=1,
    )
    grad_slices, losses, stats = neighbours(
        nar,
        query_key,
        key_slices,
        part_norms,
        mine(nbr_ids),
        cols,
        jnp.concatenate([temper, mix_weight]),
    )
    token_loss = losses[:, 0, :]
    grad_ffn, grad_hidden_one, grad_attended, proj_part, gain_sums = ffn_back(
        grad_slices,
        attended_own,
        mine(output_cotangent),
        hidden_one,
        hidden_two,
        gains,
        pre_act,
        bundle,
    )
    grad_ffn_all = lax.all_gather(grad_ffn, "narrow", axis=0, tiled=True)
    grad_w_proj = lax.psum_scatter(proj_part, "narrow", scatter_dimension=0, tiled=True)[0]
    qkv_all = gather_weight(w_qkv)

    grad_attended = exchange(grad_attended, 3).reshape(rows, local_width)
    grad_qkv = attend_back(qkv, grad_attended, lse, seg_column, seg_row, seqs_here, heads_here)
    sums = jnp.concatenate(
        [
            jnp.zeros((1, width), F32),
            gain_sums,
            jnp.broadcast_to(jnp.sum(stats[0]), (1, width)),
            jnp.broadcast_to(stats[1, 0], (1, width)),
            jnp.zeros((3, width), F32),
        ],
        axis=0,
    )
    grad_input, totals = tail(
        grad_qkv.reshape(nar, tok, 3 * local_width),
        qkv_all,
        inputs_own,
        grad_hidden_one,
        gains,
        sums,
        wid,
        4,
    )

    pre_loc = product(normed_two_all, w_in)
    act_loc = gelu_tanh(pre_loc).astype(BF16)
    grad_pre_loc = jax.vjp(gelu_tanh, pre_loc)[1](through_t(grad_ffn_all, w_out))[0].astype(BF16)
    grad_w_in = outer_sum(normed_two_all, grad_pre_loc)
    grad_w_out = outer_sum(act_loc, grad_ffn_all)
    grad_w_qkv = outer_sum(grad_qkv, normed_one)

    by_column = jnp.concatenate(
        [grad_w_qkv.astype(BF16), grad_w_proj, grad_w_out.astype(BF16)], axis=0
    )
    by_column = lax.psum_scatter(by_column, "wide", scatter_dimension=1, tiled=True).astype(F32)
    by_row = lax.psum_scatter(
        grad_w_in.astype(BF16), "wide", scatter_dimension=0, tiled=True
    ).astype(F32)

    return (
        block_output.reshape(seqs_here, length, width),
        token_loss.reshape(seqs_here, length),
        grad_input.astype(F32).reshape(seqs_here, length, width),
        by_column[:local_width],
        by_column[local_width : 2 * local_width],
        by_column[2 * local_width : 3 * local_width],
        by_column[3 * local_width : 4 * local_width],
        by_row,
        by_column[4 * local_width :],
        totals[0],
        totals[1],
        totals[2],
        totals[3, 0:1],
        totals[4, 0:1],
    )


def solution(mesh):
    return jax.shard_map(
        on_device,
        mesh=mesh,
        in_specs=(
            P("wide", None, None),
            P("wide", None, None),
            P("wide", None),
            P("wide", None),
            P("wide", None, "narrow", None),
            P("wide", None),
            P("wide", None, None),
            P("wide", None),
            P("wide", None),
            P("narrow", None),
            P("narrow", None),
            P("narrow", None),
            P("narrow", None),
            P(None, "narrow"),
            P("narrow", None),
            P(),
            P(),
            P(),
            P(),
            P(),
        ),
        out_specs=(
            P("wide", None, None),
            P("wide", None),
            P("wide", None, None),
            P("narrow", "wide"),
            P("narrow", "wide"),
            P("narrow", "wide"),
            P("narrow", "wide"),
            P("wide", "narrow"),
            P("narrow", "wide"),
            P("wide"),
            P("wide"),
            P("wide"),
            P(),
            P(),
        ),
        check_vma=False,
    )
```

time: 1750 us -> 769 us (0.44)
  waiting for transfers between devices: 1360 us -> 284 us
  Pallas kernels: 0 us -> 352 us
  matrix products: 179 us -> 26.8 us
  other arithmetic: 134 us -> 42.9 us
    psum x5 -> x0, waiting for transfers between devices: 1100 us -> none  [the longest x1 273 us: on_device(): hidden_one = inputs + lax.psum(product(attended, w_proj), 'narrow')]
    pallas_call x0 -> x8, Pallas kernels: none -> 352 us  [the longest x1 149 us: tail(): pl.pallas_call(functools.partial(tail_kernel, nar, wid, first, chunks), o...]
    dot_general x26 -> x4, matrix products: 155 us -> 24.4 us  [the longest x3 17.5 us: outer_sum(): return jnp.einsum('ta,tb->ab', left, right, preferred_element_type=F32)]
    all_gather x1 -> x5, waiting for transfers between devices: 125 us -> 214 us  [the longest x2 150 us: gather_weight(): full = lax.all_gather(own, ('narrow', 'wide'), axis=0, tiled=True)]
    reduce_scatter x6 -> x3, waiting for transfers between devices: 135 us -> 69.3 us  [the longest x1 32.9 us: on_device(): lax.psum_scatter(by_column, 'wide', scatter_dimension=1, tiled=True)]
    reduce_sum x10 -> x1, other arithmetic: 35.5 us -> 0.6 us  [on_device(): jnp.sum(stats[0])]
    add x6 -> x0, other arithmetic: 24.6 us -> none  [the longest x1 11.9 us: on_device(): grad_input_rows = grad_hidden_one + grad_input_n]
    dot_general x6 -> x1, matrix products: 24.2 us -> 2.43 us  [through_t(): lax.dot_general(grads, weight, (((1,), (1,)), ((), ())), preferred_elemen...]
  transfers between devices with their start and end apart: 12 -> 8, of which waited for: 12 -> 6; matrix products, arithmetic and copies ran while one was open for 4% -> 11% of each run, Pallas kernels for 0% -> 44%
where the time goes in v1:
time: 769 us; the launch traced here: 766 us
  Pallas kernels  352 us (46%)
  waiting for transfers between devices  284 us (37%)
  other arithmetic  42.9 us (6%)
  local copies, waits for them, and re-layouts  41.6 us (5%)
  matrix products  26.8 us (3%)
  between operations  16.3 us (2%)
    all_gather x2, waiting for transfers between devices, gather_weight(): full = lax.all_gather(own, ('narrow', 'wide'), axis=0, tiled=True)  150 us
    pallas_call x1, Pallas kernels, tail(): pl.pallas_call(functools.partial(tail_kernel, nar, wid, first, chunks), o...  149 us
    pallas_call x1, Pallas kernels, neighbours(): pl.pallas_call(functools.partial(neighbour_kernel, nar, tiles, tile, kept...  110 us
    all_gather x1, waiting for transfers between devices, on_device(): grad_ffn_all = lax.all_gather(grad_ffn, 'narrow', axis=0, tiled=True)  64 us
    pallas_call x2, Pallas kernels, exchange(): pl.pallas_call(functools.partial(exchange_kernel, nar), out_shape=jax.Sha...  39.8 us
    reduce_scatter x1, waiting for transfers between devices, on_device(): lax.psum_scatter(by_column, 'wide', scatter_dimension=1, tiled=True)  32.9 us
    unnamed x84, local copies, waits for them, and re-layouts  25.7 us
    reduce_scatter x1, waiting for transfers between devices, on_device(): lax.psum_scatter(proj_part, 'narrow', scatter_dimension=0, tiled=True)[0]  25.7 us
  transfers between devices with their start and end apart: 8, of which 6 were waited for; matrix products, arithmetic and copies ran while one was open for 11% of the time, Pallas kernels for 44%

profile of v1, /device:TPU:0, one launch (start us, length us, event | category | flops | bytes accessed | tf_op | source)
XLA Modules:
  0.0 765.6 jit_solution(3189725453350493346)
XLA Ops:
  7.3 2.5 copy.43
  16.2 2.8 convert_reduce_fusion
  22.2 2.4 multiply_convert_fusion.2.qkv_ref
  24.7 7.0 shard_map.299
  34.6 22.4 %shard_map.300.att_ref = bf16[8,256,128]{2,1,0:T(8,128)(2,1)} custom-call(bf16[8,256,128]{2,1,0:T(8,128)(2,1)} %bitcast.81), custom_call_target="tpu_custom_call" | custom-call | tf_op jit(solution)/shard_map/pallas_call | solution.py:431
  58.2 85.3 %all-gather.6.cloned.1.call-done = bf16[9216,1024]{1,0:T(8,128)(2,1)} async-done(((bf16[288,1024]{1,0:T(8,128)(2,1)}), bf16[9216,1024]{1,0:T(8,128)(2,1)}) %all-gather.6.cloned.1.call-update) | async-done | bytes 18874384 | tf_op jit(solution)/shard_map/all_gather | solution.py:55
  144.5 15.5 %shard_map.301 = (f32[256,1024]{1,0:T(8,128)S(1)}, f32[256,1024]{1,0:T(8,128)S(1)}, bf16[256,1024]{1,0:T(8,128)(2,1)}, bf16[256,1024]{1,0:T(8,128)(2,1)}, bf16[8...) custom-call(bf16[8,256,128]{2,1,0:T(8,128)(2,1)S(1)} %copy-done.6, ...), custom_call_target="tpu_custom_call" | custom-call | tf_op jit(solution)/shard_map/pallas_call | solution.py:264
  167.8 22.6 %fusion.norms_ref = f32[2048,128]{1,0:T(8,128)} fusion(bf16[2,1024,128,128]{3,2,1,0:T(8,128)(2,1)} %param.24), kind=kLoop, calls=%fused_computation.1 | loop fusion | flops 100401152 | bytes 68157440 | tf_op jit(solution)/shard_map/tdj,tdj->tj/dot_general | solution.py:956
  190.4 110.4 %shard_map.302 = (bf16[8,256,128]{2,1,0:T(8,128)(2,1)}, f32[8,8,256]{2,1,0:T(8,128)}, f32[2,128]{1,0:T(2,128)}) custom-call(bf16[8,256,128]{2,1,0:T(8,128)(2,1)} %copy-done.17, bf16[2048,128,128]{2,1,0:T(8,128)(2,1)} %bitcast.11.keys_ref, f32[2048,128]{1,0:T(8,128)} %fusion.norms_ref, s32[256,128]{1,0:T(8,128)} %constant_dynamic-slice_fusion.2.ids_ref, ...), custom_call_target="tpu_custom_call" | custom-call | tf_op jit(solution)/shard_map/pallas_call | solution.py:869
  304.3 18.2 %shard_map.303 = (bf16[256,1024]{1,0:T(8,128)(2,1)}, f32[256,1024]{1,0:T(8,128)S(1)}, bf16[8,256,128]{2,1,0:T(8,128)(2,1)S(1)}, bf16[8,128,1024]{2,1,0:T(8,128)(2,1)}, f32[2,1024]{1,0:T(2,128)S(1)}) custom-call(bf16[8,256,128]{2,1,0:T(8,128)(2,1)S(1)} %copy-done.20, bf16[8,256,128]{2,1,0:T(8,128)(2,1)S(1)} %copy-done.7, ...), custom_call_target="tpu_custom_call" | custom-call | tf_op jit(solution)/shard_map/pallas_call | solution.py:373
  326.5 6.8 fusion.40
  333.4 64.0 %all-gather.14.cloned.1.call-done = bf16[2048,1024]{1,0:T(8,128)(2,1)} async-done(((bf16[256,1024]{1,0:T(8,128)(2,1)}), bf16[2048,1024]{1,0:T(8,128)(2,1)}) %all-gather.14.cloned.1.call-update) | async-done | bytes 4194320 | tf_op jit(solution)/shard_map/all_gather | solution.py:995
  397.4 12.2 %fusion.18 = bf16[1024,512]{1,0:T(8,128)(2,1)} fusion(bf16[2048,1024]{1,0:T(8,128)(2,1)} %all-gather.12.cloned.1.call-done, f32[2048,512]{1,0:T(8,128)} %fusion.40, bf16[2048,1024]{1,0:T(8,128)(2,1)} %all-gather.14.cloned.1.call-done, bf16[512,1024]{1,0:T(8,128)(2,1)} %param.34), kind=kOutput, calls=%fused_computation.30 | convolution fusion | flops 4316463104 | bytes 14680064 | tf_op jit(solution)/shard_map/ta,tb->ab/dot_general | solution.py:28
  409.9 17.4 %shard_map.304 = bf16[8,256,128]{2,1,0:T(8,128)(2,1)} custom-call(bf16[8,256,128]{2,1,0:T(8,128)(2,1)} %copy-done.18), custom_call_target="tpu_custom_call" | custom-call | tf_op jit(solution)/shard_map/pallas_call | solution.py:431
  429.9 11.8 %shard_map.305 = bf16[2048,384]{1,0:T(8,128)(2,1)S(1)} custom-call(bf16[2048,384]{1,0:T(8,128)(2,1)S(1)} %copy-done.5, bf16[2048,128]{1,0:T(8,128)(2,1)S(1)} %bitcast.80, f32[2048,2]{1,0:T(8,128)S(1)} %copy-done.12, s32[2048,1]{1,0:T(8,128)S(1)} %bitcast.78, s32[2,1,1024]{2,1,0:T(1,128)S(1)} %reshape.129.row_ref), custom_call_target="tpu_custom_call" | custom-call | tf_op jit(solution)/shard_map/pallas_call | solution.py:180
  445.8 3.5 fusion.17
  449.3 25.7 %reduce-scatter.4.cloned.1.call-done = bf16[1,128,1024]{2,1,0:T(8,128)(2,1)} async-done(((bf16[8,128,1024]{2,1,0:T(8,128)(2,1)}), bf16[1,128,1024]{2,1,0:T(8,128)(2,1)}) %reduce-scatter.4.cloned.1.call-update) | async-done | bytes 262160 | tf_op jit(solution)/shard_map/reduce_scatter | solution.py:996
  475.0 2.8 pad_maximum_fusion
  481.8 64.6 %all-gather.10.cloned.1.call-done = bf16[3072,1024]{1,0:T(8,128)(2,1)} async-done(((bf16[96,1024]{1,0:T(8,128)(2,1)}), bf16[3072,1024]{1,0:T(8,128)(2,1)}) %all-gather.10.cloned.1.call-update) | async-done | bytes 6291472 | tf_op jit(solution)/shard_map/all_gather | solution.py:55
  547.6 149.5 %shard_map.306 = (bf16[8,256,1024]{2,1,0:T(8,128)(2,1)}, f32[8,256]{1,0:T(8,128)S(1)}) custom-call(bf16[8,256,384]{2,1,0:T(8,128)(2,1)S(1)} %bitcast.79, bf16[8,384,1024]{2,1,0:T(8,128)(2,1)} %bitcast.87, bf16[256,1024]{1,0:T(8,128)(2,1)S(1)} %constant_dynamic-slice_fusion.3.input_ref, f32[256,1024]{1,0:T(8,128)S(1)} %copy-done.10, ...), custom_call_target="tpu_custom_call" | custom-call | tf_op jit(solution)/shard_map/pallas_call | solution.py:585
  698.1 6.7 bitcast_convert_fusion
  704.9 10.6 %reduce-scatter.8.cloned.1.call-done = bf16[256,512]{1,0:T(8,128)(2,1)} async-done(((bf16[1024,512]{1,0:T(8,128)(2,1)}), bf16[256,512]{1,0:T(8,128)(2,1)}) %reduce-scatter.8.cloned.1.call-update) | async-done | bytes 262160 | tf_op jit(solution)/shard_map/reduce_scatter | solution.py:1033
  717.3 32.9 %reduce-scatter.6.cloned.1.call-done = bf16[1024,256]{1,0:T(8,128)(2,1)} async-done(((bf16[1024,1024]{1,0:T(8,128)(2,1)}), bf16[1024,256]{1,0:T(8,128)(2,1)}) %reduce-scatter.6.cloned.1.call-update) | async-done | bytes 524304 | tf_op jit(solution)/shard_map/reduce_scatter | solution.py:1032
  753.7 4.7 copy.76
  (136 shorter events, 46.9 us)
Async XLA Ops:
  7.2 158.9 %copy-start = (s32[2,1024,128]{2,1,0:T(8,128)S(1)}, s32[2,1024,128]{2,1,0:T(8,128)}, u32[]{:S(2)}) copy-start(s32[2,1024,128]{2,1,0:T(8,128)} %param.26) | copy-start | bytes 3145732
  7.2 5.3 copy-start.26
  7.2 136.2 %all-gather.6.cloned.1.call-start = ((), (), s32[]{:S(2)}) async-start(), calls=%async_computation.3 | async-start | bytes 19464192 | tf_op jit(solution)/shard_map/all_gather | solution.py:55
  11.8 314.7 %all-gather.12.cloned.1.call-start = ((), (), s32[]{:S(2)}) async-start(), calls=%async_computation.7 | async-start | bytes 4718592 | tf_op jit(solution)/shard_map/all_gather | solution.py:964
  12.9 6.1 copy-start.21
  16.2 4.3 copy-start.27
  22.2 34.8 %copy-start.32 = (f32[1024]{0:T(1024)S(1)}, f32[1024]{0:T(1024)}, u32[]{:S(2)}) copy-start(f32[1024]{0:T(1024)} %param.37) | copy-start | bytes 12292
  22.2 34.8 %copy-start.33 = (f32[1024]{0:T(1024)S(1)}, f32[1024]{0:T(1024)}, u32[]{:S(2)}) copy-start(f32[1024]{0:T(1024)} %param.36) | copy-start | bytes 12292
  144.5 18.6 %copy-start.28 = (s32[2,1024]{1,0:T(2,128)S(1)}, s32[2,1024]{1,0:T(2,128)}, u32[]{:S(2)}) copy-start(s32[2,1024]{1,0:T(2,128)} %param.27) | copy-start | bytes 24580
  144.5 18.6 %copy-start.29 = (s32[2,1024]{1,0:T(2,128)S(1)}, s32[2,1024]{1,0:T(2,128)}, u32[]{:S(2)}) copy-start(s32[2,1024]{1,0:T(2,128)} %param.25) | copy-start | bytes 24580
  144.5 18.6 %copy-start.30 = (f32[2,1024]{1,0:T(2,128)S(1)}, f32[2,1024]{1,0:T(2,128)}, u32[]{:S(2)}) copy-start(f32[2,1024]{1,0:T(2,128)} %param.28) | copy-start | bytes 24580
  144.5 18.7 %copy-start.31 = (f32[2,1024]{1,0:T(2,128)S(1)}, f32[2,1024]{1,0:T(2,128)}, u32[]{:S(2)}) copy-start(f32[2,1024]{1,0:T(2,128)} %param.22) | copy-start | bytes 24580
  162.8 234.6 %all-gather.14.cloned.1.call-start = ((), (), s32[]{:S(2)}) async-start(), calls=%async_computation.8 | async-start | bytes 4718592 | tf_op jit(solution)/shard_map/all_gather | solution.py:995
  190.4 110.4 %copy-start.7 = (bf16[8,256,128]{2,1,0:T(8,128)(2,1)S(1)}, bf16[8,256,128]{2,1,0:T(8,128)(2,1)}, u32[]{:S(2)}) copy-start(bf16[8,256,128]{2,1,0:T(8,128)(2,1)} %shard_map.300.att_ref) | copy-start | bytes 1572868
  324.3 150.7 %reduce-scatter.4.cloned.1.call-start = ((), (), s32[]{:S(2)}) async-start(), calls=%async_computation.6 | async-start | bytes 2359296 | tf_op jit(solution)/shard_map/reduce_scatter | solution.py:996
  324.9 221.4 %all-gather.10.cloned.1.call-start = ((), (), s32[]{:S(2)}) async-start(), calls=%async_computation.5 | async-start | bytes 6488064 | tf_op jit(solution)/shard_map/all_gather | solution.py:55
  325.7 379.2 %all-gather.8.cloned.1.call-start = ((), (), s32[]{:S(2)}) async-start(), calls=%async_computation.4 | async-start | bytes 4718592 | tf_op jit(solution)/shard_map/all_gather | solution.py:965
  326.3 389.2 %reduce-scatter.8.cloned.1.call-start = ((), (), s32[]{:S(2)}) async-start(), calls=%async_computation.10 | async-start | bytes 1310720 | tf_op jit(solution)/shard_map/reduce_scatter | solution.py:1033
  333.4 94.0 %copy-start.12 = (f32[2048,2]{1,0:T(8,128)S(1)}, f32[2048,2]{1,0:T(8,128)}, u32[]{:S(2)}) copy-start(f32[2048,2]{1,0:T(8,128)} %copy-done.11) | copy-start | bytes 49156
  409.6 340.6 %reduce-scatter.6.cloned.1.call-start = ((), (), s32[]{:S(2)}) async-start(), calls=%async_computation.9 | async-start | bytes 2621440 | tf_op jit(solution)/shard_map/reduce_scatter | solution.py:1032
  429.9 11.8 %copy-start.23 = (bf16[2048,1024]{1,0:T(8,128)(2,1)S(1)}, bf16[2048,1024]{1,0:T(8,128)(2,1)}, u32[]{:S(2)}) copy-start(bf16[2048,1024]{1,0:T(8,128)(2,1)} %copy-done.22) | copy-start | bytes 12582916
  449.3 28.5 %copy-start.35 = (f32[2,128]{1,0:T(2,128)S(1)}, f32[2,128]{1,0:T(2,128)}, u32[]{:S(2)}) copy-start(f32[2,128]{1,0:T(2,128)} %get-tuple-element.44) | copy-start | bytes 3076
  449.3 97.0 %copy-start.3 = (bf16[2048,384]{1,0:T(8,128)(2,1)S(1)}, bf16[2048,384]{1,0:T(8,128)(2,1)}, u32[]{:S(2)}) copy-start(bf16[2048,384]{1,0:T(8,128)(2,1)} %copy-done.2) | copy-start | bytes 4718596
  753.7 4.7 copy-start.1
  (21 other events, 32.5 us)
Sparse Core Ops, SparseCore 0:
  12.0 131.4 all-gather.5
  163.0 108.9 all-gather.11
  324.5 72.8 all-gather.13
  400.8 74.2 reduce-scatter.3
  477.8 68.5 all-gather.9
  548.9 137.4 all-gather.7
  689.0 26.4 reduce-scatter.7
  718.8 31.4 reduce-scatter.5

commit v2 on v1

v2 whole, which is shorter than its diff:
```python
import functools

import jax
import jax.numpy as jnp
from jax import lax
from jax.experimental import pallas as pl
from jax.experimental.pallas import tpu as pltpu
from jax.sharding import PartitionSpec as P

HD = 64
EPSILON = 1e-05
F32 = jnp.float32
BF16 = jnp.bfloat16
MESH = pl.DeviceIdType.MESH
J = 128
KEPT_BYTES = 44 * 2**20


def outer_sum(left, right):
    return jnp.einsum("ta,tb->ab", left, right, preferred_element_type=F32)


def place(index, second):
    return {"z": index // second, "y": lax.rem(index, second)}


def push(src, dst, send, recv, target):
    return pltpu.make_async_remote_copy(
        src_ref=src,
        dst_ref=dst,
        send_sem=send,
        recv_sem=recv,
        device_id=target,
        device_id_type=MESH,
    )


def greet(peers):
    barrier = pltpu.get_barrier_semaphore()
    for peer in peers:
        pl.semaphore_signal(barrier, inc=1, device_id=peer, device_id_type=MESH)
    pl.semaphore_wait(barrier, len(peers))


def normalise(values):
    centred = values - jnp.mean(values, axis=-1, keepdims=True)
    inverse = lax.rsqrt(jnp.mean(centred * centred, axis=-1, keepdims=True) + EPSILON)
    return centred * inverse, inverse


def normalise_back(grad_out, normed, inverse, gain):
    scaled = grad_out * gain
    return inverse * (
        scaled
        - jnp.mean(scaled, axis=-1, keepdims=True)
        - normed * jnp.mean(scaled * normed, axis=-1, keepdims=True)
    )


def head_lanes(values, head):
    lanes = lax.broadcasted_iota(jnp.int32, values.shape, 1)
    return jnp.where(lanes // HD == head, values, jnp.zeros_like(values))


def head_kernel(
    nar,
    first,
    wid,
    seqs,
    heads,
    block,
    tile,
    ring,
    input_ref,
    gain_ref,
    qkv_weight_ref,
    col_ref,
    row_ref,
    keys_ref,
    in_ref,
    out_ref,
    pq_ref,
    normed_ref,
    qkv_ref,
    lse_ref,
    norms_ref,
    att_ref,
    in_all,
    out_all,
    pq_all,
    attended,
    slots,
    slot_sem,
    own_sem,
    a_send,
    a_recv,
    z_send,
    z_recv,
    y_send,
    y_recv,
    x_send,
    x_recv,
    c_send,
    c_recv,
):
    second = nar // first
    outer = wid // 2
    za, yb = lax.axis_index("z"), lax.axis_index("y")
    me = za * second + yb
    wide = lax.axis_index("wide")
    chip, core = wide // 2, lax.rem(wide, 2)
    rows, width = input_ref.shape
    tok = rows // nar
    length = rows // seqs
    local = heads * HD
    tiles = rows // tile
    last = (((1,), (1,)), ((), ()))

    def fetch(index, slot):
        return pltpu.make_async_copy(
            keys_ref.at[pl.ds(index * tile, tile)], slots.at[slot], slot_sem.at[slot]
        )

    for i in range(ring):
        fetch(i, i).start()

    greet(
        [place(lax.rem(me + k, nar), second) for k in range(1, nar)]
        + [{"wide": chip * 2 + (1 - core)}]
        + [{"wide": lax.rem(chip + o, outer) * 2 + core} for o in range(1, outer)]
    )

    stacks = ((pq_ref, pq_all), (in_ref, in_all), (out_ref, out_all))

    def shard_of(t, source):
        return source if t == 0 else source // second

    def quarter(t, source, owner):
        own, stack = stacks[t]
        count = own.shape[0] // wid
        at = pl.ds(pl.multiple_of(owner * count, count), count)
        return stack.at[shard_of(t, source), at]

    def own_quarter(t):
        own, _ = stacks[t]
        count = own.shape[0] // wid
        return own.at[pl.ds(pl.multiple_of(wide * count, count), count)]

    reach = ((1, 2), (0, 2), (1, 3), (2, 1))
    relay = {1: (0, (2, 3)), 2: (3, (0, 1))}
    if first != 4:
        reach = tuple(tuple(b for b in range(first) if b != a) for a in range(first))
        relay = {}

    def line_copy(t, source, z, slot, own):
        return push(
            own_quarter(t) if own else quarter(t, source, wide),
            quarter(t, source, wide),
            z_send.at[t, source // second, slot],
            z_recv.at[t, source // second],
            {"z": z, "y": yb},
        )

    def owner_of(o):
        return lax.rem(chip + outer - o, outer) * 2 + core

    def row_copy(source, j, o, own):
        owner = owner_of(o)
        count = pq_ref.shape[0] // wid
        at = pl.ds(pl.multiple_of(owner * count, count), count)
        return push(
            pq_ref.at[at] if own else quarter(0, source, owner),
            quarter(0, source, owner),
            y_send.at[source, j, o],
            y_recv.at[source, j, o],
            {"z": za, "y": lax.rem(yb + j, second)},
        )

    def chip_copy(t, source, o):
        return push(
            quarter(t, source, wide),
            quarter(t, source, wide),
            x_send.at[t, source, o],
            x_recv.at[t, source, o],
            {"wide": lax.rem(chip + o, outer) * 2 + core},
        )

    def chip_arrival(t, source, o):
        owner = owner_of(o)
        return push(
            quarter(t, source, owner),
            quarter(t, source, owner),
            x_send.at[t, source, o],
            x_recv.at[t, source, o],
            {"wide": owner},
        )

    def core_copy(t, source, o, away):
        owner = lax.rem(chip + outer - o, outer) * 2 + jnp.where(away, 1 - core, core)
        return push(
            quarter(t, source, owner),
            quarter(t, source, owner),
            c_send.at[t, source, o],
            c_recv.at[t, source, o],
            {"wide": chip * 2 + (1 - core)},
        )

    def att_copy(target, source):
        return push(
            attended.at[target],
            att_ref.at[source],
            a_send.at[target],
            a_recv.at[source],
            place(target, second),
        )

    own_copies = [
        pltpu.make_async_copy(own, stack.at[shard_of(t, me)], own_sem.at[t])
        for t, (own, stack) in enumerate(stacks)
    ]

    def send_own(t):
        for z in range(first):

            @pl.when(za == z)
            def _(z=z):
                for slot, target in enumerate(reach[z]):
                    line_copy(t, me, target, slot, True).start()

        if t == 0:
            for j in range(1, second):
                for o in range(outer):
                    row_copy(me, j, o, True).start()
        own_copies[t].start()

    def line_arrivals(t, begin, end):
        for d in range(begin, end):
            for way in (-1, 1):
                z = za + way * d

                @pl.when((z >= 0) & (z < first))
                def _(z=z):
                    source = z * second + yb
                    line_copy(t, source, za, 0, False).wait_recv()
                    for middle, (target, sources) in relay.items():

                        @pl.when((za == middle) & ((z == sources[0]) | (z == sources[1])))
                        def _(target=target):
                            line_copy(t, source, target, 0, False).start()

                    for o in range(1, outer):
                        chip_copy(t, source, o).start()
                    core_copy(t, source, 0, False).start()

    def chip_arrivals(t):
        for n in range(first):
            source = n * second + yb

            @pl.when(source != me)
            def _(source=source):
                for o in range(1, outer):
                    chip_arrival(t, source, o).wait_recv()
                    core_copy(t, source, o, False).start()
                if t == 0:
                    for j in range(1, second):
                        for o in range(outer):
                            row_copy(source, j, o, False).start()

    def row_arrivals():
        for j in range(1, second):
            for z in range(first):
                source = z * second + lax.rem(yb + second - j, second)
                for o in range(outer):
                    row_copy(source, j, o, False).wait_recv()
                    core_copy(0, source, o, False).start()

    def each_source(t, do):
        for n in range(nar if t == 0 else first):
            source = n if t == 0 else n * second + yb

            @pl.when(source != me)
            def _(source=source):
                do(source)

    def core_arrivals(t):
        def do(source):
            for o in range(outer):
                core_copy(t, source, o, True).wait_recv()

        each_source(t, do)

    for t in range(3):
        send_own(t)

    def project(r, carry):
        at = pl.ds(pl.multiple_of(r * block, block), block)
        normed, _ = normalise(input_ref[at, :].astype(F32))
        low = (normed * gain_ref[0:1, :]).astype(BF16)
        normed_ref[at, :] = low
        out = lax.dot_general(low, qkv_weight_ref[...], last, preferred_element_type=F32)
        lanes = lax.broadcasted_iota(jnp.int32, out.shape, 1)
        qkv_ref[at, :] = jnp.where(lanes < local, out * HD ** (-0.5), out).astype(BF16)
        return carry

    lax.fori_loop(0, rows // block, project, 0)
    line_arrivals(0, 1, 2)

    def sequence(seq, carry):
        base = seq * length
        for start in range(0, length, block):
            keys = start + block
            at = pl.ds(pl.multiple_of(base + start, block), block)
            whole = pl.ds(pl.multiple_of(base, length), keys)
            query_segment = col_ref[at, 0:1]
            key_segment = row_ref[seq, 0:1, 0:keys]
            spot = lax.broadcasted_iota(jnp.int32, (block, keys), 1)
            own = lax.broadcasted_iota(jnp.int32, (block, keys), 0) + start
            allowed = (spot <= own) & (query_segment == key_segment)
            query = qkv_ref[at, 0:local]
            key = qkv_ref[whole, local : 2 * local]
            value = qkv_ref[whole, 2 * local : 3 * local]
            total = jnp.zeros((block, local), F32)
            for head in range(heads):
                scores = lax.dot_general(
                    head_lanes(query, head), key, last, preferred_element_type=F32
                )
                scores = jnp.where(allowed, scores, -1e30)
                peak = jnp.max(scores, axis=-1, keepdims=True)
                expo = jnp.exp(scores - peak)
                sums = jnp.sum(expo, axis=-1, keepdims=True)
                out = jnp.dot(expo.astype(BF16), value, preferred_element_type=F32) / sums
                total = total + head_lanes(out, head)
                lse_ref[at, head : head + 1] = peak + jnp.log(sums)
            each = min(tok, block)
            for r in range(0, block, each):
                target = seq * (nar // seqs) + (start + r) // tok
                spot_row = (start + r) % tok
                attended[target, spot_row : spot_row + each, :] = total[r : r + each, :].astype(
                    BF16
                )

        def leave(b, c):
            target = seq * (nar // seqs) + b

            @pl.when(target != me)
            def _():
                att_copy(target, me).start()

            return c

        lax.fori_loop(0, nar // seqs, leave, 0)
        return carry

    lax.fori_loop(0, seqs, sequence, 0)
    att_ref[me] = attended[me]

    def norms(begin, end):
        def body(index, carry):
            slot = lax.rem(index, ring)
            fetch(index, slot).wait()
            keys = slots[slot].astype(F32)
            at = pl.ds(pl.multiple_of(index * tile, tile), tile)
            norms_ref[at, :] = jnp.sum(keys * keys, axis=1)

            @pl.when(index + ring < tiles)
            def _():
                fetch(index + ring, slot).start()

            return carry

        lax.fori_loop(begin, end, body, 0)

    def some(*calls):
        def run():
            for call in calls:
                call()

        return run

    steps = [
        some(lambda: line_arrivals(1, 1, 2), lambda: line_arrivals(0, 2, first)),
        some(lambda: chip_arrivals(0), lambda: line_arrivals(2, 1, 2)),
        lambda: line_arrivals(1, 2, first),
        lambda: line_arrivals(2, 2, first),
    ]
    share_of = tiles // len(steps)
    for n, step in enumerate(steps):
        step()
        norms(n * share_of, tiles if n == len(steps) - 1 else (n + 1) * share_of)
    row_arrivals()
    chip_arrivals(1)
    chip_arrivals(2)
    for t in range(3):
        core_arrivals(t)
    for k in range(1, nar):
        source = lax.rem(me + k, nar)
        att_copy(source, source).wait_recv()
        att_copy(source, me).wait_send()
    for t in range(3):
        own_copies[t].wait()

        def sent(source, t=t):
            for o in range(outer):
                core_copy(t, source, o, False).wait_send()

        each_source(t, sent)
        for n in range(first):
            source = n * second + yb

            @pl.when(source != me)
            def _(source=source, t=t):
                for o in range(1, outer):
                    chip_copy(t, source, o).wait_send()

        for z in range(first):

            @pl.when(za == z)
            def _(z=z, t=t):
                for slot, target in enumerate(reach[z]):
                    line_copy(t, me, target, slot, True).wait_send()
                if z in relay:
                    target, sources = relay[z]
                    for n in sources:
                        line_copy(t, n * second + yb, target, 0, False).wait_send()

    for z in range(first):
        for j in range(1, second):
            for o in range(outer):
                row_copy(z * second + yb, j, o, False).wait_send()


def head(block_input, gain, w_qkv, columns, row_form, keys, w_in, w_out, pq, first, nar, wid, name):
    rows, width = block_input.shape
    seqs, _, length = row_form.shape
    second = nar // first
    outer = wid // 2
    local = w_qkv.shape[0] // 3
    heads = local // HD
    hidden = w_in.shape[1]
    tok = rows // nar
    depth = keys.shape[1]
    tile, ring = 32, 4
    block = min(256, length)
    vmem = pl.BlockSpec(memory_space=pltpu.VMEM)
    dma = pltpu.SemaphoreType.DMA
    return pl.pallas_call(
        functools.partial(head_kernel, nar, first, wid, seqs, heads, block, tile, ring),
        out_shape=(
            jax.ShapeDtypeStruct((rows, width), BF16),
            jax.ShapeDtypeStruct((rows, 3 * local), BF16),
            jax.ShapeDtypeStruct((rows, heads), F32),
            jax.ShapeDtypeStruct((rows, J), F32),
            jax.ShapeDtypeStruct((nar, tok, local), BF16),
            jax.ShapeDtypeStruct((first, width, hidden), BF16),
            jax.ShapeDtypeStruct((first, hidden, width), BF16),
            jax.ShapeDtypeStruct((nar,) + pq.shape, BF16),
        ),
        in_specs=[vmem] * 5 + [pl.BlockSpec(memory_space=pl.ANY)] + [vmem] * 3,
        out_specs=(vmem,) * 8,
        scratch_shapes=[
            pltpu.VMEM((nar, tok, local), BF16),
            pltpu.VMEM((ring, tile, depth, J), BF16),
            dma((ring,)),
            dma((3,)),
            dma((nar,)),
            dma((nar,)),
            dma((3, first, 2)),
            dma((3, first)),
            dma((nar, second, outer)),
            dma((nar, second, outer)),
            dma((3, nar, outer)),
            dma((3, nar, outer)),
            dma((3, nar, outer)),
            dma((3, nar, outer)),
        ],
        compiler_params=pltpu.CompilerParams(
            collective_id=name, has_side_effects=True, vmem_limit_bytes=58 * 2**20
        ),
    )(block_input, gain, w_qkv, columns, row_form, keys, w_in, w_out, pq)


INNER = 0.7978845608028654
CUBIC = 0.044715


def gelu_parts(values):
    tanh = jnp.tanh(INNER * (values + CUBIC * values * values * values))
    return 0.5 * values * (1.0 + tanh), tanh


def ffn_kernel(
    chunks,
    att_ref,
    input_ref,
    gains_ref,
    proj_ref,
    in_ref,
    mid_ref,
    one_ref,
    two_ref,
    output_ref,
    key_ref,
    normed_ref,
    pre_ref,
    back_out,
    back_in,
    n_send,
    n_recv,
    b_send,
    b_recv,
):
    nar, tok, local = att_ref.shape
    first, width, hidden = in_ref.shape
    second = nar // first
    part = tok // chunks
    za, yb = lax.axis_index("z"), lax.axis_index("y")

    greet([{"z": za, "y": lax.rem(yb + j, second)} for j in range(1, second)])

    def n_copy(j, c):
        at = pl.ds(c * part, part)
        target = {"z": za, "y": lax.rem(yb + j, second)}
        return push(
            normed_ref.at[0, at], normed_ref.at[j, at], n_send.at[j, c], n_recv.at[j, c], target
        )

    def b_copy(j, c):
        at = pl.ds(c * part, part)
        target = {"z": za, "y": lax.rem(yb + second - j, second)}
        return push(
            back_out.at[j, at], back_in.at[j, at], b_send.at[j, c], b_recv.at[j, c], target
        )

    def through(j, start, count):
        total = jnp.zeros((count, width), F32)
        for z in range(first):
            pre = jnp.dot(
                normed_ref[j, start : start + count, :], in_ref[z], preferred_element_type=F32
            )
            pre_ref[j, start : start + count, z * hidden : (z + 1) * hidden] = pre
            activated = gelu_parts(pre)[0].astype(BF16)
            total = total + jnp.dot(activated, mid_ref[z], preferred_element_type=F32)
        return total

    att = jnp.concatenate([att_ref[n] for n in range(nar)], axis=1)
    one = input_ref[...].astype(F32) + jnp.dot(
        att, proj_ref[...].reshape(nar * local, width), preferred_element_type=F32
    )
    one_ref[...] = one
    normed, _ = normalise(one)
    normed_ref[0] = (normed * gains_ref[1:2, :]).astype(BF16)
    for c in range(chunks):
        for j in range(1, second):
            n_copy(j, c).start()
    two_ref[...] = one_ref[...] + through(0, 0, tok)
    for c in range(chunks):
        for j in range(1, second):
            n_copy(j, c).wait_recv()
            back_out[j, c * part : (c + 1) * part, :] = through(j, c * part, part).astype(BF16)
            b_copy(j, c).start()
    for c in range(chunks):
        at = slice(c * part, (c + 1) * part)
        for j in range(1, second):
            b_copy(j, c).wait_recv()
            two_ref[at, :] += back_in[j, at, :].astype(F32)
    hidden_two = two_ref[...]
    output_ref[...] = hidden_two.astype(BF16)
    normed, _ = normalise(hidden_two)
    query_key = (normed * gains_ref[2:3, :]).astype(BF16)
    for n in range(nar):
        key_ref[n] = query_key[:, n * (width // nar) : (n + 1) * (width // nar)]
    for c in range(chunks):
        for j in range(1, second):
            n_copy(j, c).wait_send()
            b_copy(j, c).wait_send()


def ffn(att, inputs, gains, proj, in_all, out_all, name):
    nar, tok, local = att.shape
    first, width, hidden = in_all.shape
    second = nar // first
    chunks = 2
    vmem = pl.BlockSpec(memory_space=pltpu.VMEM)
    dma = pltpu.SemaphoreType.DMA((second, chunks))
    return pl.pallas_call(
        functools.partial(ffn_kernel, chunks),
        out_shape=(
            jax.ShapeDtypeStruct((tok, width), F32),
            jax.ShapeDtypeStruct((tok, width), F32),
            jax.ShapeDtypeStruct((tok, width), BF16),
            jax.ShapeDtypeStruct((nar, tok, width // nar), BF16),
            jax.ShapeDtypeStruct((second, tok, width), BF16),
            jax.ShapeDtypeStruct((second, tok, first * hidden), F32),
        ),
        in_specs=[vmem] * 6,
        out_specs=(vmem,) * 6,
        scratch_shapes=[pltpu.VMEM((second, tok, width), BF16)] * 2 + [dma] * 4,
        compiler_params=pltpu.CompilerParams(
            collective_id=name, has_side_effects=True, vmem_limit_bytes=48 * 2**20
        ),
    )(att, inputs, gains, proj, in_all, out_all)


def ffn_back_kernel(
    chunks,
    slices_ref,
    att_ref,
    cot_ref,
    one_ref,
    two_ref,
    gains_ref,
    pre_ref,
    normed_ref,
    proj_ref,
    in_ref,
    mid_ref,
    grad_one_ref,
    grad_att_ref,
    gain_ref,
    pre_turned_ref,
    act_turned_ref,
    att_turned_ref,
    normed_cols_ref,
    ffn_cols_ref,
    branch_cols_ref,
    grads,
    grad_two,
    total,
    back_out,
    back_in,
    n_send,
    n_recv,
    b_send,
    b_recv,
):
    nar, tok, local = att_ref.shape
    first, width, hidden = in_ref.shape
    second = nar // first
    wid = branch_cols_ref.shape[0]
    columns = width // wid
    part = tok // chunks
    last = (((1,), (1,)), ((), ()))
    za, yb = lax.axis_index("z"), lax.axis_index("y")

    greet([{"z": za, "y": lax.rem(yb + j, second)} for j in range(1, second)])

    def n_copy(j, c):
        at = pl.ds(c * part, part)
        target = {"z": za, "y": lax.rem(yb + j, second)}
        return push(grads.at[0, at], grads.at[j, at], n_send.at[j, c], n_recv.at[j, c], target)

    def b_copy(j, c):
        at = pl.ds(c * part, part)
        target = {"z": za, "y": lax.rem(yb + second - j, second)}
        return push(
            back_out.at[j, at], back_in.at[j, at], b_send.at[j, c], b_recv.at[j, c], target
        )

    def through(j, start, count):
        at = slice(start, start + count)
        sums = jnp.zeros((count, width), F32)
        for z in range(first):
            own = slice(z * hidden, (z + 1) * hidden)
            pre = pre_ref[j, at, own]
            activated, tanh = gelu_parts(pre)
            slope = 0.5 * (1.0 + tanh) + 0.5 * pre * (1.0 - tanh * tanh) * INNER * (
                1.0 + 3.0 * CUBIC * pre * pre
            )
            grad_act = lax.dot_general(
                grads[j, at, :], mid_ref[z], last, preferred_element_type=F32
            )
            grad_pre = slope * grad_act
            to = slice(j * tok + start, j * tok + start + count)
            act_turned_ref[own, to] = jnp.transpose(activated).astype(BF16)
            pre_turned_ref[own, to] = jnp.transpose(grad_pre).astype(BF16)
            sums = sums + lax.dot_general(
                grad_pre.astype(BF16), in_ref[z], last, preferred_element_type=F32
            )
        return sums

    grad_key = jnp.concatenate([slices_ref[n] for n in range(nar)], axis=1).astype(F32)
    normed, inverse = normalise(two_ref[...])
    gain_ref[1:2, :] = jnp.sum(grad_key * normed, axis=0, keepdims=True)
    grad = cot_ref[...].astype(F32) + normalise_back(
        grad_key, normed, inverse, gains_ref[2:3, :]
    )
    grad_two[...] = grad
    grads[0] = grad.astype(BF16)
    for c in range(chunks):
        for j in range(1, second):
            n_copy(j, c).start()
    total[...] = through(0, 0, tok)
    for c in range(chunks):
        for j in range(1, second):
            n_copy(j, c).wait_recv()
            back_out[j, c * part : (c + 1) * part, :] = through(j, c * part, part).astype(BF16)
            b_copy(j, c).start()
    att_turned_ref[...] = jnp.concatenate(
        [jnp.transpose(att_ref[n].astype(F32)).astype(BF16) for n in range(nar)], axis=0
    )
    for j in range(second):
        for w in range(wid):
            own = slice(w * columns, (w + 1) * columns)
            normed_cols_ref[w, j * tok : (j + 1) * tok, :] = normed_ref[j, :, own]
            ffn_cols_ref[w, j * tok : (j + 1) * tok, :] = grads[j, :, own]
    for c in range(chunks):
        at = slice(c * part, (c + 1) * part)
        for j in range(1, second):
            b_copy(j, c).wait_recv()
            total[at, :] += back_in[j, at, :].astype(F32)
    normed, inverse = normalise(one_ref[...])
    gain_ref[0:1, :] = jnp.sum(total[...] * normed, axis=0, keepdims=True)
    grad = grad_two[...] + normalise_back(total[...], normed, inverse, gains_ref[1:2, :])
    grad_one_ref[...] = grad
    branch = grad.astype(BF16)
    grad_att = lax.dot_general(
        branch, proj_ref[...].reshape(nar * local, width), last, preferred_element_type=F32
    ).astype(BF16)
    for n in range(nar):
        grad_att_ref[n] = grad_att[:, n * local : (n + 1) * local]
    for w in range(wid):
        branch_cols_ref[w] = branch[:, w * columns : (w + 1) * columns]
    for c in range(chunks):
        for j in range(1, second):
            n_copy(j, c).wait_send()
            b_copy(j, c).wait_send()


def ffn_back(slices, att, cot, one, two, gains, pre, normed, proj, in_all, out_all, wid, name):
    nar, tok, local = att.shape
    first, width, hidden = in_all.shape
    second = nar // first
    chunks = 2
    columns = width // wid
    vmem = pl.BlockSpec(memory_space=pltpu.VMEM)
    dma = pltpu.SemaphoreType.DMA((second, chunks))
    return pl.pallas_call(
        functools.partial(ffn_back_kernel, chunks),
        out_shape=(
            jax.ShapeDtypeStruct((tok, width), F32),
            jax.ShapeDtypeStruct((nar, tok, local), BF16),
            jax.ShapeDtypeStruct((2, width), F32),
            jax.ShapeDtypeStruct((first * hidden, second * tok), BF16),
            jax.ShapeDtypeStruct((first * hidden, second * tok), BF16),
            jax.ShapeDtypeStruct((nar * local, tok), BF16),
            jax.ShapeDtypeStruct((wid, second * tok, columns), BF16),
            jax.ShapeDtypeStruct((wid, second * tok, columns), BF16),
            jax.ShapeDtypeStruct((wid, tok, columns), BF16),
        ),
        in_specs=[vmem] * 11,
        out_specs=(vmem,) * 9,
        scratch_shapes=[
            pltpu.VMEM((second, tok, width), BF16),
            pltpu.VMEM((tok, width), F32),
            pltpu.VMEM((tok, width), F32),
            pltpu.VMEM((second, tok, width), BF16),
            pltpu.VMEM((second, tok, width), BF16),
        ]
        + [dma] * 4,
        compiler_params=pltpu.CompilerParams(
            collective_id=name, has_side_effects=True, vmem_limit_bytes=52 * 2**20
        ),
    )(slices, att, cot, one, two, gains, pre, normed, proj, in_all, out_all)


def grad_kernel(
    nar,
    first,
    wid,
    seqs,
    heads,
    block,
    grad_ref,
    qkv_ref,
    lse_ref,
    col_ref,
    row_ref,
    weight_ref,
    input_ref,
    above_ref,
    gain_ref,
    pre_ref,
    act_ref,
    att_ref,
    normed_ref,
    ffn_ref,
    branch_ref,
    out_ref,
    own_ref,
    sum_ref,
    ffn_grad_ref,
    proj_grad_ref,
    grads,
    got,
    grad_key,
    grad_value,
    core_out,
    core_in,
    chip_out,
    chip_in,
    held,
    turn_out,
    turn_in,
    line_out,
    line_in,
    a_send,
    a_recv,
    b_send,
    b_recv,
    c_send,
    c_recv,
    x_send,
    x_recv,
    y_send,
    y_recv,
    z_send,
    z_recv,
):
    second = nar // first
    outer = wid // 2
    za, yb = lax.axis_index("z"), lax.axis_index("y")
    me = za * second + yb
    wide = lax.axis_index("wide")
    chip, core = wide // 2, lax.rem(wide, 2)
    tok, local = grad_ref.shape[1:]
    hidden = pre_ref.shape[0] // first
    columns = normed_ref.shape[2]
    rows = 2 * hidden
    body = first * rows
    length = nar * tok // seqs
    per_seq = nar // seqs
    width = heads * HD
    across = (((0,), (0,)), ((), ()))
    last = (((1,), (1,)), ((), ()))

    greet(
        [place(lax.rem(me + k, nar), second) for k in range(1, nar)]
        + [{"wide": chip * 2 + (1 - core)}]
        + [{"wide": lax.rem(chip + i, outer) * 2 + core} for i in range(1, outer)]
    )

    def a_copy(target, source):
        return push(
            grad_ref.at[target],
            grads.at[source],
            a_send.at[target],
            a_recv.at[source],
            place(target, second),
        )

    def b_copy(target, source):
        return push(
            out_ref.at[pl.ds(pl.multiple_of(target * tok, tok), tok)],
            got.at[source],
            b_send.at[target],
            b_recv.at[source],
            place(target, second),
        )

    def c_copy(o):
        return push(
            core_out.at[o],
            core_in.at[o],
            c_send.at[o],
            c_recv.at[o],
            {"wide": chip * 2 + (1 - core)},
        )

    def span(z):
        return pl.ds(pl.multiple_of(z * rows, rows), rows)

    tail_rows = pl.ds(body, nar * local)

    def x_copy(i, q, at):
        return push(
            chip_out.at[i, at],
            chip_in.at[i, at],
            x_send.at[i, q],
            x_recv.at[i, q],
            {"wide": lax.rem(chip + i, outer) * 2 + core},
        )

    def y_copy(j):
        target = {"z": za, "y": lax.rem(yb + j, second)}
        return push(turn_out.at[j], turn_in.at[j], y_send.at[j], y_recv.at[j], target)

    def z_copy(i):
        target = {"z": lax.rem(za + i, first), "y": yb}
        return push(line_out.at[i], line_in.at[i], z_send.at[i], z_recv.at[i], target)

    def product_rows(w, z):
        own = pl.ds(pl.multiple_of(z * hidden, hidden), hidden)
        return (
            jnp.dot(pre_ref[own, :], normed_ref[w], preferred_element_type=F32),
            jnp.dot(act_ref[own, :], ffn_ref[w], preferred_element_type=F32),
        )

    def product_tail(w):
        return jnp.dot(att_ref[...], branch_ref[w], preferred_element_type=F32)

    for k in range(1, nar):
        a_copy(lax.rem(me + k, nar), me).start()
    grads[me] = grad_ref[me]

    def for_core(o, carry):
        w = o * 2 + (1 - core)

        def line(z, c):
            upper, lower = product_rows(w, z)
            at = pl.multiple_of(z * rows, rows)
            core_out[o, pl.ds(at, hidden), :] = upper.astype(BF16)
            core_out[o, pl.ds(at + hidden, hidden), :] = lower.astype(BF16)
            return c

        lax.fori_loop(0, first, line, 0)
        core_out[o, tail_rows, :] = product_tail(w).astype(BF16)
        c_copy(o).start()
        return carry

    for i in range(1, outer + 1):
        for_core(lax.rem(chip + i, outer), 0)

    for i in range(1, outer):
        o = lax.rem(chip + i, outer)
        w = o * 2 + core
        c_copy(o).wait_recv()
        total = product_tail(w) + core_in[o, tail_rows, :].astype(F32)
        chip_out[i, tail_rows, :] = total.astype(BF16)
        x_copy(i, 0, tail_rows).start()

        def line(n, c, o=o, w=w, i=i):
            z = lax.rem(za + n, first)
            upper, lower = product_rows(w, z)
            at = pl.multiple_of(z * rows, rows)
            high, low = pl.ds(at, hidden), pl.ds(at + hidden, hidden)
            chip_out[i, high, :] = (upper + core_in[o, high, :].astype(F32)).astype(BF16)
            chip_out[i, low, :] = (lower + core_in[o, low, :].astype(F32)).astype(BF16)
            x_copy(i, n, span(z)).start()
            return c

        lax.fori_loop(1, first + 1, line, 0)

    def sequence(seq, carry):
        base = seq * length

        def arrive(b, c):
            source = seq * per_seq + b

            @pl.when(source != me)
            def _():
                a_copy(source, source).wait_recv()

            return c

        lax.fori_loop(0, per_seq, arrive, 0)
        grad_key[...] = jnp.zeros_like(grad_key)
        grad_value[...] = jnp.zeros_like(grad_value)
        for start in range(0, length, block):
            keys = start + block
            at = pl.multiple_of(base + start, block)
            query_segment = col_ref[pl.ds(at, block), 0:1]
            key_segment = row_ref[seq, 0:1, 0:keys]
            spot = lax.broadcasted_iota(jnp.int32, (block, keys), 1)
            own = lax.broadcasted_iota(jnp.int32, (block, keys), 0) + start
            allowed = (spot <= own) & (query_segment == key_segment)
            whole = pl.ds(pl.multiple_of(base, length), keys)
            query = qkv_ref[pl.ds(at, block), 0:width]
            key = qkv_ref[whole, width : 2 * width]
            value = qkv_ref[whole, 2 * width : 3 * width]
            each = min(tok, block)
            grad = jnp.concatenate(
                [
                    grads[
                        seq * per_seq + (start + r) // tok,
                        (start + r) % tok : (start + r) % tok + each,
                        :,
                    ]
                    for r in range(0, block, each)
                ],
                axis=0,
            )
            total = jnp.zeros((block, width), F32)
            for head in range(heads):
                own_query = head_lanes(query, head)
                own_grad = head_lanes(grad, head)
                scores = lax.dot_general(own_query, key, last, preferred_element_type=F32)
                probs = jnp.where(
                    allowed, jnp.exp(scores - lse_ref[pl.ds(at, block), head : head + 1]), 0.0
                )
                grad_probs = lax.dot_general(own_grad, value, last, preferred_element_type=F32)
                delta = jnp.sum(probs * grad_probs, axis=-1, keepdims=True)
                grad_scores = (probs * (grad_probs - delta)).astype(BF16)
                total = total + head_lanes(
                    jnp.dot(grad_scores, key, preferred_element_type=F32), head
                )
                grad_key[0:keys, :] += lax.dot_general(
                    grad_scores, own_query, across, preferred_element_type=F32
                )
                grad_value[0:keys, :] += lax.dot_general(
                    probs.astype(BF16), own_grad, across, preferred_element_type=F32
                )
            out_ref[pl.ds(at, block), 0:width] = (total * HD ** (-0.5)).astype(BF16)
        every = pl.ds(pl.multiple_of(base, length), length)
        out_ref[every, width : 2 * width] = grad_key[...].astype(BF16)
        out_ref[every, 2 * width : 3 * width] = grad_value[...].astype(BF16)

        def leave(b, c):
            target = seq * per_seq + b

            @pl.when(target != me)
            def _():
                b_copy(target, me).start()

            return c

        lax.fori_loop(0, per_seq, leave, 0)
        return carry

    lax.fori_loop(0, seqs, sequence, 0)

    w = chip * 2 + core
    c_copy(chip).wait_recv()
    held[tail_rows, :] = product_tail(w) + core_in[chip, tail_rows, :].astype(F32)

    def line_own(z, c):
        upper, lower = product_rows(w, z)
        at = pl.multiple_of(z * rows, rows)
        high, low = pl.ds(at, hidden), pl.ds(at + hidden, hidden)
        held[high, :] = upper + core_in[chip, high, :].astype(F32)
        held[low, :] = lower + core_in[chip, low, :].astype(F32)
        return c

    lax.fori_loop(0, first, line_own, 0)

    for i in range(1, outer):
        x_copy(i, 0, tail_rows).wait_recv()
        held[tail_rows, :] += chip_in[i, tail_rows, :].astype(F32)
    for j in range(1, second):
        column = lax.rem(yb + j, second)
        for z in range(first):
            at = pl.ds(pl.multiple_of(body + (z * second + column) * local, local), local)
            turn_out[j, z] = held[at, :].astype(BF16)
        y_copy(j).start()

    normed, inverse = normalise(input_ref[...].astype(F32))
    mine = out_ref[pl.ds(pl.multiple_of(me * tok, tok), tok), :]
    total = jnp.dot(mine, weight_ref[me], preferred_element_type=F32)
    for k in range(1, nar):
        source = lax.rem(me + k, nar)
        b_copy(source, source).wait_recv()
        total = total + jnp.dot(got[source], weight_ref[source], preferred_element_type=F32)
    grad = above_ref[...] + normalise_back(total, normed, inverse, gain_ref[0:1, :])
    own_ref[...] = grad.astype(BF16)
    sum_ref[...] = jnp.sum(total * normed, axis=0, keepdims=True)

    for j in range(1, second):
        y_copy(j).wait_recv()
    for n in range(1, first + 1):
        z = lax.rem(za + n, first)
        at = pl.ds(pl.multiple_of(body + (z * second + yb) * local, local), local)
        part = held[at, :]
        for j in range(1, second):
            part = part + turn_in[j, z].astype(F32)
        whole = held[span(z), :]
        for i in range(1, outer):
            x_copy(i, n, span(z)).wait_recv()
            whole = whole + chip_in[i, span(z), :].astype(F32)
        if n < first:
            line_out[n, 0:rows, :] = whole.astype(BF16)
            line_out[n, rows:, :] = part.astype(BF16)
            z_copy(n).start()
        else:
            ffn_grad_ref[...] = whole
            proj_grad_ref[...] = part
    for n in range(1, first):
        z_copy(n).wait_recv()
        ffn_grad_ref[...] += line_in[n, 0:rows, :].astype(F32)
        proj_grad_ref[...] += line_in[n, rows:, :].astype(F32)

    for k in range(1, nar):
        a_copy(lax.rem(me + k, nar), me).wait_send()
        b_copy(lax.rem(me + k, nar), me).wait_send()
    for o in range(outer):
        c_copy(o).wait_send()
    for i in range(1, outer):
        x_copy(i, 0, tail_rows).wait_send()
        for n in range(1, first + 1):
            x_copy(i, n, span(lax.rem(za + n, first))).wait_send()
    for j in range(1, second):
        y_copy(j).wait_send()
    for n in range(1, first):
        z_copy(n).wait_send()


def attention_grads(
    grads, qkv, lse, columns, row_form, weights, inputs, above, gain, first, wid, sides, name
):
    nar, tok, local = grads.shape
    rows, wide = qkv.shape
    width = inputs.shape[1]
    seqs, _, length = row_form.shape
    second = nar // first
    outer = wid // 2
    hidden = sides[0].shape[0] // first
    piece = width // wid
    body = first * 2 * hidden + nar * local
    line = 2 * hidden + local
    vmem = pl.BlockSpec(memory_space=pltpu.VMEM)
    dma = pltpu.SemaphoreType.DMA
    return pl.pallas_call(
        functools.partial(grad_kernel, nar, first, wid, seqs, local // HD, min(256, length)),
        out_shape=(
            jax.ShapeDtypeStruct((rows, wide), BF16),
            jax.ShapeDtypeStruct((tok, width), BF16),
            jax.ShapeDtypeStruct((1, width), F32),
            jax.ShapeDtypeStruct((2 * hidden, piece), F32),
            jax.ShapeDtypeStruct((local, piece), F32),
        ),
        in_specs=[vmem] * 15,
        out_specs=(vmem,) * 5,
        scratch_shapes=[
            pltpu.VMEM((nar, tok, local), BF16),
            pltpu.VMEM((nar, tok, wide), BF16),
            pltpu.VMEM((length, local), F32),
            pltpu.VMEM((length, local), F32),
            pltpu.VMEM((outer, body, piece), BF16),
            pltpu.VMEM((outer, body, piece), BF16),
            pltpu.VMEM((outer, body, piece), BF16),
            pltpu.VMEM((outer, body, piece), BF16),
            pltpu.VMEM((body, piece), F32),
            pltpu.VMEM((second, first, local, piece), BF16),
            pltpu.VMEM((second, first, local, piece), BF16),
            pltpu.VMEM((first, line, piece), BF16),
            pltpu.VMEM((first, line, piece), BF16),
            dma((nar,)),
            dma((nar,)),
            dma((nar,)),
            dma((nar,)),
            dma((outer,)),
            dma((outer,)),
            dma((outer, first + 1)),
            dma((outer, first + 1)),
            dma((second,)),
            dma((second,)),
            dma((first,)),
            dma((first,)),
        ],
        compiler_params=pltpu.CompilerParams(
            collective_id=name, has_side_effects=True, vmem_limit_bytes=60 * 2**20
        ),
    )(grads, qkv, lse, columns, row_form, weights, inputs, above, gain, *sides)


def tail_kernel(
    nar,
    wid,
    first,
    chunks,
    own_ref,
    sums_ref,
    out_ref,
    total_ref,
    all_sums,
    pieces_out,
    pieces_in,
    z_send,
    z_recv,
    y_send,
    y_recv,
    s_send,
    s_recv,
    p_send,
    p_recv,
):
    second = nar // first
    za, yb = lax.axis_index("z"), lax.axis_index("y")
    me = za * second + yb
    mine = lax.axis_index("wide")
    tok = own_ref.shape[0]
    piece = total_ref.shape[1]
    part = tok // chunks

    greet(
        [place(lax.rem(me + k, nar), second) for k in range(1, nar)]
        + [{"wide": lax.rem(mine + w, wid)} for w in range(1, wid)]
    )

    def z_copy(i, c):
        rows = pl.ds(c * part, part)
        target = lax.rem(za + i, first) * second + yb
        return push(
            own_ref.at[rows],
            out_ref.at[me, rows],
            z_send.at[i, c],
            z_recv.at[i, c],
            place(target, second),
        )

    def y_copy(i, j, c):
        source = lax.rem(za + first - i, first) * second + yb
        rows = pl.ds(c * part, part)
        target = za * second + lax.rem(yb + j, second)
        return push(
            own_ref.at[rows] if i == 0 else out_ref.at[source, rows],
            out_ref.at[source, rows],
            y_send.at[i, j, c],
            y_recv.at[i, j, c],
            place(target, second),
        )

    def s_copy(k):
        return push(
            sums_ref,
            all_sums.at[k],
            s_send.at[k],
            s_recv.at[k],
            place(lax.rem(me + k, nar), second),
        )

    def p_copy(w):
        target = lax.rem(mine + w, wid)
        return push(
            pieces_out.at[target], pieces_in.at[w], p_send.at[w], p_recv.at[w], {"wide": target}
        )

    for k in range(1, nar):
        s_copy(k).start()
    for c in range(chunks):
        for i in range(1, first):
            z_copy(i, c).start()
        for j in range(1, second):
            y_copy(0, j, c).start()
    out_ref[me] = own_ref[...]
    sums = sums_ref[...]
    for k in range(1, nar):
        s_copy(k).wait_recv()
        sums = sums + all_sums[k]
    for w in range(wid):
        pieces_out[w] = sums[:, w * piece : (w + 1) * piece]
    for w in range(1, wid):
        p_copy(w).start()
    for c in range(chunks):
        for i in range(1, first):
            z_copy(i, c).wait_recv()
            for j in range(1, second):
                y_copy(i, j, c).start()
    answer = pieces_out[mine]
    for w in range(1, wid):
        p_copy(w).wait()
        answer = answer + pieces_in[w]
    total_ref[...] = answer
    for k in range(1, nar):
        s_copy(k).wait_send()
    for c in range(chunks):
        for i in range(1, first):
            z_copy(i, c).wait_send()
        for i in range(first):
            for j in range(1, second):
                y_copy(i, j, c).wait()


def tail(own, sums, nar, first, wid, name):
    tok, width = own.shape
    second = nar // first
    chunks = 4
    vmem = pl.BlockSpec(memory_space=pltpu.VMEM)
    dma = pltpu.SemaphoreType.DMA
    return pl.pallas_call(
        functools.partial(tail_kernel, nar, wid, first, chunks),
        out_shape=(
            jax.ShapeDtypeStruct((nar, tok, width), BF16),
            jax.ShapeDtypeStruct((8, width // wid), F32),
        ),
        in_specs=[vmem] * 2,
        out_specs=(vmem, vmem),
        scratch_shapes=[
            pltpu.VMEM((nar, 8, width), F32),
            pltpu.VMEM((wid, 8, width // wid), F32),
            pltpu.VMEM((wid, 8, width // wid), F32),
            dma((first, chunks)),
            dma((first, chunks)),
            dma((first, second, chunks)),
            dma((first, second, chunks)),
            dma((nar,)),
            dma((nar,)),
            dma((wid,)),
            dma((wid,)),
        ],
        compiler_params=pltpu.CompilerParams(
            collective_id=name, has_side_effects=True, vmem_limit_bytes=48 * 2**20
        ),
    )(own, sums)


def neighbour_kernel(
    nar,
    first,
    tiles,
    tile,
    kept,
    ring,
    query_ref,
    keys_ref,
    norms_ref,
    ids_ref,
    cols_ref,
    scal_ref,
    grad_ref,
    loss_ref,
    stat_ref,
    queries,
    partial,
    dist,
    grads,
    sends,
    slots,
    loss_own,
    slot_sem,
    q_send,
    q_recv,
    d_send,
    d_recv,
    g_send,
    g_recv,
    l_send,
    l_recv,
    o_send,
    o_recv,
):
    second = nar // first
    me = lax.axis_index("z") * second + lax.axis_index("y")
    tok = query_ref.shape[1]
    depth = query_ref.shape[2]
    group = 16
    per_block = tok // tile
    late = tiles - kept

    def peer(k):
        return lax.rem(me + k, nar)

    def origin(k):
        return lax.rem(me + nar - k, nar)

    def load(index, slot):
        block, sub = index // per_block, lax.rem(index, per_block)
        row = origin(block) * tok + sub * tile
        return pltpu.make_async_copy(
            keys_ref.at[pl.ds(row, tile)], slots.at[slot], slot_sem.at[slot]
        )

    for i in range(kept + ring):
        load(i, i).start()

    greet([place(peer(k), second) for k in range(1, nar)])

    def q_copy(k):
        return push(
            query_ref.at[peer(k)],
            queries.at[k],
            q_send.at[k],
            q_recv.at[k],
            place(peer(k), second),
        )

    def d_copy(k):
        return push(
            partial.at[k], dist.at[k], d_send.at[k], d_recv.at[k], place(origin(k), second)
        )

    def g_copy(k):
        return push(
            grads.at[0], grads.at[k], g_send.at[k], g_recv.at[k], place(peer(k), second)
        )

    def l_copy(k):
        return push(
            loss_own, loss_ref.at[me], l_send.at[k], l_recv.at[k], place(peer(k), second)
        )

    def o_copy(k):
        return push(
            sends.at[k], grad_ref.at[me], o_send.at[k], o_recv.at[k], place(origin(k), second)
        )

    for k in range(1, nar):
        q_copy(k).start()
    queries[0] = query_ref[me]

    row_of = lax.broadcasted_iota(jnp.int32, (group, J), 0)

    def slot_of(index):
        return jnp.where(index < kept, index, kept + lax.rem(index - kept, ring))

    def slot_late(n):
        return kept + lax.rem(n, ring)

    def forward_tile(k, sub, slot):
        def one(g, carry):
            at = pl.multiple_of(sub * tile + g * group, group)
            own = queries[k, pl.ds(at, group), :].astype(F32)
            keys = slots[slot, pl.ds(g * group, group), :, :].reshape(group * depth, J)
            wide = jnp.concatenate(
                [jnp.where(row_of[:, :depth] == t, own, 0.0) for t in range(group)], axis=1
            ).astype(BF16)
            out = jnp.dot(wide, keys, preferred_element_type=F32)
            row = pl.multiple_of(origin(k) * tok + at, group)
            partial[k, pl.ds(at, group), :] = 2.0 * out - norms_ref[pl.ds(row, group), :]
            return carry

        lax.fori_loop(0, tile // group, one, 0, unroll=True)

    def forward_block(k):
        def body(sub, carry):
            index = k * per_block + sub
            slot = slot_of(index)
            load(index, slot).wait()
            forward_tile(k, sub, slot)

            @pl.when(index >= kept)
            def _():
                nxt = index - kept + ring

                @pl.when(nxt < 2 * late)
                def _():
                    load(kept + lax.rem(nxt, late), slot).start()

            return carry

        lax.fori_loop(0, per_block, body, 0)

    forward_block(0)

    def forward_rest(k, carry):
        q_copy(k).wait_recv()
        forward_block(k)
        d_copy(k).start()
        return carry

    lax.fori_loop(1, nar, forward_rest, 0)

    def collect(k, total):
        d_copy(k).wait_recv()
        return total + dist[k]

    distance = lax.fori_loop(1, nar, collect, partial[0])
    temper_value = scal_ref[0]
    mix_value = scal_ref[1]
    count = cols_ref[:, 0:1]
    target = cols_ref[:, 1:2]
    base = cols_ref[:, 2:3]
    loss_weight = cols_ref[:, 3:4]
    logits = distance / temper_value
    spot = lax.broadcasted_iota(jnp.int32, (tok, J), 1).astype(F32)
    masked = jnp.where(spot < count, logits, -1e30)
    peak = jnp.max(masked, axis=-1, keepdims=True)
    expo = jnp.exp(masked - peak)
    weights = expo / jnp.sum(expo, axis=-1, keepdims=True)
    matches = jnp.where(ids_ref[...].astype(F32) == target, 1.0, 0.0)
    knn_prob = jnp.sum(weights * matches, axis=-1, keepdims=True)
    mixture = mix_value * knn_prob + (1.0 - mix_value) * base
    grad_mixture = -loss_weight / mixture
    grad_logits = weights * (mix_value * grad_mixture) * (matches - knn_prob)
    grads[0] = (2.0 * grad_logits / temper_value).astype(BF16)
    for k in range(1, nar):
        g_copy(k).start()
    loss = jnp.transpose(jnp.broadcast_to(-jnp.log(mixture), (tok, J)))[0:8, :]
    loss_own[...] = loss
    for k in range(1, nar):
        l_copy(k).start()
    loss_ref[me] = loss
    term_temper = -jnp.sum(grad_logits * logits, axis=0, keepdims=True) / temper_value
    term_mix = jnp.sum((knn_prob - base) * grad_mixture, axis=0, keepdims=True)
    stat_ref[0:1, :] = term_temper
    stat_ref[1:2, :] = jnp.broadcast_to(term_mix, (1, J))

    def backward_tile(k, sub, slot):
        def one(g, carry):
            at = pl.multiple_of(sub * tile + g * group, group)
            own = grads[k, pl.ds(at, group), :]
            keys = slots[slot, pl.ds(g * group, group), :, :].reshape(group * depth, J)
            out = lax.dot_general(
                own, keys, (((1,), (1,)), ((), ())), preferred_element_type=F32
            )
            total = jnp.zeros((group, depth), F32)
            for t in range(group):
                total = jnp.where(
                    row_of[:, :depth] == t, out[:, t * depth : (t + 1) * depth], total
                )
            sends[k, pl.ds(at, group), :] = total.astype(BF16)
            return carry

        lax.fori_loop(0, tile // group, one, 0, unroll=True)

    def backward_block(k):
        def body(sub, carry):
            index = k * per_block + sub

            @pl.when(index < kept)
            def _():
                backward_tile(k, sub, index)

            @pl.when(index >= kept)
            def _():
                n = index - kept + late
                slot = slot_late(n)
                load(index, slot).wait()
                backward_tile(k, sub, slot)

                @pl.when(n + ring < 2 * late)
                def _():
                    load(kept + lax.rem(n + ring, late), slot).start()

            return carry

        lax.fori_loop(0, per_block, body, 0)

    backward_block(0)
    grad_ref[me] = sends[0]

    def backward_rest(k, carry):
        g_copy(k).wait_recv()
        backward_block(k)
        o_copy(k).start()
        return carry

    lax.fori_loop(1, nar, backward_rest, 0)

    for k in range(1, nar):
        q_copy(k).wait_send()
        d_copy(k).wait_send()
        g_copy(k).wait_send()
        l_copy(k).wait()
        o_copy(k).wait()


def neighbours(nar, first, query, keys, norms, ids, cols, scal):
    tok, depth = query.shape[1:]
    rows = keys.shape[0]
    tile = 32
    tiles = rows // tile
    bytes_tile = tile * depth * J * 2
    ring = 4
    kept = min(tiles - 2 * ring, (KEPT_BYTES // bytes_tile))
    vmem = pl.BlockSpec(memory_space=pltpu.VMEM)
    dma = pltpu.SemaphoreType.DMA((nar,))
    return pl.pallas_call(
        functools.partial(neighbour_kernel, nar, first, tiles, tile, kept, ring),
        out_shape=(
            jax.ShapeDtypeStruct((nar, tok, depth), BF16),
            jax.ShapeDtypeStruct((nar, 8, tok), F32),
            jax.ShapeDtypeStruct((2, J), F32),
        ),
        in_specs=[
            vmem,
            pl.BlockSpec(memory_space=pl.ANY),
            vmem,
            vmem,
            vmem,
            pl.BlockSpec(memory_space=pltpu.SMEM),
        ],
        out_specs=(vmem, vmem, vmem),
        scratch_shapes=[
            pltpu.VMEM((nar, tok, depth), BF16),
            pltpu.VMEM((nar, tok, J), F32),
            pltpu.VMEM((nar, tok, J), F32),
            pltpu.VMEM((nar, tok, J), BF16),
            pltpu.VMEM((nar, tok, depth), BF16),
            pltpu.VMEM((kept + ring, tile, depth, J), BF16),
            pltpu.VMEM((8, tok), F32),
            pltpu.SemaphoreType.DMA((kept + ring,)),
        ]
        + [dma] * 10,
        compiler_params=pltpu.CompilerParams(
            collective_id=1, has_side_effects=True, vmem_limit_bytes=60 * 2**20
        ),
    )(query, keys, norms, ids, cols, scal)


def on_device(
    block_input,
    output_cotangent,
    loss_weight,
    segments,
    nbr_keys,
    nbr_count,
    nbr_ids,
    targets,
    base_prob,
    w_query,
    w_key,
    w_value,
    w_proj,
    w_in,
    w_out,
    gain_attn,
    gain_ffn,
    gain_key,
    temper,
    mix_weight,
):
    seqs_here, length, width = block_input.shape
    rows = seqs_here * length
    wid = lax.axis_size("wide")
    first = lax.axis_size("z")
    nar = first * lax.axis_size("y")
    own = lax.axis_index("z") * lax.axis_size("y") + lax.axis_index("y")
    tok = rows // nar
    local_width = w_query.shape[0]

    def mine(values):
        flat = values.reshape((rows,) + values.shape[2:])
        return lax.dynamic_slice_in_dim(flat, own * tok, tok, 0)

    hidden = w_in.shape[1]
    seg_column = segments.reshape(rows, 1)
    seg_row = segments.reshape(seqs_here, 1, length)
    key_slices = nbr_keys.reshape(rows, nbr_keys.shape[2], nbr_keys.shape[3])
    gains = jnp.stack([gain_attn, gain_ffn, gain_key])
    w_qkv = jnp.concatenate([w_query, w_key, w_value], axis=0)
    normed_one, qkv, lse, part_norms, attended_own, in_all, out_all, pq_all = head(
        block_input.reshape(rows, width),
        gains,
        w_qkv,
        seg_column,
        seg_row,
        key_slices,
        w_in,
        w_out,
        jnp.concatenate([w_proj, w_qkv], axis=0),
        first,
        nar,
        wid,
        2,
    )
    proj_all = pq_all[:, :local_width]
    qkv_all = pq_all[:, local_width:]
    inputs_own = mine(block_input)
    hidden_one, hidden_two, output_own, query_key, normed_two, pre_act = ffn(
        attended_own, inputs_own, gains, proj_all, in_all, out_all, 3
    )
    block_output = lax.all_gather(output_own, ("z", "y"), axis=0, tiled=True)
    cols = jnp.stack(
        [
            mine(nbr_count).astype(F32),
            mine(targets).astype(F32),
            mine(base_prob),
            mine(loss_weight),
        ],
        axis=1,
    )
    grad_slices, losses, stats = neighbours(
        nar,
        first,
        query_key,
        key_slices,
        part_norms,
        mine(nbr_ids),
        cols,
        jnp.concatenate([temper, mix_weight]),
    )
    token_loss = losses[:, 0, :]
    grad_hidden_one, grad_attended, gain_sums, *sides = ffn_back(
        grad_slices,
        attended_own,
        mine(output_cotangent),
        hidden_one,
        hidden_two,
        gains,
        pre_act,
        normed_two,
        proj_all,
        in_all,
        out_all,
        wid,
        5,
    )
    grad_attended, block_output = lax.optimization_barrier((grad_attended, block_output))
    grad_qkv, grad_own, attn_sums, grad_ffn_pair, grad_w_proj = attention_grads(
        grad_attended,
        qkv,
        lse,
        seg_column,
        seg_row,
        qkv_all,
        inputs_own,
        grad_hidden_one,
        gains,
        first,
        wid,
        sides,
        6,
    )
    grad_w_qkv = outer_sum(grad_qkv, normed_one).astype(BF16)
    grad_w_qkv, grad_own = lax.optimization_barrier((grad_w_qkv, grad_own))
    grad_w_qkv = lax.psum_scatter(grad_w_qkv, "wide", scatter_dimension=1, tiled=True).astype(F32)
    sums = jnp.concatenate(
        [
            attn_sums,
            gain_sums,
            jnp.broadcast_to(jnp.sum(stats[0]), (1, width)),
            jnp.broadcast_to(stats[1, 0], (1, width)),
            jnp.zeros((3, width), F32),
        ],
        axis=0,
    )
    grad_input, totals = tail(grad_own, sums, nar, first, wid, 4)

    return (
        block_output.reshape(seqs_here, length, width),
        token_loss.reshape(seqs_here, length),
        grad_input.astype(F32).reshape(seqs_here, length, width),
        grad_w_qkv[:local_width],
        grad_w_qkv[local_width : 2 * local_width],
        grad_w_qkv[2 * local_width :],
        grad_w_proj,
        grad_ffn_pair[:hidden].T,
        grad_ffn_pair[hidden:],
        totals[0],
        totals[1],
        totals[2],
        totals[3, 0:1],
        totals[4, 0:1],
    )


def solution(mesh):
    wide, narrow = mesh.devices.shape
    first = 4 if narrow % 4 == 0 else narrow
    split = jax.sharding.Mesh(
        mesh.devices.reshape(wide, first, narrow // first), ("wide", "z", "y")
    )
    narrow = ("z", "y")
    return jax.shard_map(
        on_device,
        mesh=split,
        in_specs=(
            P("wide", None, None),
            P("wide", None, None),
            P("wide", None),
            P("wide", None),
            P("wide", None, narrow, None),
            P("wide", None),
            P("wide", None, None),
            P("wide", None),
            P("wide", None),
            P(narrow, None),
            P(narrow, None),
            P(narrow, None),
            P(narrow, None),
            P(None, narrow),
            P(narrow, None),
            P(),
            P(),
            P(),
            P(),
            P(),
        ),
        out_specs=(
            P("wide", None, None),
            P("wide", None),
            P("wide", None, None),
            P(narrow, "wide"),
            P(narrow, "wide"),
            P(narrow, "wide"),
            P(narrow, "wide"),
            P("wide", narrow),
            P(narrow, "wide"),
            P("wide"),
            P("wide"),
            P("wide"),
            P(),
            P(),
        ),
        check_vma=False,
    )
```

time: 769 us -> 539 us (0.70)
  waiting for transfers between devices: 284 us -> 0.04 us
  Pallas kernels: 352 us -> 466 us
  other arithmetic: 42.9 us -> 9.45 us
  matrix products: 26.8 us -> 5.44 us
    all_gather x5 -> x1, waiting for transfers between devices: 214 us -> 0.01 us  [on_device(): block_output = lax.all_gather(output_own, ('z', 'y'), axis=0, tiled=True)]
    pallas_call x7 -> x5, Pallas kernels: 203 us -> 387 us  [the longest x1 111 us: neighbours(): pl.pallas_call(functools.partial(neighbour_kernel, nar, first, tiles, til...]
    pallas_call x1, Pallas kernels: 149 us -> 78.6 us  [tail(): pl.pallas_call(functools.partial(tail_kernel, nar, wid, first, chunks), o...]
    reduce_scatter x3 -> x1, waiting for transfers between devices: 69.3 us -> 0.01 us  [on_device(): lax.psum_scatter(grad_w_qkv, 'wide', scatter_dimension=1, tiled=True)]
    dot_general x1 -> x0, other arithmetic: 22.6 us -> none  [on_device(): jnp.einsum('tdj,tdj->tj', key_slices, key_slices, preferred_element_type=...]
    dot_general x3 -> x1, matrix products: 17.5 us -> 5.44 us  [outer_sum(): return jnp.einsum('ta,tb->ab', left, right, preferred_element_type=F32)]
    unnamed x84 -> x65, local copies, waits for them, and re-layouts: 25.7 us -> 14.7 us
    dot_general x2 -> x0, matrix products: 9.27 us -> none  [the longest x1 6.84 us: product(): return jnp.dot(left, right, preferred_element_type=F32)]
  transfers between devices with their start and end apart: 8 -> 2, of which waited for: 6 -> 0; matrix products, arithmetic and copies ran while one was open for 11% -> 4% of each run, Pallas kernels for 44% -> 42%
where the time goes in v2:
time: 539 us; the launch traced here: 533 us
  Pallas kernels  466 us (86%)
  local copies, waits for them, and re-layouts  36.1 us (7%)
  between operations  16.2 us (3%)
  other arithmetic  9.45 us (2%)
  matrix products  5.44 us (1%)
    pallas_call x1, Pallas kernels, neighbours(): pl.pallas_call(functools.partial(neighbour_kernel, nar, first, tiles, til...  111 us
    pallas_call x1, Pallas kernels, head(): pl.pallas_call(functools.partial(head_kernel, nar, first, wid, seqs, head...  106 us
    pallas_call x1, Pallas kernels, attention_grads(): pl.pallas_call(functools.partial(grad_kernel, nar, first, wid, seqs, loca...  101 us
    pallas_call x1, Pallas kernels, tail(): pl.pallas_call(functools.partial(tail_kernel, nar, wid, first, chunks), o...  78.6 us
    pallas_call x1, Pallas kernels, ffn_back(): pl.pallas_call(functools.partial(ffn_back_kernel, chunks), out_shape=(jax...  36.5 us
    pallas_call x1, Pallas kernels, ffn(): pl.pallas_call(functools.partial(ffn_kernel, chunks), out_shape=(jax.Shap...  33.4 us
    unnamed x65, local copies, waits for them, and re-layouts  14.7 us
  transfers between devices with their start and end apart: 2, of which 0 were waited for; matrix products, arithmetic and copies ran while one was open for 4% of the time, Pallas kernels for 42%

profile of v2, /device:TPU:0, one launch (start us, length us, event | category | flops | bytes accessed | tf_op | source)
XLA Modules:
  0.0 533.0 jit_solution(1176344118668507901)
XLA Ops:
  7.3 1.4 reshape.70.row_ref
  9.4 1.4 copy.47
  10.8 2.1 pad_maximum_fusion.1.qkv_weight_ref
  12.9 1.0 pad_maximum_fusion.pq_ref
  14.6 105.9 %shard_map.299 = (bf16[2048,1024]{1,0:T(8,128)(2,1)}, bf16[2048,384]{1,0:T(8,128)(2,1)}, f32[2048,2]{1,0:T(8,128)}, f32[2048,128]{1,0:T(8,128)}, bf16[8,256,128]...) custom-call(bf16[2048,1024]{1,0:T(8,128)(2,1)} %bitcast.50, ...), custom_call_target="tpu_custom_call" | custom-call | tf_op jit(solution)/shard_map/pallas_call | solution.py:446
  120.5 3.1 slice.45.proj_ref
  123.6 2.1 constant_dynamic-slice_fusion
  125.8 33.4 %shard_map.300 = (f32[256,1024]{1,0:T(8,128)S(1)}, f32[256,1024]{1,0:T(8,128)S(1)}, bf16[256,1024]{1,0:T(8,128)(2,1)}, bf16[8,256,128]{2,1,0:T(8,128)(2,1)S(1)},...) custom-call(bf16[8,256,128]{2,1,0:T(8,128)(2,1)S(1)} %copy-done.3, ...), custom_call_target="tpu_custom_call" | custom-call | tf_op jit(solution)/shard_map/pallas_call | solution.py:585
  159.2 1.0 copy-done.4
  160.2 1.0 copy-done.5
  161.2 1.0 copy-done.6
  163.1 6.2 %slice.47.weight_ref = bf16[8,384,1024]{2,1,0:T(8,128)(2,1)} slice(bf16[8,512,1024]{2,1,0:T(8,128)(2,1)} %get-tuple-element.52), slice={[0:8], [128:512], [0:1024]} | slice | bytes 12582912 | tf_op jit(solution)/shard_map/slice | solution.py:1636
  171.0 0.8 copy.43.cols_ref
  173.0 110.6 %shard_map.301 = (bf16[8,256,128]{2,1,0:T(8,128)(2,1)}, f32[8,8,256]{2,1,0:T(8,128)}, f32[2,128]{1,0:T(2,128)}) custom-call(bf16[8,256,128]{2,1,0:T(8,128)(2,1)} %copy-done.7, bf16[2048,128,128]{2,1,0:T(8,128)(2,1)} %bitcast.4.keys_ref, f32[2048,128]{1,0:T(8,128)} %get-tuple-element.56.norms_ref, s32[256,128]{1,0:T(8,128)} %constant_dynamic-slice_fusion.1.ids_ref, ...), custom_call_target="tpu_custom_call" | custom-call | tf_op jit(solution)/shard_map/pallas_call | solution.py:1546
  283.6 36.5 %shard_map.302 = (f32[256,1024]{1,0:T(8,128)}, bf16[8,256,128]{2,1,0:T(8,128)(2,1)S(1)}, f32[2,1024]{1,0:T(2,128)S(1)}, bf16[2048,512]{1,0:T(8,128)(2,1)}, bf16[...) custom-call(bf16[8,256,128]{2,1,0:T(8,128)(2,1)} %get-tuple-element., ...), custom_call_target="tpu_custom_call" | custom-call | tf_op jit(solution)/shard_map/pallas_call | solution.py:737
  322.4 100.7 %shard_map.303 = (bf16[2048,384]{1,0:T(8,128)(2,1)}, bf16[256,1024]{1,0:T(8,128)(2,1)}, f32[1,1024]{1,0:T(1,128)}, f32[1024,256]{1,0:T(8,128)}, f32[128,256]{1,0:T(8,128)}) custom-call(bf16[8,256,128]{2,1,0:T(8,128)(2,1)} %copy-done.8, bf16[2048,384]{1,0:T(8,128)(2,1)} %get-tuple-element.67.qkv_ref, f32[2048,2]{1,0:T(8,128)} %get-tuple-element.68.lse_ref, ...), custom_call_target="tpu_custom_call" | custom-call | tf_op jit(solution)/shard_map/pallas_call | solution.py:1110
  423.1 5.4 %convolution_convert_fusion = bf16[384,1024]{1,0:T(8,128)(2,1)} fusion(bf16[2048,384]{1,0:T(8,128)(2,1)} %get-tuple-element.76, bf16[2048,1024]{1,0:T(8,128)(2,1)} %get-tuple-element.77), kind=kOutput, calls=%fused_computation.1 | convolution fusion | flops 1611005952 | bytes 6553600 | tf_op jit(solution)/shard_map/ta,tb->ab/dot_general | solution.py:20
  429.1 0.9 slice_reduce_fusion
  431.2 0.9 fusion
  432.1 1.0 copy.45
  434.4 78.6 %shard_map.304 = (bf16[8,256,1024]{2,1,0:T(8,128)(2,1)S(1)}, f32[8,256]{1,0:T(8,128)S(1)}) custom-call(bf16[256,1024]{1,0:T(8,128)(2,1)S(1)} %copy-done.11, f32[8,1024]{1,0:T(8,128)S(1)} %concatenate.16.sums_ref), custom_call_target="tpu_custom_call" | custom-call | tf_op jit(solution)/shard_map/pallas_call | solution.py:1268
  514.2 4.4 bitcast_convert_fusion
  518.6 1.7 fusion.1
  520.3 4.7 copy.64
  (81 shorter events, 11.0 us)
Async XLA Ops:
  7.2 165.2 %copy-start = (s32[2,1024,128]{2,1,0:T(8,128)S(1)}, s32[2,1024,128]{2,1,0:T(8,128)}, u32[]{:S(2)}) copy-start(s32[2,1024,128]{2,1,0:T(8,128)} %param.26) | copy-start | bytes 3145732
  7.2 5.7 %copy-start.14 = (bf16[128,1024]{1,0:T(8,128)(2,1)S(1)}, bf16[128,1024]{1,0:T(8,128)(2,1)}, u32[]{:S(2)}) copy-start(bf16[128,1024]{1,0:T(8,128)(2,1)} %param.31) | copy-start | bytes 786436
  7.2 5.7 %copy-start.15 = (bf16[128,1024]{1,0:T(8,128)(2,1)S(1)}, bf16[128,1024]{1,0:T(8,128)(2,1)}, u32[]{:S(2)}) copy-start(bf16[128,1024]{1,0:T(8,128)(2,1)} %param.30) | copy-start | bytes 786436
  7.2 5.7 %copy-start.16 = (bf16[128,1024]{1,0:T(8,128)(2,1)S(1)}, bf16[128,1024]{1,0:T(8,128)(2,1)}, u32[]{:S(2)}) copy-start(bf16[128,1024]{1,0:T(8,128)(2,1)} %param.29) | copy-start | bytes 786436
  7.2 5.7 %copy-start.17 = (bf16[128,1024]{1,0:T(8,128)(2,1)S(1)}, bf16[128,1024]{1,0:T(8,128)(2,1)}, u32[]{:S(2)}) copy-start(bf16[128,1024]{1,0:T(8,128)(2,1)} %param.32) | copy-start | bytes 786436
  7.2 315.2 %all-gather.2.cloned.1.call-start = ((), (), s32[]{:S(2)}) async-start(), calls=%async_computation.1 | async-start | bytes 4718592 | tf_op jit(solution)/shard_map/all_gather | solution.py:1641
  10.8 3.1 copy-start.23
  10.8 3.1 copy-start.24
  10.8 3.1 copy-start.25
  123.6 2.1 copy-start.3
  123.6 2.1 copy-start.12
  125.7 33.5 %copy-start.2 = (bf16[256,1024]{1,0:T(8,128)(2,1)}, bf16[256,1024]{1,0:T(8,128)(2,1)S(1)}, u32[]{:S(2)}) copy-start(bf16[256,1024]{1,0:T(8,128)(2,1)S(1)} %get-tuple-element.143.input_ref) | copy-start | bytes 1572868
  161.2 1.0 copy-start.6
  163.0 7.6 %copy-start.19 = (f32[2,1024]{1,0:T(2,128)S(1)}, f32[2,1024]{1,0:T(2,128)}, u32[]{:S(2)}) copy-start(f32[2,1024]{1,0:T(2,128)} %param.22) | copy-start | bytes 24580
  163.1 7.7 %copy-start.20 = (s32[2,1024]{1,0:T(2,128)S(1)}, s32[2,1024]{1,0:T(2,128)}, u32[]{:S(2)}) copy-start(s32[2,1024]{1,0:T(2,128)} %param.25) | copy-start | bytes 24580
  163.1 7.7 %copy-start.21 = (s32[2,1024]{1,0:T(2,128)S(1)}, s32[2,1024]{1,0:T(2,128)}, u32[]{:S(2)}) copy-start(s32[2,1024]{1,0:T(2,128)} %param.27) | copy-start | bytes 24580
  163.1 7.7 %copy-start.22 = (f32[2,1024]{1,0:T(2,128)S(1)}, f32[2,1024]{1,0:T(2,128)}, u32[]{:S(2)}) copy-start(f32[2,1024]{1,0:T(2,128)} %param.28) | copy-start | bytes 24580
  163.1 355.5 %reduce-scatter.2.cloned.1.call-start = ((), (), s32[]{:S(2)}) async-start(), calls=%async_computation.2 | async-start | bytes 983040 | tf_op jit(solution)/shard_map/reduce_scatter | solution.py:1695
  423.1 5.5 %copy-start.27 = (f32[2,128]{1,0:T(2,128)S(1)}, f32[2,128]{1,0:T(2,128)}, u32[]{:S(2)}) copy-start(f32[2,128]{1,0:T(2,128)} %get-tuple-element.82) | copy-start | bytes 3076
  423.1 8.1 %copy-start.13 = (f32[1024,256]{1,0:T(8,128)S(1)}, f32[1024,256]{1,0:T(8,128)}, u32[]{:S(2)}) copy-start(f32[1024,256]{1,0:T(8,128)} %get-tuple-element.86) | copy-start | bytes 3145732
  428.6 5.8 %copy-start.26 = (f32[1,1024]{1,0:T(1,128)S(1)}, f32[1,1024]{1,0:T(1,128)}, u32[]{:S(2)}) copy-start(f32[1,1024]{1,0:T(1,128)} %get-tuple-element.80) | copy-start | bytes 12292
  428.6 5.9 %copy-start.11 = (bf16[256,1024]{1,0:T(8,128)(2,1)S(1)}, bf16[256,1024]{1,0:T(8,128)(2,1)}, u32[]{:S(2)}) copy-start(bf16[256,1024]{1,0:T(8,128)(2,1)} %get-tuple-element.79.own_ref) | copy-start | bytes 1572868
  520.3 4.7 copy-start.18
  520.3 5.4 %copy-start.1 = (s32[2,1024,128]{2,1,0:T(8,128)S(1)}, s32[2,1024,128]{2,1,0:T(8,128)}, u32[]{:S(2)}) copy-start(s32[2,1024,128]{2,1,0:T(8,128)} %param.26) | copy-start | bytes 3145732
  (6 other events, 5.2 us)
Sparse Core Ops, SparseCore 0:
  163.2 118.6 all-gather.1
  428.7 38.2 reduce-scatter.1

commit v3 on v2

--- a/solution.py
+++ b/solution.py
@@ -14,10 +14,6 @@
 MESH = pl.DeviceIdType.MESH
 J = 128
 KEPT_BYTES = 44 * 2**20
-
-
-def outer_sum(left, right):
-    return jnp.einsum("ta,tb->ab", left, right, preferred_element_type=F32)
 
 
 def place(index, second):
@@ -614,6 +610,7 @@
     proj_ref,
     in_ref,
     mid_ref,
+    stat_ref,
     grad_one_ref,
     grad_att_ref,
     gain_ref,
@@ -680,7 +677,11 @@
 
     grad_key = jnp.concatenate([slices_ref[n] for n in range(nar)], axis=1).astype(F32)
     normed, inverse = normalise(two_ref[...])
-    gain_ref[1:2, :] = jnp.sum(grad_key * normed, axis=0, keepdims=True)
+    gain_ref[...] = jnp.zeros_like(gain_ref)
+    gain_ref[2:3, :] = jnp.sum(grad_key * normed, axis=0, keepdims=True)
+    temper_sum = jnp.sum(stat_ref[0:1, :], axis=1, keepdims=True)
+    gain_ref[3:4, :] = jnp.broadcast_to(temper_sum, (1, width))
+    gain_ref[4:5, :] = jnp.broadcast_to(stat_ref[1:2, 0:1], (1, width))
     grad = cot_ref[...].astype(F32) + normalise_back(
         grad_key, normed, inverse, gains_ref[2:3, :]
     )
@@ -709,7 +710,7 @@
             b_copy(j, c).wait_recv()
             total[at, :] += back_in[j, at, :].astype(F32)
     normed, inverse = normalise(one_ref[...])
-    gain_ref[0:1, :] = jnp.sum(total[...] * normed, axis=0, keepdims=True)
+    gain_ref[1:2, :] = jnp.sum(total[...] * normed, axis=0, keepdims=True)
     grad = grad_two[...] + normalise_back(total[...], normed, inverse, gains_ref[1:2, :])
     grad_one_ref[...] = grad
     branch = grad.astype(BF16)
@@ -726,7 +727,9 @@
             b_copy(j, c).wait_send()
 
 
-def ffn_back(slices, att, cot, one, two, gains, pre, normed, proj, in_all, out_all, wid, name):
+def ffn_back(
+    slices, att, cot, one, two, gains, pre, normed, proj, in_all, out_all, stats, wid, name
+):
     nar, tok, local = att.shape
     first, width, hidden = in_all.shape
     second = nar // first
@@ -739,7 +742,7 @@
         out_shape=(
             jax.ShapeDtypeStruct((tok, width), F32),
             jax.ShapeDtypeStruct((nar, tok, local), BF16),
-            jax.ShapeDtypeStruct((2, width), F32),
+            jax.ShapeDtypeStruct((8, width), F32),
             jax.ShapeDtypeStruct((first * hidden, second * tok), BF16),
             jax.ShapeDtypeStruct((first * hidden, second * tok), BF16),
             jax.ShapeDtypeStruct((nar * local, tok), BF16),
@@ -747,7 +750,7 @@
             jax.ShapeDtypeStruct((wid, second * tok, columns), BF16),
             jax.ShapeDtypeStruct((wid, tok, columns), BF16),
         ),
-        in_specs=[vmem] * 11,
+        in_specs=[vmem] * 12,
         out_specs=(vmem,) * 9,
         scratch_shapes=[
             pltpu.VMEM((second, tok, width), BF16),
@@ -760,7 +763,22 @@
         compiler_params=pltpu.CompilerParams(
             collective_id=name, has_side_effects=True, vmem_limit_bytes=52 * 2**20
         ),
-    )(slices, att, cot, one, two, gains, pre, normed, proj, in_all, out_all)
+    )(slices, att, cot, one, two, gains, pre, normed, proj, in_all, out_all, stats)
+
+
+REACH = ((1, 2), (0, 2), (1, 3), (2, 1))
+RELAY = {1: (0, (2, 3)), 2: (3, (0, 1))}
+
+
+def line_plan(first):
+    if first == 4:
+        return REACH, RELAY
+    return tuple(tuple(b for b in range(first) if b != a) for a in range(first)), {}
+
+
+def segment_column(seg_ref, seq, start, block):
+    row = seg_ref[pl.ds(seq, 1), start : start + block].astype(F32)
+    return jnp.transpose(jnp.broadcast_to(row, (8, block)))[:, 0:1]
 
 
 def grad_kernel(
@@ -770,26 +788,43 @@
     seqs,
     heads,
     block,
+    chunks,
     grad_ref,
-    qkv_ref,
-    lse_ref,
-    col_ref,
-    row_ref,
-    weight_ref,
-    input_ref,
-    above_ref,
+    seg_ref,
     gain_ref,
+    sums_ref,
+    pre_any,
+    act_any,
+    att_any,
+    normed_any,
+    ffn_any,
+    branch_any,
+    qkv_any,
+    lse_any,
+    one_any,
+    input_any,
+    above_any,
+    pq_any,
+    all_ref,
+    total_ref,
+    in_grad_ref,
+    out_grad_ref,
+    proj_grad_ref,
+    qkv_grad_ref,
     pre_ref,
     act_ref,
     att_ref,
     normed_ref,
     ffn_ref,
     branch_ref,
+    qkv_ref,
+    lse_ref,
+    one_ref,
+    input_ref,
+    above_ref,
+    pq_ref,
+    load_sem,
     out_ref,
-    own_ref,
-    sum_ref,
-    ffn_grad_ref,
-    proj_grad_ref,
     grads,
     got,
     grad_key,
@@ -798,11 +833,18 @@
     core_in,
     chip_out,
     chip_in,
-    held,
+    tail_sum,
     turn_out,
     turn_in,
-    line_out,
     line_in,
+    qkv_out,
+    qkv_in,
+    own_ref,
+    own_sums,
+    all_sums,
+    pieces_out,
+    pieces_in,
+    own_sem,
     a_send,
     a_recv,
     b_send,
@@ -815,6 +857,16 @@
     y_recv,
     z_send,
     z_recv,
+    w_send,
+    w_recv,
+    g_send,
+    g_recv,
+    h_send,
+    h_recv,
+    s_send,
+    s_recv,
+    p_send,
+    p_recv,
 ):
     second = nar // first
     outer = wid // 2
@@ -827,16 +879,38 @@
     columns = normed_ref.shape[2]
     rows = 2 * hidden
     body = first * rows
+    line = rows + local
     length = nar * tok // seqs
     per_seq = nar // seqs
     width = heads * HD
+    part = tok // chunks
     across = (((0,), (0,)), ((), ()))
     last = (((1,), (1,)), ((), ()))
+    reach, relay = line_plan(first)
+
+    pairs = (
+        (pre_any, pre_ref),
+        (act_any, act_ref),
+        (att_any, att_ref),
+        (normed_any, normed_ref),
+        (ffn_any, ffn_ref),
+        (branch_any, branch_ref),
+        (qkv_any, qkv_ref),
+        (lse_any, lse_ref),
+        (one_any, one_ref),
+        (input_any, input_ref),
+        (above_any, above_ref),
+        (pq_any, pq_ref),
+    )
+    loads = [
+        pltpu.make_async_copy(src, dst, load_sem.at[n]) for n, (src, dst) in enumerate(pairs)
+    ]
+    for load in loads:
+        load.start()
 
     greet(
         [place(lax.rem(me + k, nar), second) for k in range(1, nar)]
-        + [{"wide": chip * 2 + (1 - core)}]
-        + [{"wide": lax.rem(chip + i, outer) * 2 + core} for i in range(1, outer)]
+        + [{"wide": lax.rem(wide + w, wid)} for w in range(1, wid)]
     )
 
     def a_copy(target, source):
@@ -873,8 +947,8 @@
 
     def x_copy(i, q, at):
         return push(
-            chip_out.at[i, at],
-            chip_in.at[i, at],
+            chip_out.at[i - 1, at],
+            chip_in.at[i - 1, at],
             x_send.at[i, q],
             x_recv.at[i, q],
             {"wide": lax.rem(chip + i, outer) * 2 + core},
@@ -886,7 +960,62 @@
 
     def z_copy(i):
         target = {"z": lax.rem(za + i, first), "y": yb}
-        return push(line_out.at[i], line_in.at[i], z_send.at[i], z_recv.at[i], target)
+        return push(
+            core_out.at[0, pl.ds((i - 1) * line, line)],
+            line_in.at[i - 1],
+            z_send.at[i],
+            z_recv.at[i],
+            target,
+        )
+
+    def w_copy(i):
+        target = lax.rem(wide + i, wid)
+        return push(
+            qkv_out.at[target], qkv_in.at[i], w_send.at[i], w_recv.at[i], {"wide": target}
+        )
+
+    def g_copy(source_z, target_z, slot, c, own):
+        at = pl.ds(c * part, part)
+        source = source_z * second + yb
+        return push(
+            own_ref.at[at] if own else all_ref.at[source, at],
+            all_ref.at[source, at],
+            g_send.at[source_z, slot, c],
+            g_recv.at[source_z, c],
+            {"z": target_z, "y": yb},
+        )
+
+    def h_copy(source_z, j, c, own):
+        at = pl.ds(c * part, part)
+        source = source_z * second + yb
+        return push(
+            own_ref.at[at] if own else all_ref.at[source, at],
+            all_ref.at[source, at],
+            h_send.at[source_z, j, c],
+            h_recv.at[source_z, j, c],
+            {"z": za, "y": lax.rem(yb + j, second)},
+        )
+
+    def h_arrival(source_z, j, c):
+        at = pl.ds(c * part, part)
+        source = source_z * second + lax.rem(yb + second - j, second)
+        return push(
+            all_ref.at[source, at],
+            all_ref.at[source, at],
+            h_send.at[source_z, j, c],
+            h_recv.at[source_z, j, c],
+            {"z": za, "y": lax.rem(yb + j, second)},
+        )
+
+    def s_copy(k):
+        target = place(lax.rem(me + k, nar), second)
+        return push(own_sums, all_sums.at[k], s_send.at[k], s_recv.at[k], target)
+
+    def p_copy(w):
+        target = lax.rem(wide + w, wid)
+        return push(
+            pieces_out.at[target], pieces_in.at[w], p_send.at[w], p_recv.at[w], {"wide": target}
+        )
 
     def product_rows(w, z):
         own = pl.ds(pl.multiple_of(z * hidden, hidden), hidden)
@@ -901,44 +1030,46 @@
     for k in range(1, nar):
         a_copy(lax.rem(me + k, nar), me).start()
     grads[me] = grad_ref[me]
-
-    def for_core(o, carry):
+    for n in range(6):
+        loads[n].wait()
+
+    for i in range(1, outer + 1):
+        o = lax.rem(chip + i, outer)
         w = o * 2 + (1 - core)
 
-        def line(z, c):
+        def for_core(z, carry, o=o, w=w):
             upper, lower = product_rows(w, z)
             at = pl.multiple_of(z * rows, rows)
             core_out[o, pl.ds(at, hidden), :] = upper.astype(BF16)
             core_out[o, pl.ds(at + hidden, hidden), :] = lower.astype(BF16)
-            return c
-
-        lax.fori_loop(0, first, line, 0)
+            return carry
+
+        lax.fori_loop(0, first, for_core, 0)
         core_out[o, tail_rows, :] = product_tail(w).astype(BF16)
         c_copy(o).start()
-        return carry
-
-    for i in range(1, outer + 1):
-        for_core(lax.rem(chip + i, outer), 0)
 
     for i in range(1, outer):
         o = lax.rem(chip + i, outer)
         w = o * 2 + core
         c_copy(o).wait_recv()
         total = product_tail(w) + core_in[o, tail_rows, :].astype(F32)
-        chip_out[i, tail_rows, :] = total.astype(BF16)
+        chip_out[i - 1, tail_rows, :] = total.astype(BF16)
         x_copy(i, 0, tail_rows).start()
 
-        def line(n, c, o=o, w=w, i=i):
+        def for_chip(n, carry, o=o, w=w, i=i):
             z = lax.rem(za + n, first)
             upper, lower = product_rows(w, z)
             at = pl.multiple_of(z * rows, rows)
             high, low = pl.ds(at, hidden), pl.ds(at + hidden, hidden)
-            chip_out[i, high, :] = (upper + core_in[o, high, :].astype(F32)).astype(BF16)
-            chip_out[i, low, :] = (lower + core_in[o, low, :].astype(F32)).astype(BF16)
+            chip_out[i - 1, high, :] = (upper + core_in[o, high, :].astype(F32)).astype(BF16)
+            chip_out[i - 1, low, :] = (lower + core_in[o, low, :].astype(F32)).astype(BF16)
             x_copy(i, n, span(z)).start()
-            return c
-
-        lax.fori_loop(1, first + 1, line, 0)
+            return carry
+
+        lax.fori_loop(1, first + 1, for_chip, 0)
+
+    loads[6].wait()
+    loads[7].wait()
 
     def sequence(seq, carry):
         base = seq * length
@@ -958,8 +1089,8 @@
         for start in range(0, length, block):
             keys = start + block
             at = pl.multiple_of(base + start, block)
-            query_segment = col_ref[pl.ds(at, block), 0:1]
-            key_segment = row_ref[seq, 0:1, 0:keys]
+            query_segment = segment_column(seg_ref, seq, start, block)
+            key_segment = seg_ref[pl.ds(seq, 1), 0:keys].astype(F32)
             spot = lax.broadcasted_iota(jnp.int32, (block, keys), 1)
             own = lax.broadcasted_iota(jnp.int32, (block, keys), 0) + start
             allowed = (spot <= own) & (query_segment == key_segment)
@@ -1018,70 +1149,152 @@
 
     lax.fori_loop(0, seqs, sequence, 0)
 
-    w = chip * 2 + core
+    loads[8].wait()
+    qkv_part = lax.dot_general(
+        out_ref[...], one_ref[...], across, preferred_element_type=F32
+    ).astype(BF16)
+    for w in range(wid):
+        qkv_out[w] = qkv_part[:, w * columns : (w + 1) * columns]
+    for i in range(1, wid):
+        w_copy(i).start()
+
+    w_own = chip * 2 + core
     c_copy(chip).wait_recv()
-    held[tail_rows, :] = product_tail(w) + core_in[chip, tail_rows, :].astype(F32)
-
-    def line_own(z, c):
-        upper, lower = product_rows(w, z)
-        at = pl.multiple_of(z * rows, rows)
-        high, low = pl.ds(at, hidden), pl.ds(at + hidden, hidden)
-        held[high, :] = upper + core_in[chip, high, :].astype(F32)
-        held[low, :] = lower + core_in[chip, low, :].astype(F32)
-        return c
-
-    lax.fori_loop(0, first, line_own, 0)
-
+    tail_sum[...] = product_tail(w_own) + core_in[chip, tail_rows, :].astype(F32)
     for i in range(1, outer):
         x_copy(i, 0, tail_rows).wait_recv()
-        held[tail_rows, :] += chip_in[i, tail_rows, :].astype(F32)
+        tail_sum[...] += chip_in[i - 1, tail_rows, :].astype(F32)
     for j in range(1, second):
         column = lax.rem(yb + j, second)
         for z in range(first):
-            at = pl.ds(pl.multiple_of(body + (z * second + column) * local, local), local)
-            turn_out[j, z] = held[at, :].astype(BF16)
+            at = pl.ds(pl.multiple_of((z * second + column) * local, local), local)
+            turn_out[j, z] = tail_sum[at, :].astype(BF16)
         y_copy(j).start()
 
+    for n in range(9, 12):
+        loads[n].wait()
     normed, inverse = normalise(input_ref[...].astype(F32))
     mine = out_ref[pl.ds(pl.multiple_of(me * tok, tok), tok), :]
-    total = jnp.dot(mine, weight_ref[me], preferred_element_type=F32)
+    total = jnp.dot(mine, pq_ref[me, local:, :], preferred_element_type=F32)
     for k in range(1, nar):
         source = lax.rem(me + k, nar)
         b_copy(source, source).wait_recv()
-        total = total + jnp.dot(got[source], weight_ref[source], preferred_element_type=F32)
+        total = total + jnp.dot(
+            got[source], pq_ref[source, local:, :], preferred_element_type=F32
+        )
     grad = above_ref[...] + normalise_back(total, normed, inverse, gain_ref[0:1, :])
     own_ref[...] = grad.astype(BF16)
-    sum_ref[...] = jnp.sum(total * normed, axis=0, keepdims=True)
-
+
+    for c in range(chunks):
+        for z in range(first):
+
+            @pl.when(za == z)
+            def _(z=z, c=c):
+                for slot, target in enumerate(reach[z]):
+                    g_copy(za, target, slot, c, True).start()
+
+        for j in range(1, second):
+            h_copy(za, j, c, True).start()
+    own_copy = pltpu.make_async_copy(own_ref, all_ref.at[me], own_sem)
+    own_copy.start()
+    own_sums[...] = sums_ref[...]
+    own_sums[0:1, :] = jnp.sum(total * normed, axis=0, keepdims=True)
+    for k in range(1, nar):
+        s_copy(k).start()
+
+    def gathered(begin, end):
+        for c in range(chunks):
+            for d in range(begin, end):
+                for way in (-1, 1):
+                    z = za + way * d
+
+                    @pl.when((z >= 0) & (z < first))
+                    def _(z=z, c=c):
+                        g_copy(z, za, 0, c, False).wait_recv()
+                        for middle, (target, sources) in relay.items():
+
+                            @pl.when((za == middle) & ((z == sources[0]) | (z == sources[1])))
+                            def _(target=target):
+                                g_copy(z, target, 0, c, False).start()
+
+                        for j in range(1, second):
+                            h_copy(z, j, c, False).start()
+
+    for o in range(outer):
+        c_copy(o).wait_send()
     for j in range(1, second):
         y_copy(j).wait_recv()
-    for n in range(1, first + 1):
+
+    def line_parts(n):
         z = lax.rem(za + n, first)
-        at = pl.ds(pl.multiple_of(body + (z * second + yb) * local, local), local)
-        part = held[at, :]
+        at = pl.ds(pl.multiple_of((z * second + yb) * local, local), local)
+        low_part = tail_sum[at, :]
         for j in range(1, second):
-            part = part + turn_in[j, z].astype(F32)
-        whole = held[span(z), :]
+            low_part = low_part + turn_in[j, z].astype(F32)
+        upper, lower = product_rows(w_own, z)
+        start = pl.multiple_of(z * rows, rows)
+        high, low = pl.ds(start, hidden), pl.ds(start + hidden, hidden)
+        upper = upper + core_in[chip, high, :].astype(F32)
+        lower = lower + core_in[chip, low, :].astype(F32)
         for i in range(1, outer):
             x_copy(i, n, span(z)).wait_recv()
-            whole = whole + chip_in[i, span(z), :].astype(F32)
-        if n < first:
-            line_out[n, 0:rows, :] = whole.astype(BF16)
-            line_out[n, rows:, :] = part.astype(BF16)
-            z_copy(n).start()
-        else:
-            ffn_grad_ref[...] = whole
-            proj_grad_ref[...] = part
+            upper = upper + chip_in[i - 1, high, :].astype(F32)
+            lower = lower + chip_in[i - 1, low, :].astype(F32)
+        return upper, lower, low_part
+
+    def send_line(n):
+        upper, lower, low_part = line_parts(n)
+        core_out[0, (n - 1) * line : (n - 1) * line + hidden, :] = upper.astype(BF16)
+        core_out[0, (n - 1) * line + hidden : (n - 1) * line + rows, :] = lower.astype(BF16)
+        core_out[0, (n - 1) * line + rows : n * line, :] = low_part.astype(BF16)
+        z_copy(n).start()
+
+    send_line(1)
+    gathered(1, 2)
+    for n in range(2, first):
+        send_line(n)
+    gathered(2, first)
+    upper, lower, low_part = line_parts(first)
+    sums = own_sums[...]
+    for k in range(1, nar):
+        s_copy(k).wait_recv()
+        sums = sums + all_sums[k]
+    piece = total_ref.shape[1]
+    for w in range(wid):
+        pieces_out[w] = sums[:, w * piece : (w + 1) * piece]
+    for w in range(1, wid):
+        p_copy(w).start()
+    qkv_sum = qkv_out[wide].astype(F32)
+    for i in range(1, wid):
+        w_copy(i).wait_recv()
+        qkv_sum = qkv_sum + qkv_in[i].astype(F32)
+    qkv_grad_ref[...] = qkv_sum
     for n in range(1, first):
         z_copy(n).wait_recv()
-        ffn_grad_ref[...] += line_in[n, 0:rows, :].astype(F32)
-        proj_grad_ref[...] += line_in[n, rows:, :].astype(F32)
-
+        upper = upper + line_in[n - 1, 0:hidden, :].astype(F32)
+        lower = lower + line_in[n - 1, hidden:rows, :].astype(F32)
+        low_part = low_part + line_in[n - 1, rows:, :].astype(F32)
+    in_grad_ref[...] = jnp.transpose(upper)
+    out_grad_ref[...] = lower
+    proj_grad_ref[...] = low_part
+    answer = pieces_out[wide]
+    for w in range(1, wid):
+        p_copy(w).wait_recv()
+        answer = answer + pieces_in[w]
+    total_ref[...] = answer
+
+    for z in range(first):
+        for j in range(1, second):
+            for c in range(chunks):
+                h_arrival(z, j, c).wait_recv()
+    own_copy.wait()
     for k in range(1, nar):
         a_copy(lax.rem(me + k, nar), me).wait_send()
         b_copy(lax.rem(me + k, nar), me).wait_send()
-    for o in range(outer):
-        c_copy(o).wait_send()
+        s_copy(k).wait_send()
+    for w in range(1, wid):
+        p_copy(w).wait_send()
+        w_copy(w).wait_send()
     for i in range(1, outer):
         x_copy(i, 0, tail_rows).wait_send()
         for n in range(1, first + 1):
@@ -1090,48 +1303,76 @@
         y_copy(j).wait_send()
     for n in range(1, first):
         z_copy(n).wait_send()
-
-
-def attention_grads(
-    grads, qkv, lse, columns, row_form, weights, inputs, above, gain, first, wid, sides, name
-):
+    for c in range(chunks):
+        for z in range(first):
+
+            @pl.when(za == z)
+            def _(z=z, c=c):
+                for slot, target in enumerate(reach[z]):
+                    g_copy(za, target, slot, c, True).wait_send()
+                if z in relay:
+                    target, sources = relay[z]
+                    for n in sources:
+                        g_copy(n, target, 0, c, False).wait_send()
+
+            for j in range(1, second):
+                h_copy(z, j, c, False).wait_send()
+
+
+def attention_grads(grads, seg, gain, sums, sides, qkv, lse, one, inputs, above, pq, first, wid, name):
     nar, tok, local = grads.shape
     rows, wide = qkv.shape
     width = inputs.shape[1]
-    seqs, _, length = row_form.shape
+    seqs, length = seg.shape
     second = nar // first
     outer = wid // 2
     hidden = sides[0].shape[0] // first
     piece = width // wid
     body = first * 2 * hidden + nar * local
     line = 2 * hidden + local
+    chunks = 2
     vmem = pl.BlockSpec(memory_space=pltpu.VMEM)
+    hbm = pl.BlockSpec(memory_space=pl.ANY)
     dma = pltpu.SemaphoreType.DMA
+    late = (*sides, qkv, lse, one, inputs, above, pq)
     return pl.pallas_call(
-        functools.partial(grad_kernel, nar, first, wid, seqs, local // HD, min(256, length)),
+        functools.partial(
+            grad_kernel, nar, first, wid, seqs, local // HD, min(256, length), chunks
+        ),
         out_shape=(
-            jax.ShapeDtypeStruct((rows, wide), BF16),
-            jax.ShapeDtypeStruct((tok, width), BF16),
-            jax.ShapeDtypeStruct((1, width), F32),
-            jax.ShapeDtypeStruct((2 * hidden, piece), F32),
+            jax.ShapeDtypeStruct((nar, tok, width), BF16),
+            jax.ShapeDtypeStruct((8, piece), F32),
+            jax.ShapeDtypeStruct((piece, hidden), F32),
+            jax.ShapeDtypeStruct((hidden, piece), F32),
             jax.ShapeDtypeStruct((local, piece), F32),
+            jax.ShapeDtypeStruct((3 * local, piece), F32),
         ),
-        in_specs=[vmem] * 15,
-        out_specs=(vmem,) * 5,
-        scratch_shapes=[
+        in_specs=[vmem] * 4 + [hbm] * 12,
+        out_specs=(hbm,) + (vmem,) * 5,
+        scratch_shapes=[pltpu.VMEM(x.shape, x.dtype) for x in late]
+        + [
+            dma((12,)),
+            pltpu.VMEM((rows, wide), BF16),
             pltpu.VMEM((nar, tok, local), BF16),
             pltpu.VMEM((nar, tok, wide), BF16),
             pltpu.VMEM((length, local), F32),
             pltpu.VMEM((length, local), F32),
             pltpu.VMEM((outer, body, piece), BF16),
             pltpu.VMEM((outer, body, piece), BF16),
-            pltpu.VMEM((outer, body, piece), BF16),
-            pltpu.VMEM((outer, body, piece), BF16),
-            pltpu.VMEM((body, piece), F32),
+            pltpu.VMEM((outer - 1, body, piece), BF16),
+            pltpu.VMEM((outer - 1, body, piece), BF16),
+            pltpu.VMEM((nar * local, piece), F32),
             pltpu.VMEM((second, first, local, piece), BF16),
             pltpu.VMEM((second, first, local, piece), BF16),
-            pltpu.VMEM((first, line, piece), BF16),
-            pltpu.VMEM((first, line, piece), BF16),
+            pltpu.VMEM((first - 1, line, piece), BF16),
+            pltpu.VMEM((wid, 3 * local, piece), BF16),
+            pltpu.VMEM((wid, 3 * local, piece), BF16),
+            pltpu.VMEM((tok, width), BF16),
+            pltpu.VMEM((8, width), F32),
+            pltpu.VMEM((nar, 8, width), F32),
+            pltpu.VMEM((wid, 8, piece), F32),
+            pltpu.VMEM((wid, 8, piece), F32),
+            dma,
             dma((nar,)),
             dma((nar,)),
             dma((nar,)),
@@ -1144,140 +1385,9 @@
             dma((second,)),
             dma((first,)),
             dma((first,)),
-        ],
-        compiler_params=pltpu.CompilerParams(
-            collective_id=name, has_side_effects=True, vmem_limit_bytes=60 * 2**20
-        ),
-    )(grads, qkv, lse, columns, row_form, weights, inputs, above, gain, *sides)
-
-
-def tail_kernel(
-    nar,
-    wid,
-    first,
-    chunks,
-    own_ref,
-    sums_ref,
-    out_ref,
-    total_ref,
-    all_sums,
-    pieces_out,
-    pieces_in,
-    z_send,
-    z_recv,
-    y_send,
-    y_recv,
-    s_send,
-    s_recv,
-    p_send,
-    p_recv,
-):
-    second = nar // first
-    za, yb = lax.axis_index("z"), lax.axis_index("y")
-    me = za * second + yb
-    mine = lax.axis_index("wide")
-    tok = own_ref.shape[0]
-    piece = total_ref.shape[1]
-    part = tok // chunks
-
-    greet(
-        [place(lax.rem(me + k, nar), second) for k in range(1, nar)]
-        + [{"wide": lax.rem(mine + w, wid)} for w in range(1, wid)]
-    )
-
-    def z_copy(i, c):
-        rows = pl.ds(c * part, part)
-        target = lax.rem(za + i, first) * second + yb
-        return push(
-            own_ref.at[rows],
-            out_ref.at[me, rows],
-            z_send.at[i, c],
-            z_recv.at[i, c],
-            place(target, second),
-        )
-
-    def y_copy(i, j, c):
-        source = lax.rem(za + first - i, first) * second + yb
-        rows = pl.ds(c * part, part)
-        target = za * second + lax.rem(yb + j, second)
-        return push(
-            own_ref.at[rows] if i == 0 else out_ref.at[source, rows],
-            out_ref.at[source, rows],
-            y_send.at[i, j, c],
-            y_recv.at[i, j, c],
-            place(target, second),
-        )
-
-    def s_copy(k):
-        return push(
-            sums_ref,
-            all_sums.at[k],
-            s_send.at[k],
-            s_recv.at[k],
-            place(lax.rem(me + k, nar), second),
-        )
-
-    def p_copy(w):
-        target = lax.rem(mine + w, wid)
-        return push(
-            pieces_out.at[target], pieces_in.at[w], p_send.at[w], p_recv.at[w], {"wide": target}
-        )
-
-    for k in range(1, nar):
-        s_copy(k).start()
-    for c in range(chunks):
-        for i in range(1, first):
-            z_copy(i, c).start()
-        for j in range(1, second):
-            y_copy(0, j, c).start()
-    out_ref[me] = own_ref[...]
-    sums = sums_ref[...]
-    for k in range(1, nar):
-        s_copy(k).wait_recv()
-        sums = sums + all_sums[k]
-    for w in range(wid):
-        pieces_out[w] = sums[:, w * piece : (w + 1) * piece]
-    for w in range(1, wid):
-        p_copy(w).start()
-    for c in range(chunks):
-        for i in range(1, first):
-            z_copy(i, c).wait_recv()
-            for j in range(1, second):
-                y_copy(i, j, c).start()
-    answer = pieces_out[mine]
-    for w in range(1, wid):
-        p_copy(w).wait()
-        answer = answer + pieces_in[w]
-    total_ref[...] = answer
-    for k in range(1, nar):
-        s_copy(k).wait_send()
-    for c in range(chunks):
-        for i in range(1, first):
-            z_copy(i, c).wait_send()
-        for i in range(first):
-            for j in range(1, second):
-                y_copy(i, j, c).wait()
-
-
-def tail(own, sums, nar, first, wid, name):
-    tok, width = own.shape
-    second = nar // first
-    chunks = 4
-    vmem = pl.BlockSpec(memory_space=pltpu.VMEM)
-    dma = pltpu.SemaphoreType.DMA
-    return pl.pallas_call(
-        functools.partial(tail_kernel, nar, wid, first, chunks),
-        out_shape=(
-            jax.ShapeDtypeStruct((nar, tok, width), BF16),
-            jax.ShapeDtypeStruct((8, width // wid), F32),
-        ),
-        in_specs=[vmem] * 2,
-        out_specs=(vmem, vmem),
-        scratch_shapes=[
-            pltpu.VMEM((nar, 8, width), F32),
-            pltpu.VMEM((wid, 8, width // wid), F32),
-            pltpu.VMEM((wid, 8, width // wid), F32),
-            dma((first, chunks)),
+            dma((wid,)),
+            dma((wid,)),
+            dma((first, 3, chunks)),
             dma((first, chunks)),
             dma((first, second, chunks)),
             dma((first, second, chunks)),
@@ -1287,9 +1397,9 @@
             dma((wid,)),
         ],
         compiler_params=pltpu.CompilerParams(
-            collective_id=name, has_side_effects=True, vmem_limit_bytes=48 * 2**20
+            collective_id=name, has_side_effects=True, vmem_limit_bytes=63 * 2**20
         ),
-    )(own, sums)
+    )(grads, seg, gain, sums, *late)
 
 
 def neighbour_kernel(
@@ -1611,7 +1721,6 @@
         flat = values.reshape((rows,) + values.shape[2:])
         return lax.dynamic_slice_in_dim(flat, own * tok, tok, 0)
 
-    hidden = w_in.shape[1]
     seg_column = segments.reshape(rows, 1)
     seg_row = segments.reshape(seqs_here, 1, length)
     key_slices = nbr_keys.reshape(rows, nbr_keys.shape[2], nbr_keys.shape[3])
@@ -1633,7 +1742,6 @@
         2,
     )
     proj_all = pq_all[:, :local_width]
-    qkv_all = pq_all[:, local_width:]
     inputs_own = mine(block_input)
     hidden_one, hidden_two, output_own, query_key, normed_two, pre_act = ffn(
         attended_own, inputs_own, gains, proj_all, in_all, out_all, 3
@@ -1671,39 +1779,27 @@
         proj_all,
         in_all,
         out_all,
+        stats,
         wid,
         5,
     )
     grad_attended, block_output = lax.optimization_barrier((grad_attended, block_output))
-    grad_qkv, grad_own, attn_sums, grad_ffn_pair, grad_w_proj = attention_grads(
+    grad_input, totals, grad_w_in, grad_w_out, grad_w_proj, grad_w_qkv = attention_grads(
         grad_attended,
+        segments,
+        gains,
+        gain_sums,
+        sides,
         qkv,
         lse,
-        seg_column,
-        seg_row,
-        qkv_all,
+        normed_one,
         inputs_own,
         grad_hidden_one,
-        gains,
+        pq_all,
         first,
         wid,
-        sides,
         6,
     )
-    grad_w_qkv = outer_sum(grad_qkv, normed_one).astype(BF16)
-    grad_w_qkv, grad_own = lax.optimization_barrier((grad_w_qkv, grad_own))
-    grad_w_qkv = lax.psum_scatter(grad_w_qkv, "wide", scatter_dimension=1, tiled=True).astype(F32)
-    sums = jnp.concatenate(
-        [
-            attn_sums,
-            gain_sums,
-            jnp.broadcast_to(jnp.sum(stats[0]), (1, width)),
-            jnp.broadcast_to(stats[1, 0], (1, width)),
-            jnp.zeros((3, width), F32),
-        ],
-        axis=0,
-    )
-    grad_input, totals = tail(grad_own, sums, nar, first, wid, 4)
 
     return (
         block_output.reshape(seqs_here, length, width),
@@ -1713,8 +1809,8 @@
         grad_w_qkv[local_width : 2 * local_width],
         grad_w_qkv[2 * local_width :],
         grad_w_proj,
-        grad_ffn_pair[:hidden].T,
-        grad_ffn_pair[hidden:],
+        grad_w_in,
+        grad_w_out,
         totals[0],
         totals[1],
         totals[2],

time: 539 us -> 500 us (0.928)
  Pallas kernels: 466 us -> 438 us
  local copies, waits for them, and re-layouts: 36.1 us -> 28.5 us
  matrix products: 5.44 us -> 0 us
    pallas_call x1 -> x0, Pallas kernels: 78.6 us -> none  [tail(): pl.pallas_call(functools.partial(tail_kernel, nar, wid, first, chunks), o...]
    pallas_call x1, Pallas kernels: 101 us -> 149 us  [attention_grads(): pl.pallas_call(functools.partial(grad_kernel, nar, first, wid, seqs, loca...]
    slice x3 -> x0, local copies, waits for them, and re-layouts: 7.58 us -> none  [the longest x1 6.2 us: on_device(): qkv_all = pq_all[:, local_width:]]
    dot_general x1 -> x0, matrix products: 5.44 us -> none  [outer_sum(): return jnp.einsum('ta,tb->ab', left, right, preferred_element_type=F32)]
    unnamed x65 -> x58, local copies, waits for them, and re-layouts: 14.7 us -> 13.6 us
  transfers between devices with their start and end apart: 2 -> 1, of which waited for: 0 -> 0; matrix products, arithmetic and copies ran while one was open for 4% -> 1% of each run, Pallas kernels for 42% -> 30%
where the time goes in v3:
time: 500 us; the launch traced here: 495 us
  Pallas kernels  438 us (88%)
  local copies, waits for them, and re-layouts  28.5 us (6%)
  between operations  15.8 us (3%)
  other arithmetic  12.4 us (2%)
    pallas_call x1, Pallas kernels, attention_grads(): pl.pallas_call(functools.partial(grad_kernel, nar, first, wid, seqs, loca...  149 us
    pallas_call x1, Pallas kernels, neighbours(): pl.pallas_call(functools.partial(neighbour_kernel, nar, first, tiles, til...  113 us
    pallas_call x1, Pallas kernels, head(): pl.pallas_call(functools.partial(head_kernel, nar, first, wid, seqs, head...  106 us
    pallas_call x1, Pallas kernels, ffn_back(): pl.pallas_call(functools.partial(ffn_back_kernel, chunks), out_shape=(jax...  36.1 us
    pallas_call x1, Pallas kernels, ffn(): pl.pallas_call(functools.partial(ffn_kernel, chunks), out_shape=(jax.Shap...  33.3 us
    unnamed x58, local copies, waits for them, and re-layouts  13.6 us
  transfers between devices with their start and end apart: 1, of which 0 were waited for; matrix products, arithmetic and copies ran while one was open for 1% of the time, Pallas kernels for 30%

profile of v3, /device:TPU:0, one launch (start us, length us, event | category | flops | bytes accessed | tf_op | source)
XLA Modules:
  0.0 494.6 jit_solution(1356510211662407675)
XLA Ops:
  7.3 1.3 reshape.70.row_ref
  9.3 1.3 copy.42
  10.6 2.1 pad_maximum_fusion.1.qkv_weight_ref
  12.7 2.2 pad_maximum_fusion.pq_ref
  15.6 105.9 %shard_map.299 = (bf16[2048,1024]{1,0:T(8,128)(2,1)}, bf16[2048,384]{1,0:T(8,128)(2,1)}, f32[2048,2]{1,0:T(8,128)}, f32[2048,128]{1,0:T(8,128)}, bf16[8,256,128]...) custom-call(bf16[2048,1024]{1,0:T(8,128)(2,1)} %bitcast.41, ...), custom_call_target="tpu_custom_call" | custom-call | tf_op jit(solution)/shard_map/pallas_call | solution.py:442
  121.5 3.1 slice.30.proj_ref
  124.6 2.1 constant_dynamic-slice_fusion
  126.8 33.3 %shard_map.300 = (f32[256,1024]{1,0:T(8,128)S(1)}, f32[256,1024]{1,0:T(8,128)S(1)}, bf16[256,1024]{1,0:T(8,128)(2,1)S(1)}, bf16[8,256,128]{2,1,0:T(8,128)(2,1)S(...) custom-call(bf16[8,256,128]{2,1,0:T(8,128)(2,1)S(1)} %copy-done.1, ...), custom_call_target="tpu_custom_call" | custom-call | tf_op jit(solution)/shard_map/pallas_call | solution.py:581
  160.1 1.0 copy-done.3
  161.1 1.0 copy-done.4
  162.1 0.8 copy-done.5
  165.3 0.8 copy.40.cols_ref
  166.7 1.6 constant_dynamic-slice_fusion.1.ids_ref
  168.3 113.5 %shard_map.301 = (bf16[8,256,128]{2,1,0:T(8,128)(2,1)}, f32[8,8,256]{2,1,0:T(8,128)}, f32[2,128]{1,0:T(2,128)}) custom-call(bf16[8,256,128]{2,1,0:T(8,128)(2,1)} %copy-done.5, bf16[2048,128,128]{2,1,0:T(8,128)(2,1)} %bitcast.4.keys_ref, f32[2048,128]{1,0:T(8,128)} %get-tuple-element.53.norms_ref, s32[256,128]{1,0:T(8,128)} %constant_dynamic-slice_fusion.1.ids_ref, ...), custom_call_target="tpu_custom_call" | custom-call | tf_op jit(solution)/shard_map/pallas_call | solution.py:1656
  281.8 0.9 slice_reduce_fusion
  283.9 36.1 %shard_map.302 = (f32[256,1024]{1,0:T(8,128)}, bf16[8,256,128]{2,1,0:T(8,128)(2,1)S(1)}, f32[8,1024]{1,0:T(8,128)S(1)}, bf16[2048,512]{1,0:T(8,128)(2,1)}, bf16[...) custom-call(bf16[8,256,128]{2,1,0:T(8,128)(2,1)} %get-tuple-element., ...), custom_call_target="tpu_custom_call" | custom-call | tf_op jit(solution)/shard_map/pallas_call | solution.py:740
  323.0 149.0 %shard_map.303 = (bf16[8,256,1024]{2,1,0:T(8,128)(2,1)}, f32[8,256]{1,0:T(8,128)}, f32[256,512]{1,0:T(8,128)}, f32[512,256]{1,0:T(8,128)}, f32[128,256]{1,0:T(8,128)}, /*index=5*/f32[384,256]{1,0:T(8,128)}) custom-call(bf16[8,256,128]{2,1,0:T(8,128)(2,1)} %copy-done.6, s32[2,1024]{1,0:T(2,128)} %seg_ref.1, f32[3,1024]{1,0:T(4,128)} %pad_maximum_fusion.2.gain_ref.gains_ref, ...), custom_call_target="tpu_custom_call" | custom-call | tf_op jit(solution)/shard_map/pallas_call | solution.py:1338
  472.0 1.3 fusion.1
  473.3 1.4 fusion.2
  474.7 1.8 fusion
  476.5 6.8 %bitcast_convert_fusion = f32[2,1024,1024]{2,1,0:T(8,128)} fusion(bf16[2,1024,1024]{2,1,0:T(8,128)(2,1)} %bitcast.44), kind=kLoop, calls=%fused_computation | loop fusion | flops 2097152 | bytes 12582912 | tf_op jit(solution)/shard_map/reshape | solution.py:1807
  483.3 2.0 copy.61
  486.0 0.8 copy.63
  486.8 0.8 copy.64
  (61 shorter events, 8.0 us)
Async XLA Ops:
  7.2 7.8 %copy-start.21 = (f32[1024]{0:T(1024)S(1)}, f32[1024]{0:T(1024)}, u32[]{:S(2)}) copy-start(f32[1024]{0:T(1024)} %param.37) | copy-start | bytes 12292
  7.2 7.7 %copy-start.22 = (f32[1024]{0:T(1024)S(1)}, f32[1024]{0:T(1024)}, u32[]{:S(2)}) copy-start(f32[1024]{0:T(1024)} %param.36) | copy-start | bytes 12292
  7.2 7.7 %copy-start.23 = (f32[1024]{0:T(1024)S(1)}, f32[1024]{0:T(1024)}, u32[]{:S(2)}) copy-start(f32[1024]{0:T(1024)} %param.35) | copy-start | bytes 12292
  7.2 315.8 %all-gather.2.cloned.1.call-start = ((), (), s32[]{:S(2)}) async-start(), calls=%async_computation | async-start | bytes 4718592 | tf_op jit(solution)/shard_map/all_gather | solution.py:1749
  121.5 5.2 %copy-start.1 = (bf16[8,256,128]{2,1,0:T(8,128)(2,1)S(1)}, bf16[8,256,128]{2,1,0:T(8,128)(2,1)}, u32[]{:S(2)}) copy-start(bf16[8,256,128]{2,1,0:T(8,128)(2,1)} %get-tuple-element.48.att_ref) | copy-start | bytes 1572868
  121.5 5.2 %copy-start.10 = (f32[3,1024]{1,0:T(4,128)S(1)}, f32[3,1024]{1,0:T(4,128)}, u32[]{:S(2)}) copy-start(f32[3,1024]{1,0:T(4,128)} %pad_maximum_fusion.2.gain_ref.gains_ref) | copy-start | bytes 36868
  126.7 33.4 %copy-start = (bf16[256,1024]{1,0:T(8,128)(2,1)}, bf16[256,1024]{1,0:T(8,128)(2,1)S(1)}, u32[]{:S(2)}) copy-start(bf16[256,1024]{1,0:T(8,128)(2,1)S(1)} %get-tuple-element.93.input_ref.input_any) | copy-start | bytes 1572868
  126.7 38.3 %copy-start.17 = (f32[2,1024]{1,0:T(2,128)S(1)}, f32[2,1024]{1,0:T(2,128)}, u32[]{:S(2)}) copy-start(f32[2,1024]{1,0:T(2,128)} %param.22) | copy-start | bytes 24580
  126.7 38.4 %copy-start.18 = (s32[2,1024]{1,0:T(2,128)S(1)}, s32[2,1024]{1,0:T(2,128)}, u32[]{:S(2)}) copy-start(s32[2,1024]{1,0:T(2,128)} %param.25) | copy-start | bytes 24580
  126.7 38.4 %copy-start.19 = (s32[2,1024]{1,0:T(2,128)S(1)}, s32[2,1024]{1,0:T(2,128)}, u32[]{:S(2)}) copy-start(s32[2,1024]{1,0:T(2,128)} %param.27) | copy-start | bytes 24580
  126.8 38.4 %copy-start.20 = (f32[2,1024]{1,0:T(2,128)S(1)}, f32[2,1024]{1,0:T(2,128)}, u32[]{:S(2)}) copy-start(f32[2,1024]{1,0:T(2,128)} %param.28) | copy-start | bytes 24580
  160.1 1.0 copy-start.3
  161.1 1.0 copy-start.4
  162.1 0.8 copy-start.5
  162.9 0.8 copy-start.9
  163.7 118.1 %copy-start.2 = (f32[256,1024]{1,0:T(8,128)}, f32[256,1024]{1,0:T(8,128)S(1)}, u32[]{:S(2)}) copy-start(f32[256,1024]{1,0:T(8,128)S(1)} %get-tuple-element.55.one_ref) | copy-start | bytes 3145732
  283.3 0.6 copy-start.12
  320.0 0.8 copy-start.6
  320.8 0.8 copy-start.7
  321.6 0.8 copy-start.8
  476.5 6.8 %copy-start.13 = (bf16[2048,1024]{1,0:T(8,128)(2,1)S(1)}, bf16[2048,1024]{1,0:T(8,128)(2,1)}, u32[]{:S(2)}) copy-start(bf16[2048,1024]{1,0:T(8,128)(2,1)} %all-gather.2.cloned.1.call-done) | copy-start | bytes 12582916
  483.3 2.0 copy-start.16
  483.3 2.7 copy-start.15
  483.3 3.5 copy-start.14
  (1 other events, 0.6 us)
Sparse Core Ops, SparseCore 0:
  163.8 118.4 all-gather.1

commit v4 on v3

--- a/solution.py
+++ b/solution.py
@@ -67,25 +67,36 @@
     block,
     tile,
     ring,
-    input_ref,
     gain_ref,
-    qkv_weight_ref,
-    col_ref,
-    row_ref,
+    seg_ref,
+    proj_any,
+    query_any,
+    key_any,
+    value_any,
+    input_any,
     keys_ref,
+    in_any,
+    out_any,
+    normed_out,
+    qkv_out,
+    lse_out,
+    norms_out,
+    att_ref,
+    in_all,
+    out_all,
+    pq_all,
+    pq_ref,
     in_ref,
     out_ref,
-    pq_ref,
+    input_ref,
     normed_ref,
     qkv_ref,
     lse_ref,
     norms_ref,
-    att_ref,
-    in_all,
-    out_all,
-    pq_all,
     attended,
     slots,
+    load_sem,
+    store_sem,
     slot_sem,
     own_sem,
     a_send,
@@ -117,8 +128,28 @@
             keys_ref.at[pl.ds(index * tile, tile)], slots.at[slot], slot_sem.at[slot]
         )
 
-    for i in range(ring):
-        fetch(i, i).start()
+    loads = [
+        pltpu.make_async_copy(src, pq_ref.at[pl.ds(n * local, local)], load_sem.at[n])
+        for n, src in enumerate((proj_any, query_any, key_any, value_any))
+    ] + [
+        pltpu.make_async_copy(src, dst, load_sem.at[4 + n])
+        for n, (src, dst) in enumerate(
+            ((in_any, in_ref), (out_any, out_ref), (input_any, input_ref))
+        )
+    ]
+    for load in loads:
+        load.start()
+    stores = [
+        pltpu.make_async_copy(src, dst, store_sem.at[n])
+        for n, (src, dst) in enumerate(
+            (
+                (normed_ref, normed_out),
+                (qkv_ref, qkv_out),
+                (lse_ref, lse_out),
+                (norms_ref, norms_out),
+            )
+        )
+    ]
 
     greet(
         [place(lax.rem(me + k, nar), second) for k in range(1, nar)]
@@ -142,11 +173,7 @@
         count = own.shape[0] // wid
         return own.at[pl.ds(pl.multiple_of(wide * count, count), count)]
 
-    reach = ((1, 2), (0, 2), (1, 3), (2, 1))
-    relay = {1: (0, (2, 3)), 2: (3, (0, 1))}
-    if first != 4:
-        reach = tuple(tuple(b for b in range(first) if b != a) for a in range(first))
-        relay = {}
+    reach, relay = REACH, RELAY
 
     def line_copy(t, source, z, slot, own):
         return push(
@@ -285,20 +312,27 @@
 
         each_source(t, do)
 
+    for n in range(6):
+        loads[n].wait()
     for t in range(3):
         send_own(t)
+    for i in range(ring):
+        fetch(i, i).start()
+    loads[6].wait()
 
     def project(r, carry):
         at = pl.ds(pl.multiple_of(r * block, block), block)
         normed, _ = normalise(input_ref[at, :].astype(F32))
         low = (normed * gain_ref[0:1, :]).astype(BF16)
         normed_ref[at, :] = low
-        out = lax.dot_general(low, qkv_weight_ref[...], last, preferred_element_type=F32)
+        out = lax.dot_general(low, pq_ref[local:, :], last, preferred_element_type=F32)
         lanes = lax.broadcasted_iota(jnp.int32, out.shape, 1)
         qkv_ref[at, :] = jnp.where(lanes < local, out * HD ** (-0.5), out).astype(BF16)
         return carry
 
     lax.fori_loop(0, rows // block, project, 0)
+    stores[0].start()
+    stores[1].start()
     line_arrivals(0, 1, 2)
 
     def sequence(seq, carry):
@@ -307,8 +341,8 @@
             keys = start + block
             at = pl.ds(pl.multiple_of(base + start, block), block)
             whole = pl.ds(pl.multiple_of(base, length), keys)
-            query_segment = col_ref[at, 0:1]
-            key_segment = row_ref[seq, 0:1, 0:keys]
+            query_segment = segment_column(seg_ref, seq, start, block)
+            key_segment = seg_ref[pl.ds(seq, 1), 0:keys].astype(F32)
             spot = lax.broadcasted_iota(jnp.int32, (block, keys), 1)
             own = lax.broadcasted_iota(jnp.int32, (block, keys), 0) + start
             allowed = (spot <= own) & (query_segment == key_segment)
@@ -348,7 +382,9 @@
         return carry
 
     lax.fori_loop(0, seqs, sequence, 0)
-    att_ref[me] = attended[me]
+    stores[2].start()
+    own_att = pltpu.make_async_copy(attended.at[me], att_ref.at[me], own_sem.at[3])
+    own_att.start()
 
     def norms(begin, end):
         def body(index, carry):
@@ -383,6 +419,7 @@
     for n, step in enumerate(steps):
         step()
         norms(n * share_of, tiles if n == len(steps) - 1 else (n + 1) * share_of)
+    stores[3].start()
     row_arrivals()
     chip_arrivals(1)
     chip_arrivals(2)
@@ -423,14 +460,17 @@
         for j in range(1, second):
             for o in range(outer):
                 row_copy(z * second + yb, j, o, False).wait_send()
-
-
-def head(block_input, gain, w_qkv, columns, row_form, keys, w_in, w_out, pq, first, nar, wid, name):
+    own_att.wait()
+    for store in stores:
+        store.wait()
+
+
+def head(gain, seg, weights, block_input, keys, w_in, w_out, first, nar, wid, name):
     rows, width = block_input.shape
-    seqs, _, length = row_form.shape
+    seqs, length = seg.shape
     second = nar // first
     outer = wid // 2
-    local = w_qkv.shape[0] // 3
+    local = weights[0].shape[0]
     heads = local // HD
     hidden = w_in.shape[1]
     tok = rows // nar
@@ -438,29 +478,42 @@
     tile, ring = 32, 4
     block = min(256, length)
     vmem = pl.BlockSpec(memory_space=pltpu.VMEM)
+    hbm = pl.BlockSpec(memory_space=pl.ANY)
     dma = pltpu.SemaphoreType.DMA
+    kept = (
+        ((rows, width), BF16),
+        ((rows, 3 * local), BF16),
+        ((rows, heads), F32),
+        ((rows, J), F32),
+    )
     return pl.pallas_call(
         functools.partial(head_kernel, nar, first, wid, seqs, heads, block, tile, ring),
-        out_shape=(
-            jax.ShapeDtypeStruct((rows, width), BF16),
-            jax.ShapeDtypeStruct((rows, 3 * local), BF16),
-            jax.ShapeDtypeStruct((rows, heads), F32),
-            jax.ShapeDtypeStruct((rows, J), F32),
+        out_shape=tuple(jax.ShapeDtypeStruct(*x) for x in kept)
+        + (
             jax.ShapeDtypeStruct((nar, tok, local), BF16),
             jax.ShapeDtypeStruct((first, width, hidden), BF16),
             jax.ShapeDtypeStruct((first, hidden, width), BF16),
-            jax.ShapeDtypeStruct((nar,) + pq.shape, BF16),
+            jax.ShapeDtypeStruct((nar, 4 * local, width), BF16),
         ),
-        in_specs=[vmem] * 5 + [pl.BlockSpec(memory_space=pl.ANY)] + [vmem] * 3,
-        out_specs=(vmem,) * 8,
+        in_specs=[vmem] * 2 + [hbm] * 8,
+        out_specs=(hbm,) * 8,
         scratch_shapes=[
+            pltpu.VMEM((4 * local, width), BF16),
+            pltpu.VMEM((width, hidden), BF16),
+            pltpu.VMEM((hidden, width), BF16),
+            pltpu.VMEM((rows, width), BF16),
+        ]
+        + [pltpu.VMEM(*x) for x in kept]
+        + [
             pltpu.VMEM((nar, tok, local), BF16),
             pltpu.VMEM((ring, tile, depth, J), BF16),
+            dma((7,)),
+            dma((4,)),
             dma((ring,)),
-            dma((3,)),
+            dma((4,)),
             dma((nar,)),
             dma((nar,)),
-            dma((3, first, 2)),
+            dma((3, first, 3)),
             dma((3, first)),
             dma((nar, second, outer)),
             dma((nar, second, outer)),
@@ -470,9 +523,9 @@
             dma((3, nar, outer)),
         ],
         compiler_params=pltpu.CompilerParams(
-            collective_id=name, has_side_effects=True, vmem_limit_bytes=58 * 2**20
+            collective_id=name, has_side_effects=True, vmem_limit_bytes=62 * 2**20
         ),
-    )(block_input, gain, w_qkv, columns, row_form, keys, w_in, w_out, pq)
+    )(gain, seg, *weights, block_input, keys, w_in, w_out)
 
 
 INNER = 0.7978845608028654
@@ -484,11 +537,28 @@
     return 0.5 * values * (1.0 + tanh), tanh
 
 
+def own_rows(tok, second):
+    me = lax.axis_index("z") * second + lax.axis_index("y")
+    return pl.ds(pl.multiple_of(me * tok, tok), tok)
+
+
 def ffn_kernel(
     chunks,
+    gain_two_ref,
+    gain_key_ref,
+    att_any,
+    input_any,
+    pq_any,
+    in_any,
+    mid_any,
+    one_out,
+    two_out,
+    output_out,
+    key_out,
+    normed_out,
+    pre_out,
     att_ref,
     input_ref,
-    gains_ref,
     proj_ref,
     in_ref,
     mid_ref,
@@ -500,6 +570,8 @@
     pre_ref,
     back_out,
     back_in,
+    load_sem,
+    store_sem,
     n_send,
     n_recv,
     b_send,
@@ -511,6 +583,30 @@
     part = tok // chunks
     za, yb = lax.axis_index("z"), lax.axis_index("y")
 
+    pairs = (
+        (att_any, att_ref),
+        (pq_any.at[:, pl.ds(0, local)], proj_ref),
+        (input_any.at[own_rows(tok, second)], input_ref),
+        (in_any, in_ref),
+        (mid_any, mid_ref),
+    )
+    loads = [
+        pltpu.make_async_copy(src, dst, load_sem.at[n]) for n, (src, dst) in enumerate(pairs)
+    ]
+    for load in loads:
+        load.start()
+    kept = (
+        (one_ref, one_out),
+        (normed_ref, normed_out),
+        (pre_ref, pre_out),
+        (key_ref, key_out),
+        (two_ref, two_out),
+        (output_ref, output_out),
+    )
+    stores = [
+        pltpu.make_async_copy(src, dst, store_sem.at[n]) for n, (src, dst) in enumerate(kept)
+    ]
+
     greet([{"z": za, "y": lax.rem(yb + j, second)} for j in range(1, second)])
 
     def n_copy(j, c):
@@ -538,82 +634,127 @@
             total = total + jnp.dot(activated, mid_ref[z], preferred_element_type=F32)
         return total
 
+    for n in range(3):
+        loads[n].wait()
     att = jnp.concatenate([att_ref[n] for n in range(nar)], axis=1)
     one = input_ref[...].astype(F32) + jnp.dot(
         att, proj_ref[...].reshape(nar * local, width), preferred_element_type=F32
     )
     one_ref[...] = one
     normed, _ = normalise(one)
-    normed_ref[0] = (normed * gains_ref[1:2, :]).astype(BF16)
+    normed_ref[0] = (normed * gain_two_ref[...]).astype(BF16)
     for c in range(chunks):
         for j in range(1, second):
             n_copy(j, c).start()
+    stores[0].start()
+    for n in range(3, 5):
+        loads[n].wait()
     two_ref[...] = one_ref[...] + through(0, 0, tok)
     for c in range(chunks):
         for j in range(1, second):
             n_copy(j, c).wait_recv()
             back_out[j, c * part : (c + 1) * part, :] = through(j, c * part, part).astype(BF16)
             b_copy(j, c).start()
+    stores[1].start()
+    stores[2].start()
     for c in range(chunks):
         at = slice(c * part, (c + 1) * part)
         for j in range(1, second):
             b_copy(j, c).wait_recv()
             two_ref[at, :] += back_in[j, at, :].astype(F32)
     hidden_two = two_ref[...]
-    output_ref[...] = hidden_two.astype(BF16)
     normed, _ = normalise(hidden_two)
-    query_key = (normed * gains_ref[2:3, :]).astype(BF16)
+    query_key = (normed * gain_key_ref[...]).astype(BF16)
     for n in range(nar):
         key_ref[n] = query_key[:, n * (width // nar) : (n + 1) * (width // nar)]
+    stores[3].start()
+    stores[4].start()
+    output_ref[...] = hidden_two.astype(BF16)
+    stores[5].start()
     for c in range(chunks):
         for j in range(1, second):
             n_copy(j, c).wait_send()
             b_copy(j, c).wait_send()
-
-
-def ffn(att, inputs, gains, proj, in_all, out_all, name):
+    for store in stores:
+        store.wait()
+
+
+def ffn(gain_two, gain_key, att, inputs, pq, in_all, out_all, name):
     nar, tok, local = att.shape
     first, width, hidden = in_all.shape
     second = nar // first
     chunks = 2
     vmem = pl.BlockSpec(memory_space=pltpu.VMEM)
-    dma = pltpu.SemaphoreType.DMA((second, chunks))
+    hbm = pl.BlockSpec(memory_space=pl.ANY)
+    dma = pltpu.SemaphoreType.DMA
+    outs = (
+        ((tok, width), F32),
+        ((tok, width), F32),
+        ((tok, width), BF16),
+        ((nar, tok, width // nar), BF16),
+        ((second, tok, width), BF16),
+        ((second, tok, first * hidden), F32),
+    )
     return pl.pallas_call(
         functools.partial(ffn_kernel, chunks),
-        out_shape=(
-            jax.ShapeDtypeStruct((tok, width), F32),
-            jax.ShapeDtypeStruct((tok, width), F32),
-            jax.ShapeDtypeStruct((tok, width), BF16),
-            jax.ShapeDtypeStruct((nar, tok, width // nar), BF16),
-            jax.ShapeDtypeStruct((second, tok, width), BF16),
-            jax.ShapeDtypeStruct((second, tok, first * hidden), F32),
+        out_shape=tuple(jax.ShapeDtypeStruct(*x) for x in outs),
+        in_specs=[vmem] * 2 + [hbm] * 5,
+        out_specs=(hbm,) * 6,
+        scratch_shapes=[
+            pltpu.VMEM(att.shape, BF16),
+            pltpu.VMEM((tok, width), BF16),
+            pltpu.VMEM((nar, local, width), BF16),
+            pltpu.VMEM(in_all.shape, BF16),
+            pltpu.VMEM(out_all.shape, BF16),
+        ]
+        + [pltpu.VMEM(*x) for x in outs]
+        + [pltpu.VMEM((second, tok, width), BF16)] * 2
+        + [dma((5,)), dma((6,))]
+        + [dma((second, chunks))] * 4,
+        compiler_params=pltpu.CompilerParams(
+            collective_id=name, has_side_effects=True, vmem_limit_bytes=62 * 2**20
         ),
-        in_specs=[vmem] * 6,
-        out_specs=(vmem,) * 6,
-        scratch_shapes=[pltpu.VMEM((second, tok, width), BF16)] * 2 + [dma] * 4,
-        compiler_params=pltpu.CompilerParams(
-            collective_id=name, has_side_effects=True, vmem_limit_bytes=48 * 2**20
-        ),
-    )(att, inputs, gains, proj, in_all, out_all)
+    )(gain_two, gain_key, att, inputs, pq, in_all, out_all)
 
 
 def ffn_back_kernel(
     chunks,
+    gain_two_ref,
+    gain_key_ref,
     slices_ref,
+    stat_ref,
+    two_any,
+    cot_any,
+    mid_any,
+    pre_any,
+    in_any,
+    att_any,
+    normed_any,
+    one_any,
+    pq_any,
+    share_any,
+    sums_ref,
+    grad_one_out,
+    grad_att_out,
+    pre_turned_out,
+    act_turned_out,
+    att_turned_out,
+    normed_cols_out,
+    ffn_cols_out,
+    branch_cols_out,
+    line_ref,
+    two_ref,
+    cot_ref,
+    mid_ref,
+    pre_ref,
+    in_ref,
     att_ref,
-    cot_ref,
+    normed_ref,
     one_ref,
-    two_ref,
-    gains_ref,
-    pre_ref,
-    normed_ref,
     proj_ref,
-    in_ref,
-    mid_ref,
-    stat_ref,
+    share_ref,
     grad_one_ref,
     grad_att_ref,
-    gain_ref,
     pre_turned_ref,
     act_turned_ref,
     att_turned_ref,
@@ -625,10 +766,15 @@
     total,
     back_out,
     back_in,
+    load_sem,
+    store_sem,
+    own_sem,
     n_send,
     n_recv,
     b_send,
     b_recv,
+    g_send,
+    g_recv,
 ):
     nar, tok, local = att_ref.shape
     first, width, hidden = in_ref.shape
@@ -638,8 +784,43 @@
     part = tok // chunks
     last = (((1,), (1,)), ((), ()))
     za, yb = lax.axis_index("z"), lax.axis_index("y")
-
-    greet([{"z": za, "y": lax.rem(yb + j, second)} for j in range(1, second)])
+    reach, relay = REACH, RELAY
+
+    pairs = (
+        (share_any, share_ref),
+        (two_any, two_ref),
+        (cot_any.at[own_rows(tok, second)], cot_ref),
+        (mid_any, mid_ref),
+        (pre_any, pre_ref),
+        (in_any, in_ref),
+        (att_any, att_ref),
+        (normed_any, normed_ref),
+        (one_any, one_ref),
+        (pq_any.at[:, pl.ds(0, local)], proj_ref),
+    )
+    loads = [
+        pltpu.make_async_copy(src, dst, load_sem.at[n]) for n, (src, dst) in enumerate(pairs)
+    ]
+    for load in loads:
+        load.start()
+    kept = (
+        (ffn_cols_ref, ffn_cols_out),
+        (pre_turned_ref, pre_turned_out),
+        (act_turned_ref, act_turned_out),
+        (att_turned_ref, att_turned_out),
+        (normed_cols_ref, normed_cols_out),
+        (grad_att_ref, grad_att_out),
+        (branch_cols_ref, branch_cols_out),
+        (grad_one_ref, grad_one_out),
+    )
+    stores = [
+        pltpu.make_async_copy(src, dst, store_sem.at[n]) for n, (src, dst) in enumerate(kept)
+    ]
+
+    greet(
+        [{"z": za, "y": lax.rem(yb + j, second)} for j in range(1, second)]
+        + [{"z": lax.rem(za + i, first), "y": yb} for i in range(1, first)]
+    )
 
     def n_copy(j, c):
         at = pl.ds(c * part, part)
@@ -652,6 +833,42 @@
         return push(
             back_out.at[j, at], back_in.at[j, at], b_send.at[j, c], b_recv.at[j, c], target
         )
+
+    def g_copy(source, target, slot, c, own):
+        at = pl.ds(c * part, part)
+        return push(
+            share_ref.at[at] if own else line_ref.at[source, at],
+            line_ref.at[source, at],
+            g_send.at[source, slot, c],
+            g_recv.at[source, c],
+            {"z": target, "y": yb},
+        )
+
+    def gathered(c, begin, end):
+        for d in range(begin, end):
+            for way in (-1, 1):
+                z = za + way * d
+
+                @pl.when((z >= 0) & (z < first))
+                def _(z=z):
+                    g_copy(z, za, 0, c, False).wait_recv()
+                    for middle, (target, sources) in relay.items():
+
+                        @pl.when((za == middle) & ((z == sources[0]) | (z == sources[1])))
+                        def _(target=target):
+                            g_copy(z, target, 0, c, False).start()
+
+    loads[0].wait()
+    for c in range(chunks):
+        for z in range(first):
+
+            @pl.when(za == z)
+            def _(z=z, c=c):
+                for slot, target in enumerate(reach[z]):
+                    g_copy(za, target, slot, c, True).start()
+
+    own_copy = pltpu.make_async_copy(share_ref, line_ref.at[za], own_sem)
+    own_copy.start()
 
     def through(j, start, count):
         at = slice(start, start + count)
@@ -675,60 +892,103 @@
             )
         return sums
 
+    for n in range(1, 3):
+        loads[n].wait()
     grad_key = jnp.concatenate([slices_ref[n] for n in range(nar)], axis=1).astype(F32)
     normed, inverse = normalise(two_ref[...])
-    gain_ref[...] = jnp.zeros_like(gain_ref)
-    gain_ref[2:3, :] = jnp.sum(grad_key * normed, axis=0, keepdims=True)
+    sums_ref[...] = jnp.zeros_like(sums_ref)
+    sums_ref[2:3, :] = jnp.sum(grad_key * normed, axis=0, keepdims=True)
     temper_sum = jnp.sum(stat_ref[0:1, :], axis=1, keepdims=True)
-    gain_ref[3:4, :] = jnp.broadcast_to(temper_sum, (1, width))
-    gain_ref[4:5, :] = jnp.broadcast_to(stat_ref[1:2, 0:1], (1, width))
+    sums_ref[3:4, :] = jnp.broadcast_to(temper_sum, (1, width))
+    sums_ref[4:5, :] = jnp.broadcast_to(stat_ref[1:2, 0:1], (1, width))
     grad = cot_ref[...].astype(F32) + normalise_back(
-        grad_key, normed, inverse, gains_ref[2:3, :]
+        grad_key, normed, inverse, gain_key_ref[...]
     )
     grad_two[...] = grad
     grads[0] = grad.astype(BF16)
     for c in range(chunks):
         for j in range(1, second):
             n_copy(j, c).start()
+    for n in range(3, 6):
+        loads[n].wait()
     total[...] = through(0, 0, tok)
+    gathered(0, 1, 2)
     for c in range(chunks):
         for j in range(1, second):
             n_copy(j, c).wait_recv()
             back_out[j, c * part : (c + 1) * part, :] = through(j, c * part, part).astype(BF16)
             b_copy(j, c).start()
-    att_turned_ref[...] = jnp.concatenate(
-        [jnp.transpose(att_ref[n].astype(F32)).astype(BF16) for n in range(nar)], axis=0
-    )
+    gathered(0, 2, first)
+    gathered(1, 1, first)
+    for n in range(6, 10):
+        loads[n].wait()
     for j in range(second):
         for w in range(wid):
             own = slice(w * columns, (w + 1) * columns)
             normed_cols_ref[w, j * tok : (j + 1) * tok, :] = normed_ref[j, :, own]
             ffn_cols_ref[w, j * tok : (j + 1) * tok, :] = grads[j, :, own]
+    att_turned_ref[...] = jnp.concatenate(
+        [jnp.transpose(att_ref[n].astype(F32)).astype(BF16) for n in range(nar)], axis=0
+    )
+    for n in range(5):
+        stores[n].start()
     for c in range(chunks):
         at = slice(c * part, (c + 1) * part)
         for j in range(1, second):
             b_copy(j, c).wait_recv()
             total[at, :] += back_in[j, at, :].astype(F32)
     normed, inverse = normalise(one_ref[...])
-    gain_ref[1:2, :] = jnp.sum(total[...] * normed, axis=0, keepdims=True)
-    grad = grad_two[...] + normalise_back(total[...], normed, inverse, gains_ref[1:2, :])
-    grad_one_ref[...] = grad
+    sums_ref[1:2, :] = jnp.sum(total[...] * normed, axis=0, keepdims=True)
+    grad = grad_two[...] + normalise_back(total[...], normed, inverse, gain_two_ref[...])
     branch = grad.astype(BF16)
     grad_att = lax.dot_general(
         branch, proj_ref[...].reshape(nar * local, width), last, preferred_element_type=F32
     ).astype(BF16)
     for n in range(nar):
         grad_att_ref[n] = grad_att[:, n * local : (n + 1) * local]
+    stores[5].start()
     for w in range(wid):
         branch_cols_ref[w] = branch[:, w * columns : (w + 1) * columns]
+    stores[6].start()
+    grad_one_ref[...] = grad
+    stores[7].start()
+    own_copy.wait()
     for c in range(chunks):
         for j in range(1, second):
             n_copy(j, c).wait_send()
             b_copy(j, c).wait_send()
+        for z in range(first):
+
+            @pl.when(za == z)
+            def _(z=z, c=c):
+                for slot, target in enumerate(reach[z]):
+                    g_copy(za, target, slot, c, True).wait_send()
+                if z in relay:
+                    target, sources = relay[z]
+                    for n in sources:
+                        g_copy(n, target, 0, c, False).wait_send()
+
+    for store in stores:
+        store.wait()
 
 
 def ffn_back(
-    slices, att, cot, one, two, gains, pre, normed, proj, in_all, out_all, stats, wid, name
+    gain_two,
+    gain_key,
+    slices,
+    stats,
+    two,
+    cot,
+    out_all,
+    pre,
+    in_all,
+    att,
+    normed,
+    one,
+    pq,
+    share,
+    wid,
+    name,
 ):
     nar, tok, local = att.shape
     first, width, hidden = in_all.shape
@@ -736,44 +996,166 @@
     chunks = 2
     columns = width // wid
     vmem = pl.BlockSpec(memory_space=pltpu.VMEM)
-    dma = pltpu.SemaphoreType.DMA((second, chunks))
+    hbm = pl.BlockSpec(memory_space=pl.ANY)
+    dma = pltpu.SemaphoreType.DMA
+    outs = (
+        ((tok, width), F32),
+        ((nar, tok, local), BF16),
+        ((first * hidden, second * tok), BF16),
+        ((first * hidden, second * tok), BF16),
+        ((nar * local, tok), BF16),
+        ((wid, second * tok, columns), BF16),
+        ((wid, second * tok, columns), BF16),
+        ((wid, tok, columns), BF16),
+    )
     return pl.pallas_call(
         functools.partial(ffn_back_kernel, chunks),
-        out_shape=(
-            jax.ShapeDtypeStruct((tok, width), F32),
-            jax.ShapeDtypeStruct((nar, tok, local), BF16),
-            jax.ShapeDtypeStruct((8, width), F32),
-            jax.ShapeDtypeStruct((first * hidden, second * tok), BF16),
-            jax.ShapeDtypeStruct((first * hidden, second * tok), BF16),
-            jax.ShapeDtypeStruct((nar * local, tok), BF16),
-            jax.ShapeDtypeStruct((wid, second * tok, columns), BF16),
-            jax.ShapeDtypeStruct((wid, second * tok, columns), BF16),
-            jax.ShapeDtypeStruct((wid, tok, columns), BF16),
-        ),
-        in_specs=[vmem] * 12,
-        out_specs=(vmem,) * 9,
+        out_shape=(jax.ShapeDtypeStruct((8, width), F32),)
+        + tuple(jax.ShapeDtypeStruct(*x) for x in outs)
+        + (jax.ShapeDtypeStruct((first, tok, width), BF16),),
+        in_specs=[vmem] * 4 + [hbm] * 10,
+        out_specs=(vmem,) + (hbm,) * 9,
         scratch_shapes=[
+            pltpu.VMEM((tok, width), F32),
+            pltpu.VMEM((tok, width), BF16),
+            pltpu.VMEM(out_all.shape, BF16),
+            pltpu.VMEM(pre.shape, F32),
+            pltpu.VMEM(in_all.shape, BF16),
+            pltpu.VMEM(att.shape, BF16),
+            pltpu.VMEM(normed.shape, BF16),
+            pltpu.VMEM((tok, width), F32),
+            pltpu.VMEM((nar, local, width), BF16),
+            pltpu.VMEM((tok, width), BF16),
+        ]
+        + [pltpu.VMEM(*x) for x in outs]
+        + [
             pltpu.VMEM((second, tok, width), BF16),
             pltpu.VMEM((tok, width), F32),
             pltpu.VMEM((tok, width), F32),
             pltpu.VMEM((second, tok, width), BF16),
             pltpu.VMEM((second, tok, width), BF16),
+            dma((10,)),
+            dma((8,)),
+            dma,
         ]
-        + [dma] * 4,
+        + [dma((second, chunks))] * 4
+        + [dma((first, 3, chunks)), dma((first, chunks))],
         compiler_params=pltpu.CompilerParams(
-            collective_id=name, has_side_effects=True, vmem_limit_bytes=52 * 2**20
+            collective_id=name, has_side_effects=True, vmem_limit_bytes=62 * 2**20
         ),
-    )(slices, att, cot, one, two, gains, pre, normed, proj, in_all, out_all, stats)
+    )(
+        gain_two,
+        gain_key,
+        slices,
+        stats,
+        two,
+        cot,
+        out_all,
+        pre,
+        in_all,
+        att,
+        normed,
+        one,
+        pq,
+        share,
+    )
+
+
+def finish_kernel(
+    second, grad_ref, block_ref, line_ref, total_ref, loss_ref, qkv_ref, proj_ref, in_ref, mid_ref, *outs
+):
+    (
+        block_out,
+        loss_out,
+        grad_out,
+        query_out,
+        key_out,
+        value_out,
+        proj_out,
+        in_out,
+        mid_out,
+        attn_out,
+        ffn_out,
+        last_out,
+        temper_out,
+        mix_out,
+    ) = outs
+    grad_out[...] = grad_ref[...].astype(F32)
+    near = lax.rem(pl.program_id(0), second) == lax.axis_index("y")
+
+    @pl.when(near)
+    def _():
+        block_out[...] = line_ref[...]
+
+    @pl.when(jnp.logical_not(near))
+    def _():
+        block_out[...] = block_ref[...]
+
+    @pl.when(pl.program_id(0) == 0)
+    def _():
+        local = proj_ref.shape[0]
+        query_out[...] = qkv_ref[0:local, :]
+        key_out[...] = qkv_ref[local : 2 * local, :]
+        value_out[...] = qkv_ref[2 * local : 3 * local, :]
+        proj_out[...] = proj_ref[...]
+        in_out[...] = in_ref[...]
+        mid_out[...] = mid_ref[...]
+        attn_out[...] = total_ref[0:1, :]
+        ffn_out[...] = total_ref[1:2, :]
+        last_out[...] = total_ref[2:3, :]
+        temper_out[...] = total_ref[3:4, 0:1]
+        mix_out[...] = total_ref[4:5, 0:1]
+        nar, _, tok = loss_ref.shape
+        seqs = loss_out.shape[0]
+        per_seq = nar // seqs
+        for n in range(nar):
+            at = (n % per_seq) * tok
+            loss_out[n // per_seq : n // per_seq + 1, at : at + tok] = loss_ref[n, 0:1, :]
+
+
+def finish(grad, block, lines, totals, losses, qkv, proj, w_in, w_out, seqs):
+    nar, tok, width = grad.shape
+    second = nar // lines.shape[0]
+    local, piece = proj.shape
+
+    def whole(shape):
+        return pl.BlockSpec(shape, lambda i: (0,) * len(shape))
+
+    def each():
+        return pl.BlockSpec((1, tok, width), lambda i: (i, 0, 0))
+
+    small = [
+        ((local, piece), F32),
+        ((local, piece), F32),
+        ((local, piece), F32),
+        (proj.shape, F32),
+        (w_in.shape, F32),
+        (w_out.shape, F32),
+        ((1, piece), F32),
+        ((1, piece), F32),
+        ((1, piece), F32),
+        ((1, 1), F32),
+        ((1, 1), F32),
+    ]
+    loss_shape = (seqs, nar * tok // seqs)
+    return pl.pallas_call(
+        functools.partial(finish_kernel, second),
+        grid=(nar,),
+        out_shape=(
+            jax.ShapeDtypeStruct((nar, tok, width), BF16),
+            jax.ShapeDtypeStruct(loss_shape, F32),
+            jax.ShapeDtypeStruct((nar, tok, width), F32),
+        )
+        + tuple(jax.ShapeDtypeStruct(*x) for x in small),
+        in_specs=[each(), each(), pl.BlockSpec((1, tok, width), lambda i: (i // second, 0, 0))]
+        + [whole(x.shape) for x in (totals, losses, qkv, proj, w_in, w_out)],
+        out_specs=(each(), whole(loss_shape), each()) + tuple(whole(x[0]) for x in small),
+        compiler_params=pltpu.CompilerParams(vmem_limit_bytes=62 * 2**20),
+    )(grad, block, lines, totals, losses, qkv, proj, w_in, w_out)
 
 
 REACH = ((1, 2), (0, 2), (1, 3), (2, 1))
 RELAY = {1: (0, (2, 3)), 2: (3, (0, 1))}
-
-
-def line_plan(first):
-    if first == 4:
-        return REACH, RELAY
-    return tuple(tuple(b for b in range(first) if b != a) for a in range(first)), {}
 
 
 def segment_column(seg_ref, seq, start, block):
@@ -789,10 +1171,11 @@
     heads,
     block,
     chunks,
-    grad_ref,
     seg_ref,
     gain_ref,
     sums_ref,
+    grad_ref,
+    line_any,
     pre_any,
     act_any,
     att_any,
@@ -806,6 +1189,7 @@
     above_any,
     pq_any,
     all_ref,
+    block_ref,
     total_ref,
     in_grad_ref,
     out_grad_ref,
@@ -837,6 +1221,7 @@
     turn_out,
     turn_in,
     line_in,
+    work,
     qkv_out,
     qkv_in,
     own_ref,
@@ -845,6 +1230,8 @@
     pieces_out,
     pieces_in,
     own_sem,
+    k_send,
+    k_recv,
     a_send,
     a_recv,
     b_send,
@@ -874,7 +1261,7 @@
     me = za * second + yb
     wide = lax.axis_index("wide")
     chip, core = wide // 2, lax.rem(wide, 2)
-    tok, local = grad_ref.shape[1:]
+    tok, local = grads.shape[1:]
     hidden = pre_ref.shape[0] // first
     columns = normed_ref.shape[2]
     rows = 2 * hidden
@@ -886,7 +1273,7 @@
     part = tok // chunks
     across = (((0,), (0,)), ((), ()))
     last = (((1,), (1,)), ((), ()))
-    reach, relay = line_plan(first)
+    reach, relay = REACH, RELAY
 
     pairs = (
         (pre_any, pre_ref),
@@ -898,7 +1285,7 @@
         (qkv_any, qkv_ref),
         (lse_any, lse_ref),
         (one_any, one_ref),
-        (input_any, input_ref),
+        (input_any.at[own_rows(tok, second)], input_ref),
         (above_any, above_ref),
         (pq_any, pq_ref),
     )
@@ -931,6 +1318,15 @@
             place(target, second),
         )
 
+    def k_copy(z, j):
+        return push(
+            line_any.at[z],
+            block_ref.at[z * second + yb],
+            k_send.at[z, j],
+            k_recv.at[z, j],
+            {"z": za, "y": lax.rem(yb + j, second)},
+        )
+
     def c_copy(o):
         return push(
             core_out.at[o],
@@ -958,14 +1354,32 @@
         target = {"z": za, "y": lax.rem(yb + j, second)}
         return push(turn_out.at[j], turn_in.at[j], y_send.at[j], y_recv.at[j], target)
 
-    def z_copy(i):
-        target = {"z": lax.rem(za + i, first), "y": yb}
-        return push(
-            core_out.at[0, pl.ds((i - 1) * line, line)],
-            line_in.at[i - 1],
-            z_send.at[i],
-            z_recv.at[i],
-            target,
+    inner = jnp.where((za == 1) | (za == 2), 1, 0)
+
+    def mirror(z):
+        return jnp.where(za < 2, z, 3 - z)
+
+    def dest(n):
+        return mirror(jnp.where(n == 1, 3, jnp.where(n == 2, 2, jnp.where(n == 3, 1 - inner, inner))))
+
+    def z_copy(n):
+        slot = jnp.where(inner == 1, (3, 4, 0)[n - 1], n - 1)
+        target = mirror(jnp.where(inner == 1, (2, 2, 0)[n - 1], 1))
+        return push(
+            core_out.at[0, pl.ds((n - 1) * line, line)],
+            line_in.at[slot],
+            z_send.at[n],
+            z_recv.at[slot],
+            {"z": target, "y": yb},
+        )
+
+    def z_arrival(slot):
+        return push(
+            core_out.at[0, pl.ds(0, line)],
+            line_in.at[slot],
+            z_send.at[0],
+            z_recv.at[slot],
+            {"z": mirror(jnp.where(inner == 1, 0, 1)), "y": yb},
         )
 
     def w_copy(i):
@@ -1029,7 +1443,10 @@
 
     for k in range(1, nar):
         a_copy(lax.rem(me + k, nar), me).start()
-    grads[me] = grad_ref[me]
+    own_grad = pltpu.make_async_copy(grad_ref.at[me], grads.at[me], own_sem.at[1])
+    own_grad.start()
+    for j in range(1, second):
+        k_copy(0, j).start()
     for n in range(6):
         loads[n].wait()
 
@@ -1057,7 +1474,7 @@
         x_copy(i, 0, tail_rows).start()
 
         def for_chip(n, carry, o=o, w=w, i=i):
-            z = lax.rem(za + n, first)
+            z = dest(n)
             upper, lower = product_rows(w, z)
             at = pl.multiple_of(z * rows, rows)
             high, low = pl.ds(at, hidden), pl.ds(at + hidden, hidden)
@@ -1070,6 +1487,7 @@
 
     loads[6].wait()
     loads[7].wait()
+    own_grad.wait()
 
     def sequence(seq, carry):
         base = seq * length
@@ -1149,6 +1567,9 @@
 
     lax.fori_loop(0, seqs, sequence, 0)
 
+    for z in range(1, first):
+        for j in range(1, second):
+            k_copy(z, j).start()
     loads[8].wait()
     qkv_part = lax.dot_general(
         out_ref[...], one_ref[...], across, preferred_element_type=F32
@@ -1195,7 +1616,7 @@
 
         for j in range(1, second):
             h_copy(za, j, c, True).start()
-    own_copy = pltpu.make_async_copy(own_ref, all_ref.at[me], own_sem)
+    own_copy = pltpu.make_async_copy(own_ref, all_ref.at[me], own_sem.at[0])
     own_copy.start()
     own_sums[...] = sums_ref[...]
     own_sums[0:1, :] = jnp.sum(total * normed, axis=0, keepdims=True)
@@ -1226,7 +1647,7 @@
         y_copy(j).wait_recv()
 
     def line_parts(n):
-        z = lax.rem(za + n, first)
+        z = dest(n)
         at = pl.ds(pl.multiple_of((z * second + yb) * local, local), local)
         low_part = tail_sum[at, :]
         for j in range(1, second):
@@ -1240,21 +1661,33 @@
             x_copy(i, n, span(z)).wait_recv()
             upper = upper + chip_in[i - 1, high, :].astype(F32)
             lower = lower + chip_in[i - 1, low, :].astype(F32)
-        return upper, lower, low_part
-
-    def send_line(n):
-        upper, lower, low_part = line_parts(n)
-        core_out[0, (n - 1) * line : (n - 1) * line + hidden, :] = upper.astype(BF16)
-        core_out[0, (n - 1) * line + hidden : (n - 1) * line + rows, :] = lower.astype(BF16)
-        core_out[0, (n - 1) * line + rows : n * line, :] = low_part.astype(BF16)
-        z_copy(n).start()
-
-    send_line(1)
+        work[0:hidden, :] = upper
+        work[hidden:rows, :] = lower
+        work[rows:, :] = low_part
+
+    def add_arrival(slot):
+        z_arrival(slot).wait_recv()
+        work[...] += line_in[slot].astype(F32)
+
+    @pl.when(inner == 0)
+    def _():
+        for n in range(1, 4):
+            line_parts(n)
+            core_out[0, (n - 1) * line : n * line, :] = work[...].astype(BF16)
+            z_copy(n).start()
+
     gathered(1, 2)
-    for n in range(2, first):
-        send_line(n)
     gathered(2, first)
-    upper, lower, low_part = line_parts(first)
+
+    @pl.when(inner == 1)
+    def _():
+        for n in range(1, 4):
+            line_parts(n)
+            add_arrival((0, 1, 3)[n - 1])
+            core_out[0, (n - 1) * line : n * line, :] = work[...].astype(BF16)
+            z_copy(n).start()
+
+    line_parts(4)
     sums = own_sums[...]
     for k in range(1, nar):
         s_copy(k).wait_recv()
@@ -1269,14 +1702,19 @@
         w_copy(i).wait_recv()
         qkv_sum = qkv_sum + qkv_in[i].astype(F32)
     qkv_grad_ref[...] = qkv_sum
-    for n in range(1, first):
-        z_copy(n).wait_recv()
-        upper = upper + line_in[n - 1, 0:hidden, :].astype(F32)
-        lower = lower + line_in[n - 1, hidden:rows, :].astype(F32)
-        low_part = low_part + line_in[n - 1, rows:, :].astype(F32)
-    in_grad_ref[...] = jnp.transpose(upper)
-    out_grad_ref[...] = lower
-    proj_grad_ref[...] = low_part
+
+    @pl.when(inner == 0)
+    def _():
+        add_arrival(0)
+
+    @pl.when(inner == 1)
+    def _():
+        add_arrival(2)
+        add_arrival(4)
+
+    in_grad_ref[...] = jnp.transpose(work[0:hidden, :])
+    out_grad_ref[...] = work[hidden:rows, :]
+    proj_grad_ref[...] = work[rows:, :]
     answer = pieces_out[wide]
     for w in range(1, wid):
         p_copy(w).wait_recv()
@@ -1288,6 +1726,9 @@
             for c in range(chunks):
                 h_arrival(z, j, c).wait_recv()
     own_copy.wait()
+    for z in range(first):
+        for j in range(1, second):
+            k_copy(z, j).wait()
     for k in range(1, nar):
         a_copy(lax.rem(me + k, nar), me).wait_send()
         b_copy(lax.rem(me + k, nar), me).wait_send()
@@ -1298,7 +1739,7 @@
     for i in range(1, outer):
         x_copy(i, 0, tail_rows).wait_send()
         for n in range(1, first + 1):
-            x_copy(i, n, span(lax.rem(za + n, first))).wait_send()
+            x_copy(i, n, span(dest(n))).wait_send()
     for j in range(1, second):
         y_copy(j).wait_send()
     for n in range(1, first):
@@ -1319,7 +1760,9 @@
                 h_copy(z, j, c, False).wait_send()
 
 
-def attention_grads(grads, seg, gain, sums, sides, qkv, lse, one, inputs, above, pq, first, wid, name):
+def attention_grads(
+    seg, gain, sums, grads, lines, sides, qkv, lse, one, inputs, above, pq, first, wid, name
+):
     nar, tok, local = grads.shape
     rows, wide = qkv.shape
     width = inputs.shape[1]
@@ -1341,15 +1784,18 @@
         ),
         out_shape=(
             jax.ShapeDtypeStruct((nar, tok, width), BF16),
+            jax.ShapeDtypeStruct((nar, tok, width), BF16),
             jax.ShapeDtypeStruct((8, piece), F32),
             jax.ShapeDtypeStruct((piece, hidden), F32),
             jax.ShapeDtypeStruct((hidden, piece), F32),
             jax.ShapeDtypeStruct((local, piece), F32),
             jax.ShapeDtypeStruct((3 * local, piece), F32),
         ),
-        in_specs=[vmem] * 4 + [hbm] * 12,
-        out_specs=(hbm,) + (vmem,) * 5,
-        scratch_shapes=[pltpu.VMEM(x.shape, x.dtype) for x in late]
+        in_specs=[vmem] * 3 + [hbm] * 14,
+        out_specs=(hbm, hbm) + (vmem,) * 5,
+        scratch_shapes=[
+            pltpu.VMEM((tok, width) if x is inputs else x.shape, x.dtype) for x in late
+        ]
         + [
             dma((12,)),
             pltpu.VMEM((rows, wide), BF16),
@@ -1364,7 +1810,8 @@
             pltpu.VMEM((nar * local, piece), F32),
             pltpu.VMEM((second, first, local, piece), BF16),
             pltpu.VMEM((second, first, local, piece), BF16),
-            pltpu.VMEM((first - 1, line, piece), BF16),
+            pltpu.VMEM((5, line, piece), BF16),
+            pltpu.VMEM((line, piece), F32),
             pltpu.VMEM((wid, 3 * local, piece), BF16),
             pltpu.VMEM((wid, 3 * local, piece), BF16),
             pltpu.VMEM((tok, width), BF16),
@@ -1372,7 +1819,9 @@
             pltpu.VMEM((nar, 8, width), F32),
             pltpu.VMEM((wid, 8, piece), F32),
             pltpu.VMEM((wid, 8, piece), F32),
-            dma,
+            dma((2,)),
+            dma((first, second)),
+            dma((first, second)),
             dma((nar,)),
             dma((nar,)),
             dma((nar,)),
@@ -1384,7 +1833,7 @@
             dma((second,)),
             dma((second,)),
             dma((first,)),
-            dma((first,)),
+            dma((5,)),
             dma((wid,)),
             dma((wid,)),
             dma((first, 3, chunks)),
@@ -1399,7 +1848,7 @@
         compiler_params=pltpu.CompilerParams(
             collective_id=name, has_side_effects=True, vmem_limit_bytes=63 * 2**20
         ),
-    )(grads, seg, gain, sums, *late)
+    )(seg, gain, sums, grads, lines, *late)
 
 
 def neighbour_kernel(
@@ -1409,12 +1858,16 @@
     tile,
     kept,
     ring,
+    count_ref,
+    target_ref,
+    base_ref,
+    weight_ref,
+    temper_ref,
+    mix_ref,
     query_ref,
     keys_ref,
-    norms_ref,
-    ids_ref,
-    cols_ref,
-    scal_ref,
+    norms_any,
+    ids_any,
     grad_ref,
     loss_ref,
     stat_ref,
@@ -1425,6 +1878,9 @@
     sends,
     slots,
     loss_own,
+    norms_ref,
+    ids_ref,
+    load_sem,
     slot_sem,
     q_send,
     q_recv,
@@ -1458,6 +1914,13 @@
             keys_ref.at[pl.ds(row, tile)], slots.at[slot], slot_sem.at[slot]
         )
 
+    loads = [
+        pltpu.make_async_copy(norms_any, norms_ref, load_sem.at[0]),
+        pltpu.make_async_copy(query_ref.at[me], queries.at[0], load_sem.at[1]),
+        pltpu.make_async_copy(ids_any.at[own_rows(tok, second)], ids_ref, load_sem.at[2]),
+    ]
+    for n in range(3):
+        loads[n].start()
     for i in range(kept + ring):
         load(i, i).start()
 
@@ -1494,7 +1957,8 @@
 
     for k in range(1, nar):
         q_copy(k).start()
-    queries[0] = query_ref[me]
+    for n in range(3):
+        loads[n].wait()
 
     row_of = lax.broadcasted_iota(jnp.int32, (group, J), 0)
 
@@ -1553,12 +2017,22 @@
         return total + dist[k]
 
     distance = lax.fori_loop(1, nar, collect, partial[0])
-    temper_value = scal_ref[0]
-    mix_value = scal_ref[1]
-    count = cols_ref[:, 0:1]
-    target = cols_ref[:, 1:2]
-    base = cols_ref[:, 2:3]
-    loss_weight = cols_ref[:, 3:4]
+    temper_value = temper_ref[0]
+    mix_value = mix_ref[0]
+    per_seq = count_ref.shape[1] // tok
+
+    def own_column(ref):
+        row = jnp.zeros((1, tok), F32)
+        for n in range(nar):
+            at = (n % per_seq) * tok
+            seq = n // per_seq
+            row = jnp.where(me == n, ref[seq : seq + 1, at : at + tok].astype(F32), row)
+        return jnp.transpose(jnp.broadcast_to(row, (8, tok)))[:, 0:1]
+
+    count = own_column(count_ref)
+    target = own_column(target_ref)
+    base = own_column(base_ref)
+    loss_weight = own_column(weight_ref)
     logits = distance / temper_value
     spot = lax.broadcasted_iota(jnp.int32, (tok, J), 1).astype(F32)
     masked = jnp.where(spot < count, logits, -1e30)
@@ -1643,7 +2117,7 @@
         o_copy(k).wait()
 
 
-def neighbours(nar, first, query, keys, norms, ids, cols, scal):
+def neighbours(nar, first, columns, temper, mix, query, keys, norms, ids):
     tok, depth = query.shape[1:]
     rows = keys.shape[0]
     tile = 32
@@ -1660,14 +2134,9 @@
             jax.ShapeDtypeStruct((nar, 8, tok), F32),
             jax.ShapeDtypeStruct((2, J), F32),
         ),
-        in_specs=[
-            vmem,
-            pl.BlockSpec(memory_space=pl.ANY),
-            vmem,
-            vmem,
-            vmem,
-            pl.BlockSpec(memory_space=pltpu.SMEM),
-        ],
+        in_specs=[vmem] * 4
+        + [pl.BlockSpec(memory_space=pltpu.SMEM)] * 2
+        + [pl.BlockSpec(memory_space=pl.ANY)] * 4,
         out_specs=(vmem, vmem, vmem),
         scratch_shapes=[
             pltpu.VMEM((nar, tok, depth), BF16),
@@ -1677,13 +2146,16 @@
             pltpu.VMEM((nar, tok, depth), BF16),
             pltpu.VMEM((kept + ring, tile, depth, J), BF16),
             pltpu.VMEM((8, tok), F32),
+            pltpu.VMEM((rows, J), F32),
+            pltpu.VMEM((tok, J), jnp.int32),
+            pltpu.SemaphoreType.DMA((3,)),
             pltpu.SemaphoreType.DMA((kept + ring,)),
         ]
         + [dma] * 10,
         compiler_params=pltpu.CompilerParams(
-            collective_id=1, has_side_effects=True, vmem_limit_bytes=60 * 2**20
+            collective_id=1, has_side_effects=True, vmem_limit_bytes=62 * 2**20
         ),
-    )(query, keys, norms, ids, cols, scal)
+    )(*columns, temper, mix, query, keys, norms, ids)
 
 
 def on_device(
@@ -1713,115 +2185,103 @@
     wid = lax.axis_size("wide")
     first = lax.axis_size("z")
     nar = first * lax.axis_size("y")
-    own = lax.axis_index("z") * lax.axis_size("y") + lax.axis_index("y")
-    tok = rows // nar
-    local_width = w_query.shape[0]
-
-    def mine(values):
-        flat = values.reshape((rows,) + values.shape[2:])
-        return lax.dynamic_slice_in_dim(flat, own * tok, tok, 0)
-
-    seg_column = segments.reshape(rows, 1)
-    seg_row = segments.reshape(seqs_here, 1, length)
-    key_slices = nbr_keys.reshape(rows, nbr_keys.shape[2], nbr_keys.shape[3])
-    gains = jnp.stack([gain_attn, gain_ffn, gain_key])
-    w_qkv = jnp.concatenate([w_query, w_key, w_value], axis=0)
-    normed_one, qkv, lse, part_norms, attended_own, in_all, out_all, pq_all = head(
-        block_input.reshape(rows, width),
-        gains,
-        w_qkv,
-        seg_column,
-        seg_row,
-        key_slices,
+    inputs = block_input.reshape(rows, width)
+    keys = nbr_keys.reshape(rows, nbr_keys.shape[2], nbr_keys.shape[3])
+    gain_one, gain_two, gain_last = (
+        gain.reshape(1, width) for gain in (gain_attn, gain_ffn, gain_key)
+    )
+    normed_one, qkv, lse, part_norms, attended, in_all, out_all, pq_all = head(
+        gain_one,
+        segments,
+        (w_proj, w_query, w_key, w_value),
+        inputs,
+        keys,
         w_in,
         w_out,
-        jnp.concatenate([w_proj, w_qkv], axis=0),
         first,
         nar,
         wid,
         2,
     )
-    proj_all = pq_all[:, :local_width]
-    inputs_own = mine(block_input)
     hidden_one, hidden_two, output_own, query_key, normed_two, pre_act = ffn(
-        attended_own, inputs_own, gains, proj_all, in_all, out_all, 3
-    )
-    block_output = lax.all_gather(output_own, ("z", "y"), axis=0, tiled=True)
-    cols = jnp.stack(
-        [
-            mine(nbr_count).astype(F32),
-            mine(targets).astype(F32),
-            mine(base_prob),
-            mine(loss_weight),
-        ],
-        axis=1,
+        gain_two, gain_last, attended, inputs, pq_all, in_all, out_all, 3
     )
     grad_slices, losses, stats = neighbours(
         nar,
         first,
+        (nbr_count, targets, base_prob, loss_weight),
+        temper,
+        mix_weight,
         query_key,
-        key_slices,
+        keys,
         part_norms,
-        mine(nbr_ids),
-        cols,
-        jnp.concatenate([temper, mix_weight]),
-    )
-    token_loss = losses[:, 0, :]
-    grad_hidden_one, grad_attended, gain_sums, *sides = ffn_back(
+        nbr_ids.reshape(rows, -1),
+    )
+    sums, grad_hidden_one, grad_attended, *sides, lines = ffn_back(
+        gain_two,
+        gain_last,
         grad_slices,
-        attended_own,
-        mine(output_cotangent),
+        stats,
+        hidden_two,
+        output_cotangent.reshape(rows, width),
+        out_all,
+        pre_act,
+        in_all,
+        attended,
+        normed_two,
         hidden_one,
-        hidden_two,
-        gains,
-        pre_act,
-        normed_two,
-        proj_all,
-        in_all,
-        out_all,
-        stats,
+        pq_all,
+        output_own,
         wid,
         5,
     )
-    grad_attended, block_output = lax.optimization_barrier((grad_attended, block_output))
-    grad_input, totals, grad_w_in, grad_w_out, grad_w_proj, grad_w_qkv = attention_grads(
+    grad_input, block_output, totals, grad_in, grad_out, grad_proj, grad_qkv = attention_grads(
+        segments,
+        gain_one,
+        sums,
         grad_attended,
-        segments,
-        gains,
-        gain_sums,
+        lines,
         sides,
         qkv,
         lse,
         normed_one,
-        inputs_own,
+        inputs,
         grad_hidden_one,
         pq_all,
         first,
         wid,
         6,
     )
-
+    results = finish(
+        grad_input,
+        block_output,
+        lines,
+        totals,
+        losses,
+        grad_qkv,
+        grad_proj,
+        grad_in,
+        grad_out,
+        seqs_here,
+    )
+    block_output, token_loss, grad_input, *weights, total_one, total_two, total_last = results[:12]
+    piece = width // wid
     return (
         block_output.reshape(seqs_here, length, width),
-        token_loss.reshape(seqs_here, length),
-        grad_input.astype(F32).reshape(seqs_here, length, width),
-        grad_w_qkv[:local_width],
-        grad_w_qkv[local_width : 2 * local_width],
-        grad_w_qkv[2 * local_width :],
-        grad_w_proj,
-        grad_w_in,
-        grad_w_out,
-        totals[0],
-        totals[1],
-        totals[2],
-        totals[3, 0:1],
-        totals[4, 0:1],
+        token_loss,
+        grad_input.reshape(seqs_here, length, width),
+        *weights,
+        total_one.reshape(piece),
+        total_two.reshape(piece),
+        total_last.reshape(piece),
+        results[12].reshape(1),
+        results[13].reshape(1),
     )
 
 
 def solution(mesh):
     wide, narrow = mesh.devices.shape
-    first = 4 if narrow % 4 == 0 else narrow
+    first = 4
     split = jax.sharding.Mesh(
         mesh.devices.reshape(wide, first, narrow // first), ("wide", "z", "y")
     )

time: 500 us -> 406 us (0.81)
  the two profiles are of different devices: /device:TPU:0 before, /device:TPU:7 now
where the time goes in v4:
time: 406 us; the launch traced here: 403 us
  Pallas kernels  400 us (99%)
    pallas_call x1, Pallas kernels, attention_grads(): pl.pallas_call(functools.partial(grad_kernel, nar, first, wid, seqs, loca...  152 us
    pallas_call x1, Pallas kernels, head(): pl.pallas_call(functools.partial(head_kernel, nar, first, wid, seqs, head...  94.7 us
    pallas_call x1, Pallas kernels, neighbours(): pl.pallas_call(functools.partial(neighbour_kernel, nar, first, tiles, til...  72.3 us
    pallas_call x1, Pallas kernels, ffn_back(): pl.pallas_call(functools.partial(ffn_back_kernel, chunks), out_shape=(jax...  39 us
    pallas_call x1, Pallas kernels, ffn(): pl.pallas_call(functools.partial(ffn_kernel, chunks), out_shape=tuple((ja...  29.5 us
    pallas_call x1, Pallas kernels, finish(): pl.pallas_call(functools.partial(finish_kernel, second), grid=(nar,), out...  12.4 us

profile of v4, /device:TPU:7, one launch (start us, length us, event | category | flops | bytes accessed | tf_op | source)
XLA Modules:
  0.0 402.5 jit_solution(17828006934842333551)
XLA Ops:
  1.9 94.7 %shard_map.299 = (bf16[2048,1024]{1,0:T(8,128)(2,1)}, bf16[2048,384]{1,0:T(8,128)(2,1)}, f32[2048,2]{1,0:T(8,128)}, f32[2048,128]{1,0:T(8,128)}, bf16[8,256,128]...) custom-call(f32[1,1024]{1,0:T(1,128)} %bitcast.23, ...), custom_call_target="tpu_custom_call" | custom-call | tf_op jit(solution)/shard_map/pallas_call | solution.py:489
  96.7 29.5 %shard_map.300 = (f32[256,1024]{1,0:T(8,128)}, f32[256,1024]{1,0:T(8,128)}, bf16[256,1024]{1,0:T(8,128)(2,1)}, bf16[8,256,128]{2,1,0:T(8,128)(2,1)}, bf16[2,256,...) custom-call(f32[1,1024]{1,0:T(1,128)} %bitcast.19, f32[1,1024]{1,0:T(1,128)} %bitcast.21, ...), custom_call_target="tpu_custom_call" | custom-call | tf_op jit(solution)/shard_map/pallas_call | solution.py:698
  126.2 72.3 %shard_map.301 = (bf16[8,256,128]{2,1,0:T(8,128)(2,1)}, f32[8,8,256]{2,1,0:T(8,128)}, f32[2,128]{1,0:T(2,128)}) custom-call(s32[2,1024]{1,0:T(2,128)} %count_ref.1, s32[2,1024]{1,0:T(2,128)} %target_ref.1, f32[2,1024]{1,0:T(2,128)} %base_ref.1, f32[2,1024]{1,0:T(2,128)} %weight_ref.1, f32[1]{0:T(128)S(6)} %copy.34.temper_ref, f32[1]{0:T(128)S(6)} %copy.35.mix_ref, ...), custom_call_target="tpu_custom_call" | custom-call | tf_op jit(solution)/shard_map/pallas_call | solution.py:2130
  198.5 39.0 %shard_map.302 = (f32[8,1024]{1,0:T(8,128)}, f32[256,1024]{1,0:T(8,128)}, bf16[8,256,128]{2,1,0:T(8,128)(2,1)}, bf16[2048,512]{1,0:T(8,128)(2,1)}, bf16[2048,512...) custom-call(f32[1,1024]{1,0:T(1,128)} %bitcast.20, ...), custom_call_target="tpu_custom_call" | custom-call | tf_op jit(solution)/shard_map/pallas_call | solution.py:1011
  237.5 152.4 %shard_map.303 = (bf16[8,256,1024]{2,1,0:T(8,128)(2,1)}, bf16[8,256,1024]{2,1,0:T(8,128)(2,1)}, f32[8,256]{1,0:T(8,128)}, f32[256,512]{1,0:T(8,128)}, f32[512,25...) custom-call(s32[2,1024]{1,0:T(2,128)} %seg_ref.3, f32[1,1024]{1,0:T(1,128)} %bitcast.24, ...), custom_call_target="tpu_custom_call" | custom-call | tf_op jit(solution)/shard_map/pallas_call | solution.py:1781
  389.9 12.4 %shard_map.304 = (bf16[8,256,1024]{2,1,0:T(8,128)(2,1)}, f32[2,1024]{1,0:T(2,128)}, f32[8,256,1024]{2,1,0:T(8,128)}, f32[128,256]{1,0:T(8,128)}, f32[128,256]{1,...) custom-call(bf16[8,256,1024]{2,1,0:T(8,128)(2,1)} %get-tuple-element, ...), custom_call_target="tpu_custom_call" | custom-call | tf_op jit(solution)/shard_map/pallas_call | solution.py:1141

commit v5 on v4

--- a/solution.py
+++ b/solution.py
@@ -275,19 +275,21 @@
                         chip_copy(t, source, o).start()
                     core_copy(t, source, 0, False).start()
 
-    def chip_arrivals(t):
-        for n in range(first):
-            source = n * second + yb
-
-            @pl.when(source != me)
-            def _(source=source):
-                for o in range(1, outer):
-                    chip_arrival(t, source, o).wait_recv()
-                    core_copy(t, source, o, False).start()
-                if t == 0:
-                    for j in range(1, second):
-                        for o in range(outer):
-                            row_copy(source, j, o, False).start()
+    def chip_arrivals(t, begin, end):
+        for d in range(begin, end):
+            for way in (-1, 1):
+                z = za + way * d
+
+                @pl.when((z >= 0) & (z < first))
+                def _(z=z):
+                    source = z * second + yb
+                    for o in range(1, outer):
+                        chip_arrival(t, source, o).wait_recv()
+                        core_copy(t, source, o, False).start()
+                    if t == 0:
+                        for j in range(1, second):
+                            for o in range(outer):
+                                row_copy(source, j, o, False).start()
 
     def row_arrivals():
         for j in range(1, second):
@@ -334,6 +336,12 @@
     stores[0].start()
     stores[1].start()
     line_arrivals(0, 1, 2)
+    middle = (za == 1) | (za == 2)
+    at_end = jnp.logical_not(middle)
+
+    @pl.when(middle)
+    def _():
+        line_arrivals(0, 2, first)
 
     def sequence(seq, carry):
         base = seq * length
@@ -402,27 +410,40 @@
 
         lax.fori_loop(begin, end, body, 0)
 
-    def some(*calls):
-        def run():
-            for call in calls:
-                call()
-
-        return run
-
-    steps = [
-        some(lambda: line_arrivals(1, 1, 2), lambda: line_arrivals(0, 2, first)),
-        some(lambda: chip_arrivals(0), lambda: line_arrivals(2, 1, 2)),
-        lambda: line_arrivals(1, 2, first),
-        lambda: line_arrivals(2, 2, first),
-    ]
-    share_of = tiles // len(steps)
-    for n, step in enumerate(steps):
-        step()
-        norms(n * share_of, tiles if n == len(steps) - 1 else (n + 1) * share_of)
+    @pl.when(at_end)
+    def _():
+        line_arrivals(1, 1, 2)
+        line_arrivals(2, 1, 2)
+        chip_arrivals(0, 1, 2)
+        line_arrivals(0, 2, first)
+
+    @pl.when(middle)
+    def _():
+        line_arrivals(1, 1, first)
+        chip_arrivals(0, 1, first)
+
+    norms(0, tiles // 3)
+
+    @pl.when(at_end)
+    def _():
+        chip_arrivals(0, 2, first)
+        line_arrivals(1, 2, first)
+
+    @pl.when(middle)
+    def _():
+        line_arrivals(2, 1, first)
+
+    norms(tiles // 3, 2 * tiles // 3)
+
+    @pl.when(at_end)
+    def _():
+        line_arrivals(2, 2, first)
+
+    norms(2 * tiles // 3, tiles)
     stores[3].start()
     row_arrivals()
-    chip_arrivals(1)
-    chip_arrivals(2)
+    chip_arrivals(1, 1, first)
+    chip_arrivals(2, 1, first)
     for t in range(3):
         core_arrivals(t)
     for k in range(1, nar):
@@ -1445,8 +1466,9 @@
         a_copy(lax.rem(me + k, nar), me).start()
     own_grad = pltpu.make_async_copy(grad_ref.at[me], grads.at[me], own_sem.at[1])
     own_grad.start()
-    for j in range(1, second):
-        k_copy(0, j).start()
+    for z in range(2):
+        for j in range(1, second):
+            k_copy(z, j).start()
     for n in range(6):
         loads[n].wait()
 
@@ -1567,7 +1589,7 @@
 
     lax.fori_loop(0, seqs, sequence, 0)
 
-    for z in range(1, first):
+    for z in range(2, first):
         for j in range(1, second):
             k_copy(z, j).start()
     loads[8].wait()

time: 406 us -> 388 us (0.956)
  Pallas kernels: 400 us -> 380 us
    pallas_call x1, Pallas kernels: 94.7 us -> 83.3 us  [head(): pl.pallas_call(functools.partial(head_kernel, nar, first, wid, seqs, head...]
    pallas_call x1, Pallas kernels: 152 us -> 141 us  [attention_grads(): pl.pallas_call(functools.partial(grad_kernel, nar, first, wid, seqs, loca...]
where the time goes in v5:
time: 388 us; the launch traced here: 382 us
  Pallas kernels  380 us (98%)
    pallas_call x1, Pallas kernels, attention_grads(): pl.pallas_call(functools.partial(grad_kernel, nar, first, wid, seqs, loca...  141 us
    pallas_call x1, Pallas kernels, head(): pl.pallas_call(functools.partial(head_kernel, nar, first, wid, seqs, head...  83.3 us
    pallas_call x1, Pallas kernels, neighbours(): pl.pallas_call(functools.partial(neighbour_kernel, nar, first, tiles, til...  72.3 us
    pallas_call x1, Pallas kernels, ffn_back(): pl.pallas_call(functools.partial(ffn_back_kernel, chunks), out_shape=(jax...  40.3 us
    pallas_call x1, Pallas kernels, ffn(): pl.pallas_call(functools.partial(ffn_kernel, chunks), out_shape=tuple((ja...  30.1 us
    pallas_call x1, Pallas kernels, finish(): pl.pallas_call(functools.partial(finish_kernel, second), grid=(nar,), out...  12.4 us

profile of v5, /device:TPU:7, one launch (start us, length us, event | category | flops | bytes accessed | tf_op | source)
XLA Modules:
  0.0 381.9 jit_solution(541374491893462537)
XLA Ops:
  1.9 83.3 %shard_map.299 = (bf16[2048,1024]{1,0:T(8,128)(2,1)}, bf16[2048,384]{1,0:T(8,128)(2,1)}, f32[2048,2]{1,0:T(8,128)}, f32[2048,128]{1,0:T(8,128)}, bf16[8,256,128]...) custom-call(f32[1,1024]{1,0:T(1,128)} %bitcast.23, ...), custom_call_target="tpu_custom_call" | custom-call | tf_op jit(solution)/shard_map/pallas_call | solution.py:510
  85.2 30.1 %shard_map.300 = (f32[256,1024]{1,0:T(8,128)}, f32[256,1024]{1,0:T(8,128)}, bf16[256,1024]{1,0:T(8,128)(2,1)}, bf16[8,256,128]{2,1,0:T(8,128)(2,1)}, bf16[2,256,...) custom-call(f32[1,1024]{1,0:T(1,128)} %bitcast.19, f32[1,1024]{1,0:T(1,128)} %bitcast.21, ...), custom_call_target="tpu_custom_call" | custom-call | tf_op jit(solution)/shard_map/pallas_call | solution.py:719
  115.4 72.3 %shard_map.301 = (bf16[8,256,128]{2,1,0:T(8,128)(2,1)}, f32[8,8,256]{2,1,0:T(8,128)}, f32[2,128]{1,0:T(2,128)}) custom-call(s32[2,1024]{1,0:T(2,128)} %count_ref.1, s32[2,1024]{1,0:T(2,128)} %target_ref.1, f32[2,1024]{1,0:T(2,128)} %base_ref.1, f32[2,1024]{1,0:T(2,128)} %weight_ref.1, f32[1]{0:T(128)S(6)} %copy.34.temper_ref, f32[1]{0:T(128)S(6)} %copy.35.mix_ref, ...), custom_call_target="tpu_custom_call" | custom-call | tf_op jit(solution)/shard_map/pallas_call | solution.py:2152
  187.7 40.3 %shard_map.302 = (f32[8,1024]{1,0:T(8,128)}, f32[256,1024]{1,0:T(8,128)}, bf16[8,256,128]{2,1,0:T(8,128)(2,1)}, bf16[2048,512]{1,0:T(8,128)(2,1)}, bf16[2048,512...) custom-call(f32[1,1024]{1,0:T(1,128)} %bitcast.20, ...), custom_call_target="tpu_custom_call" | custom-call | tf_op jit(solution)/shard_map/pallas_call | solution.py:1032
  228.0 141.2 %shard_map.303 = (bf16[8,256,1024]{2,1,0:T(8,128)(2,1)}, bf16[8,256,1024]{2,1,0:T(8,128)(2,1)}, f32[8,256]{1,0:T(8,128)}, f32[256,512]{1,0:T(8,128)}, f32[512,25...) custom-call(s32[2,1024]{1,0:T(2,128)} %seg_ref.3, f32[1,1024]{1,0:T(1,128)} %bitcast.24, ...), custom_call_target="tpu_custom_call" | custom-call | tf_op jit(solution)/shard_map/pallas_call | solution.py:1803
  369.2 12.4 %shard_map.304 = (bf16[8,256,1024]{2,1,0:T(8,128)(2,1)}, f32[2,1024]{1,0:T(2,128)}, f32[8,256,1024]{2,1,0:T(8,128)}, f32[128,256]{1,0:T(8,128)}, f32[128,256]{1,...) custom-call(bf16[8,256,1024]{2,1,0:T(8,128)(2,1)} %get-tuple-element, ...), custom_call_target="tpu_custom_call" | custom-call | tf_op jit(solution)/shard_map/pallas_call | solution.py:1162

commit v6 on v5

--- a/solution.py
+++ b/solution.py
@@ -13,7 +13,7 @@
 BF16 = jnp.bfloat16
 MESH = pl.DeviceIdType.MESH
 J = 128
-KEPT_BYTES = 44 * 2**20
+KEPT_BYTES = 24 * 2**20
 
 
 def place(index, second):
@@ -1102,15 +1102,15 @@
         mix_out,
     ) = outs
     grad_out[...] = grad_ref[...].astype(F32)
-    near = lax.rem(pl.program_id(0), second) == lax.axis_index("y")
-
-    @pl.when(near)
-    def _():
-        block_out[...] = line_ref[...]
-
-    @pl.when(jnp.logical_not(near))
-    def _():
-        block_out[...] = block_ref[...]
+    for j in range(second):
+
+        @pl.when(lax.axis_index("y") == j)
+        def _(j=j):
+            block_out[j] = line_ref[0]
+
+        @pl.when(lax.axis_index("y") != j)
+        def _(j=j):
+            block_out[j] = block_ref[j]
 
     @pl.when(pl.program_id(0) == 0)
     def _():
@@ -1143,7 +1143,7 @@
         return pl.BlockSpec(shape, lambda i: (0,) * len(shape))
 
     def each():
-        return pl.BlockSpec((1, tok, width), lambda i: (i, 0, 0))
+        return pl.BlockSpec((second, tok, width), lambda i: (i, 0, 0))
 
     small = [
         ((local, piece), F32),
@@ -1161,14 +1161,14 @@
     loss_shape = (seqs, nar * tok // seqs)
     return pl.pallas_call(
         functools.partial(finish_kernel, second),
-        grid=(nar,),
+        grid=(nar // second,),
         out_shape=(
             jax.ShapeDtypeStruct((nar, tok, width), BF16),
             jax.ShapeDtypeStruct(loss_shape, F32),
             jax.ShapeDtypeStruct((nar, tok, width), F32),
         )
         + tuple(jax.ShapeDtypeStruct(*x) for x in small),
-        in_specs=[each(), each(), pl.BlockSpec((1, tok, width), lambda i: (i // second, 0, 0))]
+        in_specs=[each(), each(), pl.BlockSpec((1, tok, width), lambda i: (i, 0, 0))]
         + [whole(x.shape) for x in (totals, losses, qkv, proj, w_in, w_out)],
         out_specs=(each(), whole(loss_shape), each()) + tuple(whole(x[0]) for x in small),
         compiler_params=pltpu.CompilerParams(vmem_limit_bytes=62 * 2**20),
@@ -1487,26 +1487,6 @@
         core_out[o, tail_rows, :] = product_tail(w).astype(BF16)
         c_copy(o).start()
 
-    for i in range(1, outer):
-        o = lax.rem(chip + i, outer)
-        w = o * 2 + core
-        c_copy(o).wait_recv()
-        total = product_tail(w) + core_in[o, tail_rows, :].astype(F32)
-        chip_out[i - 1, tail_rows, :] = total.astype(BF16)
-        x_copy(i, 0, tail_rows).start()
-
-        def for_chip(n, carry, o=o, w=w, i=i):
-            z = dest(n)
-            upper, lower = product_rows(w, z)
-            at = pl.multiple_of(z * rows, rows)
-            high, low = pl.ds(at, hidden), pl.ds(at + hidden, hidden)
-            chip_out[i - 1, high, :] = (upper + core_in[o, high, :].astype(F32)).astype(BF16)
-            chip_out[i - 1, low, :] = (lower + core_in[o, low, :].astype(F32)).astype(BF16)
-            x_copy(i, n, span(z)).start()
-            return carry
-
-        lax.fori_loop(1, first + 1, for_chip, 0)
-
     loads[6].wait()
     loads[7].wait()
     own_grad.wait()
@@ -1588,6 +1568,26 @@
         return carry
 
     lax.fori_loop(0, seqs, sequence, 0)
+
+    for i in range(1, outer):
+        o = lax.rem(chip + i, outer)
+        w = o * 2 + core
+        c_copy(o).wait_recv()
+        total = product_tail(w) + core_in[o, tail_rows, :].astype(F32)
+        chip_out[i - 1, tail_rows, :] = total.astype(BF16)
+        x_copy(i, 0, tail_rows).start()
+
+        def for_chip(n, carry, o=o, w=w, i=i):
+            z = dest(n)
+            upper, lower = product_rows(w, z)
+            at = pl.multiple_of(z * rows, rows)
+            high, low = pl.ds(at, hidden), pl.ds(at + hidden, hidden)
+            chip_out[i - 1, high, :] = (upper + core_in[o, high, :].astype(F32)).astype(BF16)
+            chip_out[i - 1, low, :] = (lower + core_in[o, low, :].astype(F32)).astype(BF16)
+            x_copy(i, n, span(z)).start()
+            return carry
+
+        lax.fori_loop(1, first + 1, for_chip, 0)
 
     for z in range(2, first):
         for j in range(1, second):
@@ -2142,7 +2142,7 @@
 def neighbours(nar, first, columns, temper, mix, query, keys, norms, ids):
     tok, depth = query.shape[1:]
     rows = keys.shape[0]
-    tile = 32
+    tile = 64
     tiles = rows // tile
     bytes_tile = tile * depth * J * 2
     ring = 4

time: 388 us -> 374 us (0.964)
  the two profiles are of different devices: /device:TPU:7 before, /device:TPU:0 now
where the time goes in v6:
time: 374 us; the launch traced here: 368 us
  Pallas kernels  366 us (98%)
    pallas_call x1, Pallas kernels, attention_grads(): pl.pallas_call(functools.partial(grad_kernel, nar, first, wid, seqs, loca...  127 us
    pallas_call x1, Pallas kernels, head(): pl.pallas_call(functools.partial(head_kernel, nar, first, wid, seqs, head...  85 us
    pallas_call x1, Pallas kernels, neighbours(): pl.pallas_call(functools.partial(neighbour_kernel, nar, first, tiles, til...  72.2 us
    pallas_call x1, Pallas kernels, ffn_back(): pl.pallas_call(functools.partial(ffn_back_kernel, chunks), out_shape=(jax...  42 us
    pallas_call x1, Pallas kernels, ffn(): pl.pallas_call(functools.partial(ffn_kernel, chunks), out_shape=tuple((ja...  29.8 us
    pallas_call x1, Pallas kernels, finish(): pl.pallas_call(functools.partial(finish_kernel, second), grid=(nar // sec...  9.99 us

profile of v6, /device:TPU:0, one launch (start us, length us, event | category | flops | bytes accessed | tf_op | source)
XLA Modules:
  0.0 368.0 jit_solution(15102049404085346930)
XLA Ops:
  1.9 85.0 %shard_map.299 = (bf16[2048,1024]{1,0:T(8,128)(2,1)}, bf16[2048,384]{1,0:T(8,128)(2,1)}, f32[2048,2]{1,0:T(8,128)}, f32[2048,128]{1,0:T(8,128)}, bf16[8,256,128]...) custom-call(f32[1,1024]{1,0:T(1,128)} %bitcast.23, ...), custom_call_target="tpu_custom_call" | custom-call | tf_op jit(solution)/shard_map/pallas_call | solution.py:510
  87.0 29.8 %shard_map.300 = (f32[256,1024]{1,0:T(8,128)}, f32[256,1024]{1,0:T(8,128)}, bf16[256,1024]{1,0:T(8,128)(2,1)}, bf16[8,256,128]{2,1,0:T(8,128)(2,1)}, bf16[2,256,...) custom-call(f32[1,1024]{1,0:T(1,128)} %bitcast.19, f32[1,1024]{1,0:T(1,128)} %bitcast.21, ...), custom_call_target="tpu_custom_call" | custom-call | tf_op jit(solution)/shard_map/pallas_call | solution.py:719
  116.8 72.2 %shard_map.301 = (bf16[8,256,128]{2,1,0:T(8,128)(2,1)}, f32[8,8,256]{2,1,0:T(8,128)}, f32[2,128]{1,0:T(2,128)}) custom-call(s32[2,1024]{1,0:T(2,128)} %count_ref.1, s32[2,1024]{1,0:T(2,128)} %target_ref.1, f32[2,1024]{1,0:T(2,128)} %base_ref.1, f32[2,1024]{1,0:T(2,128)} %weight_ref.1, f32[1]{0:T(128)S(6)} %copy.34.temper_ref, f32[1]{0:T(128)S(6)} %copy.35.mix_ref, ...), custom_call_target="tpu_custom_call" | custom-call | tf_op jit(solution)/shard_map/pallas_call | solution.py:2152
  189.0 42.0 %shard_map.302 = (f32[8,1024]{1,0:T(8,128)}, f32[256,1024]{1,0:T(8,128)}, bf16[8,256,128]{2,1,0:T(8,128)(2,1)}, bf16[2048,512]{1,0:T(8,128)(2,1)}, bf16[2048,512...) custom-call(f32[1,1024]{1,0:T(1,128)} %bitcast.20, ...), custom_call_target="tpu_custom_call" | custom-call | tf_op jit(solution)/shard_map/pallas_call | solution.py:1032
  231.0 126.8 %shard_map.303 = (bf16[8,256,1024]{2,1,0:T(8,128)(2,1)}, bf16[8,256,1024]{2,1,0:T(8,128)(2,1)}, f32[8,256]{1,0:T(8,128)}, f32[256,512]{1,0:T(8,128)}, f32[512,25...) custom-call(s32[2,1024]{1,0:T(2,128)} %seg_ref.3, f32[1,1024]{1,0:T(1,128)} %bitcast.24, ...), custom_call_target="tpu_custom_call" | custom-call | tf_op jit(solution)/shard_map/pallas_call | solution.py:1803
  357.8 10.0 %shard_map.304 = (bf16[8,256,1024]{2,1,0:T(8,128)(2,1)}, f32[2,1024]{1,0:T(2,128)}, f32[8,256,1024]{2,1,0:T(8,128)}, f32[128,256]{1,0:T(8,128)}, f32[128,256]{1,...) custom-call(bf16[8,256,1024]{2,1,0:T(8,128)(2,1)} %get-tuple-element, ...), custom_call_target="tpu_custom_call" | custom-call | tf_op jit(solution)/shard_map/pallas_call | solution.py:1162

commit v7 on v6

--- a/solution.py
+++ b/solution.py
@@ -13,7 +13,7 @@
 BF16 = jnp.bfloat16
 MESH = pl.DeviceIdType.MESH
 J = 128
-KEPT_BYTES = 24 * 2**20
+KEPT_BYTES = 20 * 2**20
 
 
 def place(index, second):
@@ -2145,7 +2145,7 @@
     tile = 64
     tiles = rows // tile
     bytes_tile = tile * depth * J * 2
-    ring = 4
+    ring = 6
     kept = min(tiles - 2 * ring, (KEPT_BYTES // bytes_tile))
     vmem = pl.BlockSpec(memory_space=pltpu.VMEM)
     dma = pltpu.SemaphoreType.DMA((nar,))

time: 374 us -> 374 us (level)
  no operation moved by 1% of the time
where the time goes in v7:
time: 374 us; the launch traced here: 368 us
  Pallas kernels  366 us (98%)
    pallas_call x1, Pallas kernels, attention_grads(): pl.pallas_call(functools.partial(grad_kernel, nar, first, wid, seqs, loca...  127 us
    pallas_call x1, Pallas kernels, head(): pl.pallas_call(functools.partial(head_kernel, nar, first, wid, seqs, head...  85 us
    pallas_call x1, Pallas kernels, neighbours(): pl.pallas_call(functools.partial(neighbour_kernel, nar, first, tiles, til...  72.2 us
    pallas_call x1, Pallas kernels, ffn_back(): pl.pallas_call(functools.partial(ffn_back_kernel, chunks), out_shape=(jax...  42.4 us
    pallas_call x1, Pallas kernels, ffn(): pl.pallas_call(functools.partial(ffn_kernel, chunks), out_shape=tuple((ja...  29.8 us
    pallas_call x1, Pallas kernels, finish(): pl.pallas_call(functools.partial(finish_kernel, second), grid=(nar // sec...  9.99 us

profile of v7, /device:TPU:0, one launch (start us, length us, event | category | flops | bytes accessed | tf_op | source)
XLA Modules:
  0.0 368.2 jit_solution(15083825834703259429)
XLA Ops:
  1.9 85.0 %shard_map.299 = (bf16[2048,1024]{1,0:T(8,128)(2,1)}, bf16[2048,384]{1,0:T(8,128)(2,1)}, f32[2048,2]{1,0:T(8,128)}, f32[2048,128]{1,0:T(8,128)}, bf16[8,256,128]...) custom-call(f32[1,1024]{1,0:T(1,128)} %bitcast.23, ...), custom_call_target="tpu_custom_call" | custom-call | tf_op jit(solution)/shard_map/pallas_call | solution.py:510
  87.0 29.8 %shard_map.300 = (f32[256,1024]{1,0:T(8,128)}, f32[256,1024]{1,0:T(8,128)}, bf16[256,1024]{1,0:T(8,128)(2,1)}, bf16[8,256,128]{2,1,0:T(8,128)(2,1)}, bf16[2,256,...) custom-call(f32[1,1024]{1,0:T(1,128)} %bitcast.19, f32[1,1024]{1,0:T(1,128)} %bitcast.21, ...), custom_call_target="tpu_custom_call" | custom-call | tf_op jit(solution)/shard_map/pallas_call | solution.py:719
  116.8 72.2 %shard_map.301 = (bf16[8,256,128]{2,1,0:T(8,128)(2,1)}, f32[8,8,256]{2,1,0:T(8,128)}, f32[2,128]{1,0:T(2,128)}) custom-call(s32[2,1024]{1,0:T(2,128)} %count_ref.1, s32[2,1024]{1,0:T(2,128)} %target_ref.1, f32[2,1024]{1,0:T(2,128)} %base_ref.1, f32[2,1024]{1,0:T(2,128)} %weight_ref.1, f32[1]{0:T(128)S(6)} %copy.34.temper_ref, f32[1]{0:T(128)S(6)} %copy.35.mix_ref, ...), custom_call_target="tpu_custom_call" | custom-call | tf_op jit(solution)/shard_map/pallas_call | solution.py:2152
  189.0 42.4 %shard_map.302 = (f32[8,1024]{1,0:T(8,128)}, f32[256,1024]{1,0:T(8,128)}, bf16[8,256,128]{2,1,0:T(8,128)(2,1)}, bf16[2048,512]{1,0:T(8,128)(2,1)}, bf16[2048,512...) custom-call(f32[1,1024]{1,0:T(1,128)} %bitcast.20, ...), custom_call_target="tpu_custom_call" | custom-call | tf_op jit(solution)/shard_map/pallas_call | solution.py:1032
  231.4 126.6 %shard_map.303 = (bf16[8,256,1024]{2,1,0:T(8,128)(2,1)}, bf16[8,256,1024]{2,1,0:T(8,128)(2,1)}, f32[8,256]{1,0:T(8,128)}, f32[256,512]{1,0:T(8,128)}, f32[512,25...) custom-call(s32[2,1024]{1,0:T(2,128)} %seg_ref.3, f32[1,1024]{1,0:T(1,128)} %bitcast.24, ...), custom_call_target="tpu_custom_call" | custom-call | tf_op jit(solution)/shard_map/pallas_call | solution.py:1803
  358.0 10.0 %shard_map.304 = (bf16[8,256,1024]{2,1,0:T(8,128)(2,1)}, f32[2,1024]{1,0:T(2,128)}, f32[8,256,1024]{2,1,0:T(8,128)}, f32[128,256]{1,0:T(8,128)}, f32[128,256]{1,...) custom-call(bf16[8,256,1024]{2,1,0:T(8,128)(2,1)} %get-tuple-element, ...), custom_call_target="tpu_custom_call" | custom-call | tf_op jit(solution)/shard_map/pallas_call | solution.py:1162
